TPU v7x, 256 devices: a whole 4x4x8 slice. The times are simulated.
256 devices in a mesh: row: 16 (over x_lo, z), col: 16 (over y, x_hi, core).
Axes of the slice: x: 4 (x_hi: 2, x_lo: 2; x = x_hi * 2 + x_lo), y: 4, z: 8, core: 2. Of those that a mesh axis runs over, the one named last changes fastest.
Arguments:
- tokens: bfloat16 [256, 256, 384], P('row', 'col'), may hold values from -8 to 8
- grad_out: bfloat16 [256, 256, 384], P('row', 'col'), may hold values from -6 to 6
- w_query: bfloat16 [384, 384], replicated, as said below
- w_key: bfloat16 [384, 384], replicated, as said below
- w_value: bfloat16 [384, 384], replicated, may hold values from -0.3125 to 0.3125
- w_out: bfloat16 [384, 384], replicated, may hold values from -0.3125 to 0.3125
Outputs:
- grad_tokens: bfloat16 [256, 256, 384], P('row', 'col')
- grad_query: float32 [384, 384], replicated
- grad_key: float32 [384, 384], replicated
- grad_value: float32 [384, 384], replicated
- grad_output: float32 [384, 384], replicated
Inputs may be any that keep to these rules, and one draw needn't show every extreme that they name: `w_query`: entries are of order one over the square root of 384. `w_key`: entries are of order one over the square root of 384.
All inputs are finite; a program needn't handle non-finite values.
Results may differ from a plain program's by a relative error of at most 0.015.
Values may be sent and summed in bfloat16 or wider, within the bound.
No kernel may reach another device: no remote copies, remote signals or barrier semaphores. Data moves between devices by JAX's collectives and lax.ppermute only.
A program may use at most 192 MiB of HBM per device.

v0:
```python
import jax
import jax.numpy as jnp
from jax import lax
from jax.sharding import PartitionSpec as P

HEADS = 6
HEAD_DIM = 64
TILE = 8


masked_value = -1e30


def padded_2(block, sides, width):
    for axis, dim in sides:
        count = lax.axis_size(axis)
        forward = [(i, i + 1) for i in range(count - 1)]
        backward = [(target, source) for source, target in forward]
        low = lax.ppermute(
            lax.slice_in_dim(block, block.shape[dim] - width, None, axis=dim), axis, forward
        )
        high = lax.ppermute(lax.slice_in_dim(block, 0, width, axis=dim), axis, backward)
        block = jnp.concatenate([low, block, high], axis=dim)
    return block


def tile_windows(padded, row_count, col_count):
    feature = padded.shape[-1]
    blocks = padded.reshape(row_count + 2, TILE, col_count + 2, TILE, feature)
    outer_list = []
    for row_pick in range(3):
        inner_list = []
        for col_pick in range(3):
            section = blocks[
                row_pick : row_pick + row_count, :, col_pick : col_pick + col_count, :, :
            ]
            inner_list.append(jnp.transpose(section, (0, 2, 1, 3, 4)))
        outer_list.append(jnp.stack(inner_list, axis=3))
    stacked = jnp.stack(outer_list, axis=2)
    return stacked.reshape(row_count * col_count, 9 * TILE * TILE, feature)


def fold_windows(totals, contrib, offset, row_count, col_count):
    feature = contrib.shape[-1]
    pieces = contrib.reshape(row_count, col_count, 3, TILE, 3, TILE, feature)
    for row_pick in range(3):
        for col_pick in range(3):
            section = jnp.transpose(pieces[:, :, row_pick, :, col_pick, :, :], (0, 2, 1, 3, 4))
            section = section.reshape(row_count * TILE, col_count * TILE, feature)
            totals = totals.at[
                offset + row_pick * TILE : offset + row_pick * TILE + row_count * TILE,
                col_pick * TILE : col_pick * TILE + col_count * TILE,
            ].add(section)
    return totals


def into_tiles(grid, row_count, col_count):
    feature = grid.shape[-1]
    blocks = grid.reshape(row_count, TILE, col_count, TILE, feature)
    return jnp.transpose(blocks, (0, 2, 1, 3, 4)).reshape(
        row_count * col_count, TILE * TILE, feature
    )


def from_tiles(tiles, row_count, col_count):
    feature = tiles.shape[-1]
    blocks = tiles.reshape(row_count, col_count, TILE, TILE, feature)
    return jnp.transpose(blocks, (0, 2, 1, 3, 4)).reshape(
        row_count * TILE, col_count * TILE, feature
    )


def tile_core(queries, grads, key_win, value_win, valid_keys):
    tile_count = queries.shape[0]
    score_scale = HEAD_DIM ** (-0.5)
    query_heads = queries.reshape(tile_count, -1, HEADS, HEAD_DIM)
    grad_heads = grads.reshape(tile_count, -1, HEADS, HEAD_DIM)
    key_heads = key_win.reshape(tile_count, -1, HEADS, HEAD_DIM)
    value_heads = value_win.reshape(tile_count, -1, HEADS, HEAD_DIM)
    scores = (
        jnp.einsum("nqhe,nkhe->nhqk", query_heads, key_heads, preferred_element_type=jnp.float32)
        * score_scale
    )
    live_mask = valid_keys[:, None, None, :]
    scores = jnp.where(live_mask, scores, masked_value)
    row_max = jnp.max(scores, axis=-1, keepdims=True)
    exp_terms = jnp.where(live_mask, jnp.exp(scores - row_max), 0.0)
    weight_full = exp_terms / jnp.sum(exp_terms, axis=-1, keepdims=True)
    weight_half = weight_full.astype(jnp.bfloat16)
    attended = jnp.einsum(
        "nhqk,nkhe->nqhe", weight_half, value_heads, preferred_element_type=jnp.float32
    ).astype(jnp.bfloat16)
    grad_weight = jnp.einsum(
        "nqhe,nkhe->nhqk", grad_heads, value_heads, preferred_element_type=jnp.float32
    )
    row_dot = jnp.sum(weight_full * grad_weight, axis=-1, keepdims=True)
    grad_score = (weight_full * (grad_weight - row_dot) * score_scale).astype(jnp.bfloat16)
    value_part = jnp.einsum(
        "nhqk,nqhe->nkhe", weight_half, grad_heads, preferred_element_type=jnp.float32
    )
    key_part = jnp.einsum(
        "nhqk,nqhe->nkhe", grad_score, query_heads, preferred_element_type=jnp.float32
    )
    grad_q = jnp.einsum(
        "nhqk,nkhe->nqhe", grad_score, key_heads, preferred_element_type=jnp.float32
    ).astype(jnp.bfloat16)
    feature = HEADS * HEAD_DIM
    return (
        attended.reshape(tile_count, -1, feature),
        grad_q.reshape(tile_count, -1, feature),
        key_part.reshape(tile_count, -1, feature),
        value_part.reshape(tile_count, -1, feature),
    )


def attention_pass(query, grad_att, key_proj, value_proj, inside, row_tiles, col_tiles):
    block_rows = 1
    while (
        block_rows * 2 <= row_tiles
        and row_tiles % (block_rows * 2) == 0
        and (block_rows * col_tiles < 8)
    ):
        block_rows = block_rows * 2
    key_totals = jnp.zeros(key_proj.shape, jnp.float32)
    value_totals = jnp.zeros(key_proj.shape, jnp.float32)
    valid_keys = tile_windows(inside, block_rows, col_tiles)[:, :, 0] > 0.5
    attended, grad_q, key_part, value_part = tile_core(
        into_tiles(query, block_rows, col_tiles),
        into_tiles(grad_att, block_rows, col_tiles),
        tile_windows(key_proj, block_rows, col_tiles),
        tile_windows(value_proj, block_rows, col_tiles),
        valid_keys,
    )
    key_totals = fold_windows(key_totals, key_part, 0, block_rows, col_tiles)
    value_totals = fold_windows(value_totals, value_part, 0, block_rows, col_tiles)
    attended_parts = from_tiles(attended, block_rows, col_tiles)
    query_parts = from_tiles(grad_q, block_rows, col_tiles)
    return (key_totals, value_totals, attended_parts, query_parts)


def inside_mask(height, breadth, margin):
    row_place = (
        lax.axis_index("row") * height - margin + jnp.arange(height + 2 * margin, dtype=jnp.int32)
    )
    col_place = (
        lax.axis_index("col") * breadth - margin + jnp.arange(breadth + 2 * margin, dtype=jnp.int32)
    )
    row_inside = (row_place >= 0) & (row_place < height * lax.axis_size("row"))
    col_inside = (col_place >= 0) & (col_place < breadth * lax.axis_size("col"))
    return (row_inside[:, None] & col_inside[None, :]).astype(jnp.float32)[:, :, None]


def rim_span(pick, length):
    if pick == 0:
        return (0, TILE, 0, TILE)
    if pick == 1:
        return (2 * TILE, length + 2 * TILE, 0, length)
    return (length + 3 * TILE, length + 4 * TILE, length - TILE, length)


def collect_rims(spread, extended, height, breadth):
    total = spread[TILE : TILE + height, TILE : TILE + breadth]
    for row_pick in range(3):
        for col_pick in range(3):
            if row_pick == 1 and col_pick == 1:
                continue
            from_top, from_end, into_top, into_end = rim_span(row_pick, height)
            from_left, from_right, into_left, into_right = rim_span(col_pick, breadth)
            total = total.at[into_top:into_end, into_left:into_right].add(
                extended[from_top:from_end, from_left:from_right]
            )
    return total


def per_device(tokens, grad_out, w_query, w_key, w_value, w_out):
    height, breadth, feature = tokens.shape
    row_tiles = height // TILE
    col_tiles = breadth // TILE
    flat_tokens = tokens.reshape(-1, feature)
    flat_grad = grad_out.reshape(-1, feature)
    contract_rows = (((0,), (0,)), ((), ()))
    contract_last = (((1,), (1,)), ((), ()))
    highest = lax.Precision.HIGHEST
    padded = padded_2(tokens, (("row", 0), ("col", 1)), TILE)
    padded_shape = (height + 2 * TILE, breadth + 2 * TILE, feature)
    flat_padded = padded.reshape(-1, feature)
    query = (
        jnp.dot(flat_tokens, w_query, preferred_element_type=jnp.float32)
        .astype(jnp.bfloat16)
        .reshape(height, breadth, feature)
    )
    key_proj = (
        jnp.dot(flat_padded, w_key, preferred_element_type=jnp.float32)
        .astype(jnp.bfloat16)
        .reshape(padded_shape)
    )
    value_proj = (
        jnp.dot(flat_padded, w_value, preferred_element_type=jnp.float32)
        .astype(jnp.bfloat16)
        .reshape(padded_shape)
    )
    grad_att = lax.dot_general(flat_grad, w_out, contract_last, preferred_element_type=jnp.float32)
    grad_att = grad_att.astype(jnp.bfloat16).reshape(height, breadth, feature)
    inside = inside_mask(height, breadth, TILE)
    key_totals, value_totals, attended_grid, query_grid = attention_pass(
        query, grad_att, key_proj, value_proj, inside, row_tiles, col_tiles
    )
    attended_flat = attended_grid.reshape(-1, feature)
    grad_q_flat = query_grid.reshape(-1, feature)
    padded_float = flat_padded.astype(jnp.float32)
    key_flat = key_totals.reshape(-1, feature)
    value_flat = value_totals.reshape(-1, feature)
    grad_key = lax.dot_general(padded_float, key_flat, contract_rows, precision=highest)
    grad_value = lax.dot_general(padded_float, value_flat, contract_rows, precision=highest)
    own_part = lax.dot_general(
        grad_q_flat, w_query, contract_last, preferred_element_type=jnp.float32
    )
    spread = lax.dot_general(
        key_flat, w_key.astype(jnp.float32), contract_last, precision=highest
    ) + lax.dot_general(value_flat, w_value.astype(jnp.float32), contract_last, precision=highest)
    spread = spread.reshape(padded_shape)
    extended = padded_2(spread.astype(jnp.bfloat16), (("row", 0), ("col", 1)), TILE).astype(
        spread.dtype
    )
    grad_tokens = own_part.reshape(height, breadth, feature) + collect_rims(
        spread, extended, height, breadth
    )
    grad_tokens = grad_tokens.astype(jnp.bfloat16)
    grad_output = lax.dot_general(
        attended_flat, flat_grad, contract_rows, preferred_element_type=jnp.float32
    )
    grad_query = lax.dot_general(
        flat_tokens, grad_q_flat, contract_rows, preferred_element_type=jnp.float32
    )
    summed = lax.psum((grad_query, grad_key, grad_value, grad_output), ("row", "col"))
    return (grad_tokens, summed[0], summed[1], summed[2], summed[3])


def solution(mesh):
    in_specs = (P("row", "col", None), P("row", "col", None), P(), P(), P(), P())
    out_specs = (P("row", "col", None), P(), P(), P(), P())
    return jax.shard_map(
        per_device, mesh=mesh, in_specs=in_specs, out_specs=out_specs, check_vma=False
    )
```

profile of v0, /device:TPU:10, one launch (start us, length us, event | category | flops | bytes accessed | tf_op | source)
XLA Modules:
  0.0 493.9 jit_solution(7431224495533205866)
XLA Ops:
  8.3 7.7 %collective-permute-start.1 = (bf16[8,16,384]{2,1,0:T(8,128)(2,1)S(1)}, bf16[8,16,384]{2,1,0:T(8,128)(2,1)S(1)}, u32[]{:S(2)}, u32[]{:S(2)}) collective-permute-start(bf16[8,16,384]{2,1,0:T(8,128)(2,1)S(1)} %get-tuple-element.383), channel_id=1, source_target_pairs={{16,0},{32,16},{48,32},{64,48},{80,64},{96,80},{112,96},{128,112},... | collective-permute-start | bytes 294920 | tf_op jit(solution)/shard_map/ppermute | solution.py:22
  26.8 6.0 %collective-permute-start.3 = (bf16[32,8,384]{2,1,0:T(8,128)(2,1)S(1)}, bf16[32,8,384]{2,1,0:T(8,128)(2,1)S(1)}, u32[]{:S(2)}, u32[]{:S(2)}) collective-permute-start(bf16[32,8,384]{2,1,0:T(8,128)(2,1)S(1)} %get-tuple-element.382), channel_id=1, source_target_pairs={{1,0},{2,1},{3,2},{4,3},{5,4},{6,5},{7,6},{8,7},{9,8},{10,9},{11,1... | collective-permute-start | bytes 589832 | tf_op jit(solution)/shard_map/ppermute | solution.py:22
  39.9 4.6 reshape_reshape.43
  44.5 6.0 %copy.108 = bf16[4,576,6,64]{1,3,2,0:T(8,128)(2,1)} copy(bf16[4,576,6,64]{3,2,1,0:T(8,128)(2,1)} %reshape_reshape.43) | data formatting | bytes 3538944 | tf_op jit(solution)/shard_map/reshape;reshape | solution.py:78
  51.3 4.4 reshape_reshape.49
  55.7 4.8 copy.107
  63.3 5.0 %fusion.72 = (f32[4,6,64]{2,1,0:T(8,128)S(1)}, f32[4,6,64,576]{3,2,1,0:T(8,128)}) fusion(pred[4,576]{1,0:T(4,128)(4,1)S(1)} %gt.15, bf16[4,64,6,64]{1,3,2,0:T(8,128)(2,1)S(1)} %copy-done.31, bf16[4,576,6,64]{1,3,2,0:T(8,128)(2,1)} %copy.108), kind=kOutput, calls=%fused_computation.178 | convolution fusion | flops 117670464 | bytes 5513472 | tf_op jit(solution)/shard_map/sub | solution.py:87
  68.3 3.1 fusion.23
  74.2 16.3 %fusion.12 = f32[4,576,6,64]{1,3,2,0:T(8,128)} fusion(bf16[4,64,6,64]{1,3,2,0:T(8,128)(2,1)S(1)} %copy-done.31, f32[4,6,64,576]{3,2,1,0:T(8,128)} %fusion.73, f32[4,6,64,576]{3,2,1,0:T(8,128)} %get-tuple-element.399, f32[4,6,64]{2,1,0:T(8,128)S(1)} %get-tuple-element.398), kind=kOutput, calls=%fused_computation.10 | convolution fusion | flops 119441472 | bytes 10819584 | tf_op jit(solution)/shard_map/nhqk,nqhe->nkhe/dot_general | solution.py:101
  91.9 7.5 %copy.123 = f32[4,576,6,64]{3,2,1,0:T(8,128)} copy(f32[4,576,6,64]{1,3,2,0:T(8,128)} %convolution_bitcast_fusion) | data formatting | bytes 7077888 | tf_op jit(solution)/shard_map/nhqk,nqhe->nkhe/transpose | solution.py:98
  99.4 8.0 %reshape_reshape.52 = f32[2,2,3,8,3,8,384]{6,5,4,3,2,1,0:T(8,128)} reshape(f32[4,576,6,64]{3,2,1,0:T(8,128)} %copy.123) | data formatting | bytes 7077888 | tf_op jit(solution)/shard_map/reshape;reshape | solution.py:45
  116.8 6.1 %scatter-add.104 = f32[32,32,384]{2,1,0:T(8,128)S(1)} dynamic-update-slice(f32[32,32,384]{2,1,0:T(8,128)S(1)} %scatter-add.101, f32[16,16,384]{2,1,0:T(8,128)S(1)} %add_select_fusion.1, s32[]{:T(128)} %bitcast.82, s32[]{:T(128)} %bitcast.83, s32[]{:T(128)} %constant.665.clone.1) | dynamic-update-slice | bytes 786436 | tf_op jit(solution)/shard_map/scatter-add | solution.py:53
  124.9 4.8 scatter-add.105
  129.7 7.7 %copy.112 = f32[4,576,6,64]{3,2,1,0:T(8,128)} copy(f32[4,576,6,64]{1,3,2,0:T(8,128)} %fusion.12) | data formatting | bytes 7077888 | tf_op jit(solution)/shard_map/nhqk,nqhe->nkhe/transpose | solution.py:101
  137.4 8.0 %reshape_reshape.51 = f32[2,2,3,8,3,8,384]{6,5,4,3,2,1,0:T(8,128)} reshape(f32[4,576,6,64]{3,2,1,0:T(8,128)} %copy.112) | data formatting | bytes 7077888 | tf_op jit(solution)/shard_map/reshape;reshape | solution.py:45
  153.6 2.8 add_select_fusion.3
  156.5 6.4 %scatter-add.89 = f32[32,32,384]{2,1,0:T(8,128)S(1)} dynamic-update-slice(f32[32,32,384]{2,1,0:T(8,128)S(1)} %scatter-add.86, f32[16,16,384]{2,1,0:T(8,128)} %add_select_fusion.3, s32[]{:T(128)} %bitcast.82, s32[]{:T(128)} %bitcast.83, s32[]{:T(128)} %constant.665.clone.1) | dynamic-update-slice | bytes 786436 | tf_op jit(solution)/shard_map/scatter-add | solution.py:53
  162.9 3.7 add_select_fusion.2
  166.6 6.0 %scatter-add.90 = f32[32,32,384]{2,1,0:T(8,128)S(1)} dynamic-update-slice(f32[32,32,384]{2,1,0:T(8,128)S(1)} %scatter-add.89, f32[16,16,384]{2,1,0:T(8,128)} %add_select_fusion.2, s32[]{:T(128)} %bitcast.87, s32[]{:T(128)} %bitcast.88, s32[]{:T(128)} %constant.665.clone.1) | dynamic-update-slice | bytes 786436 | tf_op jit(solution)/shard_map/scatter-add | solution.py:53
  184.0 6.4 %collective-permute-start.5 = (bf16[8,32,384]{2,1,0:T(8,128)(2,1)S(1)}, bf16[8,32,384]{2,1,0:T(8,128)(2,1)S(1)}, u32[]{:S(2)}, u32[]{:S(2)}) collective-permute-start(bf16[8,32,384]{2,1,0:T(8,128)(2,1)S(1)} %get-tuple-element.362), channel_id=1, source_target_pairs={{16,0},{32,16},{48,32},{64,48},{80,64},{96,80},{112,96},{128,112},... | collective-permute-start | bytes 589832 | tf_op jit(solution)/shard_map/ppermute | solution.py:22
  195.0 14.8 %fusion.24 = bf16[4,64,6,64]{1,3,2,0:T(8,128)(2,1)S(1)} fusion(bf16[4,576,6,64]{1,3,2,0:T(8,128)(2,1)} %copy.108, f32[4,6,64,576]{3,2,1,0:T(8,128)} %fusion.73, f32[4,6,64,576]{3,2,1,0:T(8,128)} %get-tuple-element.399, f32[4,6,64]{2,1,0:T(8,128)S(1)} %get-tuple-element.398), kind=kOutput, calls=%fused_computation.29 | convolution fusion | flops 119539776 | bytes 9050112 | tf_op jit(solution)/shard_map/nhqk,nkhe->nqhe/dot_general | solution.py:104
  210.7 3.1 collective-permute-start.6
  213.8 4.8 collective-permute-start.7
  230.9 250.4 %all-reduce.5.cloned.1.call-done = (f32[384,384]{0,1:T(8,128)}, f32[384,384]{1,0:T(8,128)}, f32[384,384]{1,0:T(8,128)}, f32[384,384]{1,0:T(8,128)}) async-done(((f32[384,384]{0,1:T(8,128)}, f32[384,384]{1,0:T(8,128)}, f32[384,384]{1,0:T(8,128)}, f32[384,384]{1,0:T(8,128)}), (f32[384,384]{0,1:T(8,128)}, f32[384,384]{1,0:T(8,128)}, f32[384,384]{1,0:T(8,128)}, ...) | async-done | bytes 2359312 | tf_op jit(solution)/shard_map/psum | solution.py:235
  (211 shorter events, 80.1 us)
Async XLA Ops:
  7.2 30.1 %copy-start = (bf16[384,384]{1,0:T(8,128)(2,1)S(1)}, bf16[384,384]{1,0:T(8,128)(2,1)}, u32[]{:S(2)}) copy-start(bf16[384,384]{1,0:T(8,128)(2,1)} %param.61) | copy-start | bytes 884740
  7.2 11.7 %copy-start.4 = (bf16[16,16,384]{2,1,0:T(8,128)(2,1)S(1)}, bf16[16,16,384]{2,1,0:T(8,128)(2,1)}, u32[]{:S(2)}) copy-start(bf16[16,16,384]{2,1,0:T(8,128)(2,1)} %param.58) | copy-start | bytes 589828
  7.2 11.4 %copy-start.32 = (bf16[384,384]{1,0:T(8,128)(2,1)S(1)}, bf16[384,384]{1,0:T(8,128)(2,1)}, u32[]{:S(2)}) copy-start(bf16[384,384]{1,0:T(8,128)(2,1)} %param.63) | copy-start | bytes 884740
  7.2 11.4 %copy-start.27 = (bf16[16,16,384]{2,1,0:T(8,128)(2,1)S(1)}, bf16[16,16,384]{2,1,0:T(8,128)(2,1)}, u32[]{:S(2)}) copy-start(bf16[16,16,384]{2,1,0:T(8,128)(2,1)} %param.59) | copy-start | bytes 589828
  7.2 11.7 %copy-start.20 = (bf16[384,384]{1,0:T(8,128)(2,1)S(1)}, bf16[384,384]{1,0:T(8,128)(2,1)}, u32[]{:S(2)}) copy-start(bf16[384,384]{1,0:T(8,128)(2,1)} %param.60) | copy-start | bytes 884740
  7.2 474.1 %all-reduce.5.cloned.1.call-start = ((), (), s32[]{:S(2)}) async-start(), calls=%async_computation | async-start | bytes 4718592 | tf_op jit(solution)/shard_map/psum | solution.py:235
  8.3 16.4 %collective-permute-start.1 = (bf16[8,16,384]{2,1,0:T(8,128)(2,1)S(1)}, bf16[8,16,384]{2,1,0:T(8,128)(2,1)S(1)}, u32[]{:S(2)}, u32[]{:S(2)}) collective-permute-start(bf16[8,16,384]{2,1,0:T(8,128)(2,1)S(1)} %get-tuple-element.383), channel_id=1, source_target_pairs={{16,0},{32,16},{48,32},{64,48},{80,64},{96,80},{112,96},{128,112},... | collective-permute-start | bytes 294920 | tf_op jit(solution)/shard_map/ppermute | solution.py:22
  16.1 8.6 %collective-permute-start = (bf16[8,16,384]{2,1,0:T(8,128)(2,1)S(1)}, bf16[8,16,384]{2,1,0:T(8,128)(2,1)S(1)}, u32[]{:S(2)}, u32[]{:S(2)}) collective-permute-start(bf16[8,16,384]{2,1,0:T(8,128)(2,1)S(1)} %get-tuple-element.384), channel_id=1, source_target_pairs={{0,16},{16,32},{32,48},{48,64},{64,80},{80,96},{96,112},{112,128},... | collective-permute-start | bytes 294920 | tf_op jit(solution)/shard_map/ppermute | solution.py:19
  20.6 12.9 %copy-start.37 = (s32[3]{0:T(128)S(1)}, s32[3]{0:T(128)}, u32[]{:S(2)}) copy-start(s32[3]{0:T(128)} %constant.675.clone.1) | copy-start | bytes 40
  20.6 12.9 %copy-start.38 = (s32[3]{0:T(128)S(1)}, s32[3]{0:T(128)}, u32[]{:S(2)}) copy-start(s32[3]{0:T(128)} %constant.673.clone.1) | copy-start | bytes 40
  21.2 15.5 %copy-start.18 = (bf16[384,384]{1,0:T(8,128)(2,1)S(1)}, bf16[384,384]{1,0:T(8,128)(2,1)}, u32[]{:S(2)}) copy-start(bf16[384,384]{1,0:T(8,128)(2,1)} %param.62) | copy-start | bytes 884740
  24.8 12.5 %copy-start.6 = (bf16[32,16,384]{2,1,0:T(8,128)(2,1)}, bf16[32,16,384]{2,1,0:T(8,128)(2,1)S(1)}, u32[]{:S(2)}) copy-start(bf16[32,16,384]{2,1,0:T(8,128)(2,1)S(1)} %constant_dynamic-update-slice_fusion) | copy-start | bytes 1179652
  24.8 9.4 %collective-permute-start.2 = (bf16[32,8,384]{2,1,0:T(8,128)(2,1)S(1)}, bf16[32,8,384]{2,1,0:T(8,128)(2,1)S(1)}, u32[]{:S(2)}, u32[]{:S(2)}) collective-permute-start(bf16[32,8,384]{2,1,0:T(8,128)(2,1)S(1)} %get-tuple-element.381), channel_id=1, source_target_pairs={{0,1},{1,2},{2,3},{3,4},{4,5},{5,6},{6,7},{7,8},{8,9},{9,10},{10,1... | collective-permute-start | bytes 589832 | tf_op jit(solution)/shard_map/ppermute | solution.py:19
  26.8 9.2 %collective-permute-start.3 = (bf16[32,8,384]{2,1,0:T(8,128)(2,1)S(1)}, bf16[32,8,384]{2,1,0:T(8,128)(2,1)S(1)}, u32[]{:S(2)}, u32[]{:S(2)}) collective-permute-start(bf16[32,8,384]{2,1,0:T(8,128)(2,1)S(1)} %get-tuple-element.382), channel_id=1, source_target_pairs={{1,0},{2,1},{3,2},{4,3},{5,4},{6,5},{7,6},{8,7},{9,8},{10,9},{11,1... | collective-permute-start | bytes 589832 | tf_op jit(solution)/shard_map/ppermute | solution.py:22
  181.7 11.0 %copy-start.3 = (f32[1024,384]{1,0:T(8,128)}, f32[1024,384]{1,0:T(8,128)S(1)}, u32[]{:S(2)}) copy-start(f32[1024,384]{1,0:T(8,128)S(1)} %convolution_add_fusion) | copy-start | bytes 4718596
  181.7 8.7 %copy-start.7 = (bf16[32,16,384]{2,1,0:T(8,128)(2,1)S(1)}, bf16[32,16,384]{2,1,0:T(8,128)(2,1)}, u32[]{:S(2)}) copy-start(bf16[32,16,384]{2,1,0:T(8,128)(2,1)} %copy-done.6) | copy-start | bytes 1179652
  181.7 8.7 %copy-start.34 = (bf16[32,8,384]{2,1,0:T(8,128)(2,1)S(1)}, bf16[32,8,384]{2,1,0:T(8,128)(2,1)}, u32[]{:S(2)}) copy-start(bf16[32,8,384]{2,1,0:T(8,128)(2,1)} %copy-done.33) | copy-start | bytes 589828
  181.9 28.0 %collective-permute-start.4 = (bf16[8,32,384]{2,1,0:T(8,128)(2,1)S(1)}, bf16[8,32,384]{2,1,0:T(8,128)(2,1)S(1)}, u32[]{:S(2)}, u32[]{:S(2)}) collective-permute-start(bf16[8,32,384]{2,1,0:T(8,128)(2,1)S(1)} %get-tuple-element.361), channel_id=1, source_target_pairs={{0,16},{16,32},{32,48},{48,64},{64,80},{80,96},{96,112},{112,128},... | collective-permute-start | bytes 589832 | tf_op jit(solution)/shard_map/ppermute | solution.py:19
  184.0 8.8 %copy-start.2 = (f32[32,32,384]{2,1,0:T(8,128)S(1)}, f32[32,32,384]{2,1,0:T(8,128)}, u32[]{:S(2)}) copy-start(f32[32,32,384]{2,1,0:T(8,128)} %copy-done.1) | copy-start | bytes 4718596
  184.0 25.9 %collective-permute-start.5 = (bf16[8,32,384]{2,1,0:T(8,128)(2,1)S(1)}, bf16[8,32,384]{2,1,0:T(8,128)(2,1)S(1)}, u32[]{:S(2)}, u32[]{:S(2)}) collective-permute-start(bf16[8,32,384]{2,1,0:T(8,128)(2,1)S(1)} %get-tuple-element.362), channel_id=1, source_target_pairs={{16,0},{32,16},{48,32},{64,48},{80,64},{96,80},{112,96},{128,112},... | collective-permute-start | bytes 589832 | tf_op jit(solution)/shard_map/ppermute | solution.py:22
  209.8 8.8 %copy-start.26 = (bf16[2,8,2,8,384]{4,3,2,1,0:T(8,128)(2,1)S(1)}, bf16[2,8,2,8,384]{4,3,2,1,0:T(8,128)(2,1)}, u32[]{:S(2)}) copy-start(bf16[2,8,2,8,384]{4,3,2,1,0:T(8,128)(2,1)} %copy.136) | copy-start | bytes 589828
  209.9 8.8 %copy-start.28 = (bf16[16,16,384]{2,1,0:T(8,128)(2,1)S(1)}, bf16[16,16,384]{2,1,0:T(8,128)(2,1)}, u32[]{:S(2)}) copy-start(bf16[16,16,384]{2,1,0:T(8,128)(2,1)} %param.59) | copy-start | bytes 589828
  210.7 13.8 %collective-permute-start.6 = (bf16[48,8,384]{2,1,0:T(8,128)(2,1)}, bf16[48,8,384]{2,1,0:T(8,128)(2,1)S(1)}, u32[]{:S(2)}, u32[]{:S(2)}) collective-permute-start(bf16[48,8,384]{2,1,0:T(8,128)(2,1)} %get-tuple-element.359), channel_id=1, source_target_pairs={{0,1},{1,2},{2,3},{3,4},{4,5},{5,6},{6,7},{7,8},{8,9},{9,10},{10,1... | collective-permute-start | bytes 884744 | tf_op jit(solution)/shard_map/ppermute | solution.py:19
  213.8 10.6 %collective-permute-start.7 = (bf16[48,8,384]{2,1,0:T(8,128)(2,1)S(1)}, bf16[48,8,384]{2,1,0:T(8,128)(2,1)S(1)}, u32[]{:S(2)}, u32[]{:S(2)}) collective-permute-start(bf16[48,8,384]{2,1,0:T(8,128)(2,1)S(1)} %get-tuple-element.360), channel_id=1, source_target_pairs={{1,0},{2,1},{3,2},{4,3},{5,4},{6,5},{7,6},{8,7},{9,8},{10,9},{11,1... | collective-permute-start | bytes 884744 | tf_op jit(solution)/shard_map/ppermute | solution.py:22
  (25 other events, 73.8 us)
Sparse Core Ops, SparseCore 0:
  224.5 256.7 all-reduce.4
where the time goes:
time: 496 us; the launch traced here: 494 us
  waiting for transfers between devices  255 us (51%)
  local copies, waits for them, and re-layouts  112 us (23%)
  matrix products  57.6 us (12%)
  starting transfers between devices  34.1 us (7%)
  other arithmetic  20.1 us (4%)
  between operations  15.2 us (3%)
    psum x1, waiting for transfers between devices, per_device(): lax.psum((grad_query, grad_key, grad_value, grad_output), ('row', 'col'))  250 us
    ppermute x4, starting transfers between devices, padded_2(): lax.ppermute(lax.slice_in_dim(block, 0, width, axis=dim), axis, backward)  25 us
    scatter-add x6, local copies, waits for them, and re-layouts, fold_windows(): totals = totals.at[offset + row_pick * TILE:offset + row_pick * TILE + ro...  23.7 us
    dot_general x1, matrix products, tile_core(): jnp.einsum('nhqk,nqhe->nkhe', grad_score, query_heads, preferred_element_...  16.3 us
    another operation x2, local copies, waits for them, and re-layouts, fold_windows(): pieces = contrib.reshape(row_count, col_count, 3, TILE, 3, TILE, feature)  16.1 us
    transpose x20, local copies, waits for them, and re-layouts, fold_windows(): jnp.transpose(pieces[:, :, row_pick, :, col_pick, :, :], (0, 2, 1, 3, 4))  15.1 us
    dot_general x1, matrix products, tile_core(): jnp.einsum('nhqk,nkhe->nqhe', grad_score, key_heads, preferred_element_ty...  14.8 us
    another operation x7, other arithmetic  13.5 us
  transfers between devices with their start and end apart: 9, of which 3 were waited for; matrix products, arithmetic and copies ran while one was open for 7% of the time, Pallas kernels for 0%

commit v1 on v0

v1 whole, which is shorter than its diff:
```python
import functools

import jax
import jax.numpy as jnp
from jax import lax
from jax.experimental import pallas as pl
from jax.experimental.pallas import tpu as pltpu
from jax.sharding import PartitionSpec as P

HEADS = 6
HEAD_DIM = 64
TILE = 8
AREA = TILE * TILE
BOTH = ("row", "col")
VMEM = pltpu.MemorySpace.VMEM
SMEM = pltpu.MemorySpace.SMEM
MASKED = -1e30
GROUPS = ((0, 4), (4, 2))


def dot(a, b, dims=((1,), (0,))):
    return lax.dot_general(a, b, (dims, ((), ())), preferred_element_type=jnp.float32)


NT = ((1,), (1,))
TN = ((0,), (0,))


def swap_pairs(size, kind):
    if kind == 0:
        return [(i, i ^ 1) for i in range(size)]
    return [(i, ((i + 1) ^ 1) - 1) for i in range(1, size - 1)]


def swap(block, axis, kind):
    return lax.ppermute(block, axis, swap_pairs(lax.axis_size(axis), kind))


def collect_halo(tokens):
    row_odd = lax.rem(lax.axis_index("row"), 2) == 1
    col_odd = lax.rem(lax.axis_index("col"), 2) == 1
    low, high = tokens[:TILE], tokens[-TILE:]
    first = swap(jnp.where(row_odd, low, high), "row", 0)
    second = swap(jnp.where(row_odd, high, low), "row", 1)
    above = jnp.where(row_odd, first, second)
    below = jnp.where(row_odd, second, first)
    tall = jnp.concatenate([above, tokens, below], axis=0)
    left, right = tall[:, :TILE], tall[:, -TILE:]
    strip_0 = swap(jnp.where(col_odd, left, right), "col", 0)
    strip_1 = swap(jnp.where(col_odd, right, left), "col", 1)
    return tall, strip_0, strip_1


def tile_of(block, row, col):
    part = block[row * TILE : (row + 1) * TILE, col * TILE : (col + 1) * TILE, :]
    return part.reshape(AREA, part.shape[-1]).astype(jnp.bfloat16)


def attention_kernel(
    place, tall, strip_0, strip_1, grad_out, w_query, w_key, w_value, w_out,
    grads, own, send_0, send_1,
    padded, key, value, key_total, value_total, flat_grad, query, grad_att, attended, grad_q,
):
    feature = w_query.shape[0]
    row_at, row_last, col_at, col_last = place[0], place[1], place[2], place[3]
    col_even = lax.rem(col_at, 2) == 0

    middle = tall[...].astype(jnp.float32)
    part_0 = strip_0[...].astype(jnp.float32)
    part_1 = strip_1[...].astype(jnp.float32)
    left = jnp.where(col_even, part_1, part_0)
    right = jnp.where(col_even, part_0, part_1)
    for i in range(4):
        for j in range(4):
            at = (i * 4 + j) * AREA
            if j == 0:
                padded[at : at + AREA, :] = tile_of(left, i, 0)
            elif j == 3:
                padded[at : at + AREA, :] = tile_of(right, i, 0)
            else:
                padded[at : at + AREA, :] = tile_of(middle, i, j - 1)
    outer = grad_out[...].astype(jnp.float32)
    for i in range(2):
        for j in range(2):
            at = (i * 2 + j) * AREA
            flat_grad[at : at + AREA, :] = tile_of(outer, i, j)

    def own_tokens():
        return jnp.concatenate([padded[320:448, :], padded[576:704, :]], axis=0)

    score_scale = HEAD_DIM**-0.5
    query[...] = (
        dot(own_tokens(), w_query[...]).astype(jnp.bfloat16).astype(jnp.float32) * score_scale
    ).astype(jnp.bfloat16)
    grad_att[...] = dot(flat_grad[...], w_out[...], NT).astype(jnp.bfloat16)
    key[...] = dot(padded[...], w_key[...]).astype(jnp.bfloat16)
    value[...] = dot(padded[...], w_value[...]).astype(jnp.bfloat16)
    key_total[...] = jnp.zeros_like(key_total)
    value_total[...] = jnp.zeros_like(value_total)

    zero, masked = jnp.float32(0.0), jnp.float32(MASKED)
    row_bias = [
        jnp.where(row_at == 0, masked, zero), None, None, jnp.where(row_at == row_last, masked, zero)
    ]
    col_bias = [
        jnp.where(col_at == 0, masked, zero), None, None, jnp.where(col_at == col_last, masked, zero)
    ]

    def bias_of(i, j):
        if row_bias[i] is None:
            return col_bias[j]
        if col_bias[j] is None:
            return row_bias[i]
        return jnp.minimum(row_bias[i], col_bias[j])

    for i in range(2):
        for j in range(2):
            mine = slice((i * 2 + j) * AREA, (i * 2 + j + 1) * AREA)
            rows = [((i + a) * 4 + j) * AREA for a in range(3)]
            for first, count in GROUPS:
                wide = count * HEAD_DIM
                cols = slice(first * HEAD_DIM, first * HEAD_DIM + wide)
                here = lax.broadcasted_iota(jnp.int32, (wide, wide), 0) // HEAD_DIM
                there = lax.broadcasted_iota(jnp.int32, (wide, wide), 1) // HEAD_DIM
                same = here == there

                def spread_heads(x):
                    full = jnp.concatenate([x.astype(jnp.float32)] * count, axis=0)
                    return jnp.where(same, full, 0.0).astype(jnp.bfloat16)

                def gather_heads(x):
                    kept = jnp.where(same, x, 0.0)
                    total = kept[:AREA]
                    for h in range(1, count):
                        total = total + kept[h * AREA : (h + 1) * AREA]
                    return total

                query_heads = spread_heads(query[mine, cols])
                grad_heads = spread_heads(grad_att[mine, cols])
                key_win = jnp.concatenate([key[r : r + 3 * AREA, cols] for r in rows], axis=0)
                value_win = jnp.concatenate([value[r : r + 3 * AREA, cols] for r in rows], axis=0)
                scores = dot(key_win, query_heads, NT)
                slabs = []
                for a in range(3):
                    for b in range(3):
                        slab = scores[(a * 3 + b) * AREA : (a * 3 + b + 1) * AREA]
                        bias = bias_of(i + a, j + b)
                        slabs.append(slab if bias is None else slab + bias)
                scores = jnp.concatenate(slabs, axis=0)
                top = jnp.max(scores, axis=0, keepdims=True)
                terms = jnp.exp(scores - top)
                weight = terms * (1.0 / jnp.sum(terms, axis=0, keepdims=True))
                weight_half = weight.astype(jnp.bfloat16)
                grad_weight = dot(value_win, grad_heads, NT)
                row_dot = jnp.sum(weight * grad_weight, axis=0, keepdims=True)
                grad_score = (weight * (grad_weight - row_dot)).astype(jnp.bfloat16)
                value_part = dot(weight_half, grad_heads)
                key_part = dot(grad_score, query_heads)
                for a in range(3):
                    span, part = slice(rows[a], rows[a] + 3 * AREA), slice(a * 192, a * 192 + 192)
                    value_total[span, cols] += value_part[part]
                    key_total[span, cols] += key_part[part]
                attended[mine, cols] = gather_heads(dot(weight_half, value_win, TN)).astype(
                    jnp.bfloat16
                )
                grad_q[mine, cols] = (
                    gather_heads(dot(grad_score, key_win, TN)) * score_scale
                ).astype(jnp.bfloat16)

    key_grad = key_total[...].astype(jnp.bfloat16)
    value_grad = value_total[...].astype(jnp.bfloat16)
    tokens_all = padded[...]
    grads[0:feature, :] = dot(attended[...], flat_grad[...], TN).astype(jnp.bfloat16)
    grads[feature : 2 * feature, :] = dot(tokens_all, value_grad, TN).astype(jnp.bfloat16)
    grads[2 * feature : 3 * feature, :] = dot(own_tokens(), grad_q[...], TN).astype(jnp.bfloat16)
    grads[3 * feature :, :] = dot(tokens_all, key_grad, TN).astype(jnp.bfloat16)

    spread = dot(key_grad, w_key[...], NT) + dot(value_grad, w_value[...], NT)
    query_part = dot(grad_q[...], w_query[...], NT)
    for i in range(4):
        at = i * 4 * AREA
        west, east = spread[at : at + AREA], spread[at + 3 * AREA : at + 4 * AREA]
        send_0[i, :, :] = jnp.where(col_even, east, west).astype(jnp.bfloat16)
        send_1[i, :, :] = jnp.where(col_even, west, east).astype(jnp.bfloat16)
        centre = spread[at + AREA : at + 3 * AREA]
        if i in (1, 2):
            centre = centre + query_part[(i - 1) * 2 * AREA : i * 2 * AREA]
        own[i, 0, :, :] = centre[:AREA]
        own[i, 1, :, :] = centre[AREA:]


def attention(place, tall, strip_0, strip_1, grad_out, w_query, w_key, w_value, w_out):
    feature = w_query.shape[0]
    whole = pl.BlockSpec(memory_space=VMEM)
    half, full = jnp.bfloat16, jnp.float32
    return pl.pallas_call(
        attention_kernel,
        out_shape=(
            jax.ShapeDtypeStruct((4 * feature, feature), half),
            jax.ShapeDtypeStruct((4, 2, AREA, feature), full),
            jax.ShapeDtypeStruct((4, AREA, feature), half),
            jax.ShapeDtypeStruct((4, AREA, feature), half),
        ),
        in_specs=[pl.BlockSpec(memory_space=SMEM)] + [whole] * 8,
        out_specs=(whole,) * 4,
        scratch_shapes=[
            pltpu.VMEM((16 * AREA, feature), half),
            pltpu.VMEM((16 * AREA, feature), half),
            pltpu.VMEM((16 * AREA, feature), half),
            pltpu.VMEM((16 * AREA, feature), full),
            pltpu.VMEM((16 * AREA, feature), full),
            pltpu.VMEM((4 * AREA, feature), half),
            pltpu.VMEM((4 * AREA, feature), half),
            pltpu.VMEM((4 * AREA, feature), half),
            pltpu.VMEM((4 * AREA, feature), half),
            pltpu.VMEM((4 * AREA, feature), half),
        ],
        compiler_params=pltpu.CompilerParams(vmem_limit_bytes=40 * 2**20),
        name="attention",
    )(place, tall, strip_0, strip_1, grad_out, w_query, w_key, w_value, w_out)


def columns_kernel(place, own, from_0, from_1, summed, send_0, send_1):
    row_even = lax.rem(place[0], 2) == 0
    col_even = lax.rem(place[2], 2) == 0
    west = jnp.where(col_even, from_1[...], from_0[...]).astype(jnp.float32)
    east = jnp.where(col_even, from_0[...], from_1[...]).astype(jnp.float32)
    for j, got in ((0, west), (1, east)):
        total = own[:, j, :, :] + got
        north, south = total[0], total[3]
        send_0[j, :, :] = jnp.where(row_even, south, north).astype(jnp.bfloat16)
        send_1[j, :, :] = jnp.where(row_even, north, south).astype(jnp.bfloat16)
        summed[0, j, :, :] = total[1]
        summed[1, j, :, :] = total[2]


def rows_kernel(place, summed, from_0, from_1, out, whole):
    row_even = lax.rem(place[0], 2) == 0
    north = jnp.where(row_even, from_1[...], from_0[...]).astype(jnp.float32)
    south = jnp.where(row_even, from_0[...], from_1[...]).astype(jnp.float32)
    for i, got in ((0, north), (1, south)):
        for j in range(2):
            total = summed[i, j, :, :] + got[j]
            whole[i * TILE : (i + 1) * TILE, j * TILE : (j + 1) * TILE, :] = total.reshape(
                TILE, TILE, total.shape[-1]
            )
    out[...] = whole[...].astype(jnp.bfloat16)


def collect_token_grads(place, own, send_0, send_1):
    feature = own.shape[-1]
    whole, scalars = pl.BlockSpec(memory_space=VMEM), pl.BlockSpec(memory_space=SMEM)
    half = jax.ShapeDtypeStruct((2, AREA, feature), jnp.bfloat16)
    from_0, from_1 = swap(send_0, "col", 0), swap(send_1, "col", 1)
    summed, send_0, send_1 = pl.pallas_call(
        columns_kernel,
        out_shape=(jax.ShapeDtypeStruct((2, 2, AREA, feature), jnp.float32), half, half),
        in_specs=[scalars] + [whole] * 3,
        out_specs=(whole,) * 3,
        name="columns",
    )(place, own, from_0, from_1)
    from_0, from_1 = swap(send_0, "row", 0), swap(send_1, "row", 1)
    return pl.pallas_call(
        rows_kernel,
        out_shape=jax.ShapeDtypeStruct((2 * TILE, 2 * TILE, feature), jnp.bfloat16),
        in_specs=[scalars] + [whole] * 3,
        out_specs=whole,
        scratch_shapes=[pltpu.VMEM((2 * TILE, 2 * TILE, feature), jnp.float32)],
        name="rows",
    )(place, summed, from_0, from_1)


def device_groups():
    planes = [
        [(a << 7) | (z << 4) | (b << 1) | c for a in range(2) for b in range(8)]
        for z in range(8)
        for c in range(2)
    ]
    lines = [[(a << 7) | (z << 4) | b for z in range(8)] for a in range(2) for b in range(16)]
    return planes, lines


def exchange(pieces, groups):
    return lax.all_to_all(pieces, BOTH, 0, 0, tiled=True, axis_index_groups=groups)


def add_up(pieces):
    return jnp.sum(pieces.astype(jnp.float32), axis=0).astype(jnp.bfloat16)


def sum_over_devices(grads):
    planes, lines = device_groups()
    core = lax.rem(lax.axis_index("col"), 2)
    feature = grads.shape[-1]
    half = grads.shape[0] // 2
    keep = lax.dynamic_slice_in_dim(grads, core * half, half, 0)
    give = lax.dynamic_slice_in_dim(grads, (1 - core) * half, half, 0)
    with jax.named_scope("core_sum"):
        part = add_up(jnp.stack([keep, swap(give, "col", 0)]))
    with jax.named_scope("plane_sum"):
        part = add_up(exchange(part.reshape(16, -1, feature), planes))
    with jax.named_scope("line_sum"):
        part = add_up(exchange(jnp.broadcast_to(part, (8,) + part.shape), lines))
    with jax.named_scope("plane_gather"):
        part = exchange(jnp.broadcast_to(part, (16,) + part.shape), planes)
        part = part.reshape(half, feature)
    with jax.named_scope("core_gather"):
        other = swap(part, "col", 0)
        first = jnp.where(core == 0, part, other).astype(jnp.float32)
        second = jnp.where(core == 0, other, part).astype(jnp.float32)
    return first[:feature], first[feature:], second[:feature], second[feature:]


def per_device(tokens, grad_out, w_query, w_key, w_value, w_out):
    place = jnp.stack(
        [
            lax.axis_index("row"),
            lax.axis_size("row") - 1,
            lax.axis_index("col"),
            lax.axis_size("col") - 1,
        ]
    ).astype(jnp.int32)
    tall, strip_0, strip_1 = collect_halo(tokens)
    grads, own, send_0, send_1 = attention(
        place, tall, strip_0, strip_1, grad_out, w_query, w_key, w_value, w_out
    )
    grad_tokens = collect_token_grads(place, own, send_0, send_1)
    grad_output, grad_value, grad_query, grad_key = sum_over_devices(grads)
    return grad_tokens, grad_query, grad_key, grad_value, grad_output


def solution(mesh):
    in_specs = (P("row", "col", None), P("row", "col", None), P(), P(), P(), P())
    out_specs = (P("row", "col", None), P(), P(), P(), P())
    return jax.shard_map(
        per_device, mesh=mesh, in_specs=in_specs, out_specs=out_specs, check_vma=False
    )
```

time: 496 us -> 114 us (0.23)
  waiting for transfers between devices: 255 us -> 21.8 us
  local copies, waits for them, and re-layouts: 112 us -> 4.48 us
  matrix products: 57.6 us -> 0 us
  blocking collectives: 0 us -> 47.8 us
  other arithmetic: 20.1 us -> 2.69 us
  between operations: 15.2 us -> 0.87 us
  Pallas kernels: 0 us -> 13.7 us
  starting transfers between devices: 34.1 us -> 22.7 us
    psum x1 -> x0, waiting for transfers between devices: 250 us -> none  [per_device(): lax.psum((grad_query, grad_key, grad_value, grad_output), ('row', 'col'))]
    dot_general x16 -> x0, matrix products: 52.6 us -> none  [the longest x1 16.3 us: tile_core(): jnp.einsum('nhqk,nqhe->nkhe', grad_score, query_heads, preferred_element_...]
    all_to_all x0 -> x3, blocking collectives: none -> 47.8 us  [exchange(): lax.all_to_all(pieces, BOTH, 0, 0, tiled=True, axis_index_groups=groups)]
    another operation x27 -> x0, local copies, waits for them, and re-layouts: 41.3 us -> none  [the longest x2 16.1 us: fold_windows(): pieces = contrib.reshape(row_count, col_count, 3, TILE, 3, TILE, feature)]
    transpose x24 -> x0, local copies, waits for them, and re-layouts: 30.9 us -> none  [the longest x20 15.1 us: fold_windows(): jnp.transpose(pieces[:, :, row_pick, :, col_pick, :, :], (0, 2, 1, 3, 4))]
    scatter-add x7 -> x0, local copies, waits for them, and re-layouts: 25.2 us -> none  [the longest x6 23.7 us: fold_windows(): totals = totals.at[offset + row_pick * TILE:offset + row_pick * TILE + ro...]
    ppermute x8 -> x10, waiting for transfers between devices: 4.54 us -> 21.8 us  [swap(): return lax.ppermute(block, axis, swap_pairs(lax.axis_size(axis), kind))]
    another operation x18 -> x1, other arithmetic: 14.6 us -> 0.08 us  [per_device(): jnp.stack([lax.axis_index('row'), lax.axis_size('row') - 1, lax.axis_inde...]
  transfers between devices with their start and end apart: 9 -> 10, of which waited for: 3 -> 5; matrix products, arithmetic and copies ran while one was open for 7% -> 0% of each run, Pallas kernels for 0% -> 3%
where the time goes in v1:
time: 114 us
  blocking collectives  47.8 us (42%)
  starting transfers between devices  22.7 us (20%)
  waiting for transfers between devices  21.8 us (19%)
  Pallas kernels  13.7 us (12%)
  local copies, waits for them, and re-layouts  4.48 us (4%)
  other arithmetic  2.69 us (2%)
    all_to_all x3, blocking collectives, exchange(): lax.all_to_all(pieces, BOTH, 0, 0, tiled=True, axis_index_groups=groups)  47.8 us
    ppermute x10, starting transfers between devices, swap(): return lax.ppermute(block, axis, swap_pairs(lax.axis_size(axis), kind))  22.7 us
    ppermute x10, waiting for transfers between devices, swap(): return lax.ppermute(block, axis, swap_pairs(lax.axis_size(axis), kind))  21.8 us
    pallas_call x1, Pallas kernels, attention(): pl.pallas_call(attention_kernel, out_shape=(jax.ShapeDtypeStruct((4 * fea...  9.78 us
    unnamed x26, local copies, waits for them, and re-layouts  2.9 us
  transfers between devices with their start and end apart: 10, of which 5 were waited for; matrix products, arithmetic and copies ran while one was open for 0% of the time, Pallas kernels for 3%

profile of v1, /device:TPU:10, one launch (start us, length us, event | category | flops | bytes accessed | tf_op | source)
XLA Modules:
  0.0 114.1 jit_solution(16870076929833061272)
XLA Ops:
  0.7 1.1 broadcast_select_fusion.5
  1.8 2.0 %collective-permute-start = (bf16[8,16,384]{2,1,0:T(8,128)(2,1)S(1)}, bf16[8,16,384]{2,1,0:T(8,128)(2,1)S(1)}, u32[]{:S(2)}, u32[]{:S(2)}) collective-permute-start(bf16[8,16,384]{2,1,0:T(8,128)(2,1)S(1)} %get-tuple-element.29), channel_id=1, source_target_pairs={{0,16},{16,0},{32,48},{48,32},{64,80},{80,64},{96,112},{112,96},{1... | collective-permute-start | bytes 294920 | tf_op jit(solution)/shard_map/ppermute | solution.py:36
  3.8 6.8 %collective-permute-start.1 = (bf16[8,16,384]{2,1,0:T(8,128)(2,1)S(1)}, bf16[8,16,384]{2,1,0:T(8,128)(2,1)S(1)}, u32[]{:S(2)}, u32[]{:S(2)}) collective-permute-start(bf16[8,16,384]{2,1,0:T(8,128)(2,1)S(1)} %get-tuple-element.30), channel_id=1, source_target_pairs={{16,32},{32,16},{48,64},{64,48},{80,96},{96,80},{112,128},{128,112... | collective-permute-start | bytes 294920 | tf_op jit(solution)/shard_map/ppermute | solution.py:36
  10.6 2.6 %collective-permute-done.1 = bf16[8,16,384]{2,1,0:T(8,128)(2,1)S(1)} collective-permute-done((bf16[8,16,384]{2,1,0:T(8,128)(2,1)S(1)}, bf16[8,16,384]{2,1,0:T(8,128)(2,1)S(1)}, u32[]{:S(2)}, u32[]{:S(2)}) %collective-permute-start.1) | collective-permute-done | bytes 98336 | tf_op jit(solution)/shard_map/ppermute | solution.py:36
  13.2 1.0 pad_maximum_fusion.tall
  14.2 2.5 %collective-permute-start.3 = (bf16[32,8,384]{2,1,0:T(8,128)(2,1)S(1)}, bf16[32,8,384]{2,1,0:T(8,128)(2,1)S(1)}, u32[]{:S(2)}, u32[]{:S(2)}) collective-permute-start(bf16[32,8,384]{2,1,0:T(8,128)(2,1)S(1)} %get-tuple-element.25), channel_id=1, source_target_pairs={{1,2},{2,1},{3,4},{4,3},{5,6},{6,5},{7,8},{8,7},{9,10},{10,9},{11,... | collective-permute-start | bytes 589832 | tf_op jit(solution)/shard_map/ppermute | solution.py:36
  16.8 2.0 %collective-permute-start.2 = (bf16[32,8,384]{2,1,0:T(8,128)(2,1)S(1)}, bf16[32,8,384]{2,1,0:T(8,128)(2,1)S(1)}, u32[]{:S(2)}, u32[]{:S(2)}) collective-permute-start(bf16[32,8,384]{2,1,0:T(8,128)(2,1)S(1)} %get-tuple-element.26), channel_id=1, source_target_pairs={{0,1},{1,0},{2,3},{3,2},{4,5},{5,4},{6,7},{7,6},{8,9},{9,8},{10,11... | collective-permute-start | bytes 589832 | tf_op jit(solution)/shard_map/ppermute | solution.py:36
  18.9 5.3 %collective-permute-done.3.strip_1 = bf16[32,8,384]{2,1,0:T(8,128)(2,1)S(1)} collective-permute-done((bf16[32,8,384]{2,1,0:T(8,128)(2,1)S(1)}, bf16[32,8,384]{2,1,0:T(8,128)(2,1)S(1)}, u32[]{:S(2)}, u32[]{:S(2)}) %collective-permute-start.3) | collective-permute-done | bytes 196640 | tf_op jit(solution)/shard_map/ppermute | solution.py:36
  24.3 9.8 %attention.1 = (bf16[1536,384]{1,0:T(8,128)(2,1)S(1)}, f32[4,2,64,384]{3,2,1,0:T(8,128)S(1)}, bf16[4,64,384]{2,1,0:T(8,128)(2,1)S(1)}, bf16[4,64,384]{2,1,0:T(8,128)(2,1)S(1)}) custom-call(s32[4]{0:T(128)S(1)} %pad_add_fusion.place, bf16[32,16,384]{2,1,0:T(8,128)(2,1)S(1)} %pad_maximum_fusion.tall, bf16[32,8,384]{2,1,0:T(8,128)(2,1)S(1)} %collective-permute-done.2.strip_0, ...), custom_call_target="tpu_custom_call" | custom-call | tf_op jit(solution)/shard_map/attention/pallas_call | solution.py:196
  34.0 0.9 copy-done
  34.9 0.7 copy-done.7
  35.8 2.0 %collective-permute-done.8 = bf16[768,384]{1,0:T(8,128)(2,1)S(1)} collective-permute-done((bf16[768,384]{1,0:T(8,128)(2,1)S(1)}, bf16[768,384]{1,0:T(8,128)(2,1)S(1)}, u32[]{:S(2)}, u32[]{:S(2)}) %collective-permute-start.8) | collective-permute-done | bytes 589856 | tf_op jit(solution)/shard_map/core_sum/ppermute | solution.py:36
  37.9 17.1 %all_to_all.15 = bf16[16,48,384]{2,1,0:T(8,128)(2,1)S(1)} all-to-all(bf16[16,48,384]{2,1,0:T(8,128)(2,1)S(1)} %bitcast.6), channel_id=1, replica_groups={{0,2,4,6,8,10,12,14,128,130,132,134,136,138,140,142},{1,3,5,7,9,11,13,1..., dimensions={0} | all-to-all | bytes 1179648 | tf_op jit(solution)/shard_map/plane_sum/all_to_all | solution.py:284
  55.1 16.7 %all_to_all.16 = bf16[8,48,384]{2,1,0:T(8,128)(2,1)S(1)} all-to-all(bf16[8,48,384]{2,1,0:T(8,128)(2,1)S(1)} %broadcast_in_dim.6), channel_id=1, replica_groups={{0,16,32,48,64,80,96,112},{1,17,33,49,65,81,97,113},{2,18,34,50,66,82,9..., dimensions={0} | all-to-all | bytes 589824 | tf_op jit(solution)/shard_map/line_sum/all_to_all | solution.py:284
  71.9 14.0 %all_to_all.17 = bf16[16,48,384]{2,1,0:T(8,128)(2,1)S(1)} all-to-all(bf16[16,48,384]{2,1,0:T(8,128)(2,1)S(1)} %broadcast_in_dim.7), channel_id=1, replica_groups={{0,2,4,6,8,10,12,14,128,130,132,134,136,138,140,142},{1,3,5,7,9,11,13,1..., dimensions={0} | all-to-all | bytes 1179648 | tf_op jit(solution)/shard_map/plane_gather/all_to_all | solution.py:284
  86.5 4.0 %collective-permute-start.5 = (bf16[4,64,384]{2,1,0:T(8,128)(2,1)S(1)}, bf16[4,64,384]{2,1,0:T(8,128)(2,1)S(1)}, u32[]{:S(2)}, u32[]{:S(2)}) collective-permute-start(bf16[4,64,384]{2,1,0:T(8,128)(2,1)S(1)} %get-tuple-element.14), channel_id=1, source_target_pairs={{1,2},{2,1},{3,4},{4,3},{5,6},{6,5},{7,8},{8,7},{9,10},{10,9},{11,... | collective-permute-start | bytes 589832 | tf_op jit(solution)/shard_map/ppermute | solution.py:36
  90.5 7.3 %collective-permute-done.5.from_1 = bf16[4,64,384]{2,1,0:T(8,128)(2,1)S(1)} collective-permute-done((bf16[4,64,384]{2,1,0:T(8,128)(2,1)S(1)}, bf16[4,64,384]{2,1,0:T(8,128)(2,1)S(1)}, u32[]{:S(2)}, u32[]{:S(2)}) %collective-permute-start.5) | collective-permute-done | bytes 196640 | tf_op jit(solution)/shard_map/ppermute | solution.py:36
  97.8 0.7 copy-done.10
  98.4 2.2 %columns.1 = (f32[2,2,64,384]{3,2,1,0:T(8,128)}, bf16[2,64,384]{2,1,0:T(8,128)(2,1)}, bf16[2,64,384]{2,1,0:T(8,128)(2,1)}) custom-call(s32[4]{0:T(128)} %copy-done.6, f32[4,2,64,384]{3,2,1,0:T(8,128)} %copy-done, bf16[4,64,384]{2,1,0:T(8,128)(2,1)} %copy-done.9, bf16[4,64,384]{2,1,0:T(8,128)(2,1)} %copy-done.10), custom_call_target="tpu_custom_call" | custom-call | tf_op jit(solution)/shard_map/columns/pallas_call | solution.py:255
  101.2 4.2 %collective-permute-start.7 = (bf16[2,64,384]{2,1,0:T(8,128)(2,1)}, bf16[2,64,384]{2,1,0:T(8,128)(2,1)S(1)}, u32[]{:S(2)}, u32[]{:S(2)}) collective-permute-start(bf16[2,64,384]{2,1,0:T(8,128)(2,1)} %get-tuple-element.17), channel_id=1, source_target_pairs={{16,32},{32,16},{48,64},{64,48},{80,96},{96,80},{112,128},{128,112... | collective-permute-start | bytes 294920 | tf_op jit(solution)/shard_map/ppermute | solution.py:36
  105.4 4.6 %collective-permute-done.7.from_1 = bf16[2,64,384]{2,1,0:T(8,128)(2,1)S(1)} collective-permute-done((bf16[2,64,384]{2,1,0:T(8,128)(2,1)}, bf16[2,64,384]{2,1,0:T(8,128)(2,1)S(1)}, u32[]{:S(2)}, u32[]{:S(2)}) %collective-permute-start.7) | collective-permute-done | bytes 98336 | tf_op jit(solution)/shard_map/ppermute | solution.py:36
  110.0 0.6 copy-done.12
  110.6 1.8 %rows.1 = bf16[16,16,384]{2,1,0:T(8,128)(2,1)} custom-call(s32[4]{0:T(128)} %copy-done.6, f32[2,2,64,384]{3,2,1,0:T(8,128)} %get-tuple-element.15.summed, bf16[2,64,384]{2,1,0:T(8,128)(2,1)} %copy-done.11, bf16[2,64,384]{2,1,0:T(8,128)(2,1)} %copy-done.12), custom_call_target="tpu_custom_call" | custom-call | tf_op jit(solution)/shard_map/rows/pallas_call | solution.py:263
  112.6 1.4 %fusion = (f32[384,384]{1,0:T(8,128)}, f32[384,384]{1,0:T(8,128)}, f32[384,384]{1,0:T(8,128)}, f32[384,384]{1,0:T(8,128)}) fusion(f32[768,384]{1,0:T(8,128)S(1)} %get-tuple-element.21, f32[768,384]{1,0:T(8,128)S(1)} %get-tuple-element.22), kind=kLoop, calls=%fused_computation.12 | loop fusion | bytes 4718592 | tf_op jit(solution)/shard_map/slice | solution.py:311
  (41 shorter events, 2.0 us)
Async XLA Ops:
  0.6 23.6 %copy-start.1 = (bf16[384,384]{1,0:T(8,128)(2,1)S(1)}, bf16[384,384]{1,0:T(8,128)(2,1)}, u32[]{:S(2)}) copy-start(bf16[384,384]{1,0:T(8,128)(2,1)} %w_query.1) | copy-start | bytes 884740
  0.6 23.6 %copy-start.2 = (bf16[384,384]{1,0:T(8,128)(2,1)S(1)}, bf16[384,384]{1,0:T(8,128)(2,1)}, u32[]{:S(2)}) copy-start(bf16[384,384]{1,0:T(8,128)(2,1)} %w_key.1) | copy-start | bytes 884740
  0.7 23.6 %copy-start.3 = (bf16[384,384]{1,0:T(8,128)(2,1)S(1)}, bf16[384,384]{1,0:T(8,128)(2,1)}, u32[]{:S(2)}) copy-start(bf16[384,384]{1,0:T(8,128)(2,1)} %w_value.1) | copy-start | bytes 884740
  0.7 23.6 %copy-start.4 = (bf16[384,384]{1,0:T(8,128)(2,1)S(1)}, bf16[384,384]{1,0:T(8,128)(2,1)}, u32[]{:S(2)}) copy-start(bf16[384,384]{1,0:T(8,128)(2,1)} %w_out.1) | copy-start | bytes 884740
  0.7 23.6 %copy-start.5 = (bf16[16,16,384]{2,1,0:T(8,128)(2,1)S(1)}, bf16[16,16,384]{2,1,0:T(8,128)(2,1)}, u32[]{:S(2)}) copy-start(bf16[16,16,384]{2,1,0:T(8,128)(2,1)} %grad_out.1) | copy-start | bytes 589828
  1.8 8.8 %collective-permute-start = (bf16[8,16,384]{2,1,0:T(8,128)(2,1)S(1)}, bf16[8,16,384]{2,1,0:T(8,128)(2,1)S(1)}, u32[]{:S(2)}, u32[]{:S(2)}) collective-permute-start(bf16[8,16,384]{2,1,0:T(8,128)(2,1)S(1)} %get-tuple-element.29), channel_id=1, source_target_pairs={{0,16},{16,0},{32,48},{48,32},{64,80},{80,64},{96,112},{112,96},{1... | collective-permute-start | bytes 294920 | tf_op jit(solution)/shard_map/ppermute | solution.py:36
  3.8 9.4 %collective-permute-start.1 = (bf16[8,16,384]{2,1,0:T(8,128)(2,1)S(1)}, bf16[8,16,384]{2,1,0:T(8,128)(2,1)S(1)}, u32[]{:S(2)}, u32[]{:S(2)}) collective-permute-start(bf16[8,16,384]{2,1,0:T(8,128)(2,1)S(1)} %get-tuple-element.30), channel_id=1, source_target_pairs={{16,32},{32,16},{48,64},{64,48},{80,96},{96,80},{112,128},{128,112... | collective-permute-start | bytes 294920 | tf_op jit(solution)/shard_map/ppermute | solution.py:36
  14.2 10.0 %collective-permute-start.3 = (bf16[32,8,384]{2,1,0:T(8,128)(2,1)S(1)}, bf16[32,8,384]{2,1,0:T(8,128)(2,1)S(1)}, u32[]{:S(2)}, u32[]{:S(2)}) collective-permute-start(bf16[32,8,384]{2,1,0:T(8,128)(2,1)S(1)} %get-tuple-element.25), channel_id=1, source_target_pairs={{1,2},{2,1},{3,4},{4,3},{5,6},{6,5},{7,8},{8,7},{9,10},{10,9},{11,... | collective-permute-start | bytes 589832 | tf_op jit(solution)/shard_map/ppermute | solution.py:36
  16.8 7.4 %collective-permute-start.2 = (bf16[32,8,384]{2,1,0:T(8,128)(2,1)S(1)}, bf16[32,8,384]{2,1,0:T(8,128)(2,1)S(1)}, u32[]{:S(2)}, u32[]{:S(2)}) collective-permute-start(bf16[32,8,384]{2,1,0:T(8,128)(2,1)S(1)} %get-tuple-element.26), channel_id=1, source_target_pairs={{0,1},{1,0},{2,3},{3,2},{4,5},{5,4},{6,7},{7,6},{8,9},{9,8},{10,11... | collective-permute-start | bytes 589832 | tf_op jit(solution)/shard_map/ppermute | solution.py:36
  18.9 16.8 %copy-start.6 = (s32[4]{0:T(128)}, s32[4]{0:T(128)S(1)}, u32[]{:S(2)}) copy-start(s32[4]{0:T(128)S(1)} %pad_add_fusion.place) | copy-start | bytes 52
  34.0 0.9 copy-start
  34.9 0.7 copy-start.7
  35.7 2.1 %collective-permute-start.8 = (bf16[768,384]{1,0:T(8,128)(2,1)S(1)}, bf16[768,384]{1,0:T(8,128)(2,1)S(1)}, u32[]{:S(2)}, u32[]{:S(2)}) collective-permute-start(bf16[768,384]{1,0:T(8,128)(2,1)S(1)} %constant_dynamic-slice_fusion), channel_id=1, source_target_pairs={{0,1},{1,0},{2,3},{3,2},{4,5},{5,4},{6,7},{7,6},{8,9},{9,8},{10,11... | collective-permute-start | bytes 1769480 | tf_op jit(solution)/shard_map/core_sum/ppermute | solution.py:36
  71.8 14.2 %copy-start.8 = (bf16[4,64,384]{2,1,0:T(8,128)(2,1)S(1)}, bf16[4,64,384]{2,1,0:T(8,128)(2,1)}, u32[]{:S(2)}) copy-start(bf16[4,64,384]{2,1,0:T(8,128)(2,1)} %copy-done.7) | copy-start | bytes 589828
  86.0 26.4 %collective-permute-start.9 = (bf16[768,384]{1,0:T(8,128)(2,1)S(1)}, bf16[768,384]{1,0:T(8,128)(2,1)S(1)}, u32[]{:S(2)}, u32[]{:S(2)}) collective-permute-start(bf16[768,384]{1,0:T(8,128)(2,1)S(1)} %bitcast.7), channel_id=1, source_target_pairs={{0,1},{1,0},{2,3},{3,2},{4,5},{5,4},{6,7},{7,6},{8,9},{9,8},{10,11... | collective-permute-start | bytes 1769480 | tf_op jit(solution)/shard_map/core_gather/ppermute | solution.py:36
  86.0 4.5 %collective-permute-start.4 = (bf16[4,64,384]{2,1,0:T(8,128)(2,1)S(1)}, bf16[4,64,384]{2,1,0:T(8,128)(2,1)S(1)}, u32[]{:S(2)}, u32[]{:S(2)}) collective-permute-start(bf16[4,64,384]{2,1,0:T(8,128)(2,1)S(1)} %copy-done.8), channel_id=1, source_target_pairs={{0,1},{1,0},{2,3},{3,2},{4,5},{5,4},{6,7},{7,6},{8,9},{9,8},{10,11... | collective-permute-start | bytes 589832 | tf_op jit(solution)/shard_map/ppermute | solution.py:36
  86.5 11.3 %collective-permute-start.5 = (bf16[4,64,384]{2,1,0:T(8,128)(2,1)S(1)}, bf16[4,64,384]{2,1,0:T(8,128)(2,1)S(1)}, u32[]{:S(2)}, u32[]{:S(2)}) collective-permute-start(bf16[4,64,384]{2,1,0:T(8,128)(2,1)S(1)} %get-tuple-element.14), channel_id=1, source_target_pairs={{1,2},{2,1},{3,4},{4,3},{5,6},{6,5},{7,8},{8,7},{9,10},{10,9},{11,... | collective-permute-start | bytes 589832 | tf_op jit(solution)/shard_map/ppermute | solution.py:36
  90.5 7.3 %copy-start.9 = (bf16[4,64,384]{2,1,0:T(8,128)(2,1)}, bf16[4,64,384]{2,1,0:T(8,128)(2,1)S(1)}, u32[]{:S(2)}) copy-start(bf16[4,64,384]{2,1,0:T(8,128)(2,1)S(1)} %collective-permute-done.4.from_0) | copy-start | bytes 589828
  97.8 0.7 copy-start.10
  100.6 4.8 %collective-permute-start.6 = (bf16[2,64,384]{2,1,0:T(8,128)(2,1)}, bf16[2,64,384]{2,1,0:T(8,128)(2,1)S(1)}, u32[]{:S(2)}, u32[]{:S(2)}) collective-permute-start(bf16[2,64,384]{2,1,0:T(8,128)(2,1)} %get-tuple-element.16), channel_id=1, source_target_pairs={{0,16},{16,0},{32,48},{48,32},{64,80},{80,64},{96,112},{112,96},{1... | collective-permute-start | bytes 294920 | tf_op jit(solution)/shard_map/ppermute | solution.py:36
  101.2 8.8 %collective-permute-start.7 = (bf16[2,64,384]{2,1,0:T(8,128)(2,1)}, bf16[2,64,384]{2,1,0:T(8,128)(2,1)S(1)}, u32[]{:S(2)}, u32[]{:S(2)}) collective-permute-start(bf16[2,64,384]{2,1,0:T(8,128)(2,1)} %get-tuple-element.17), channel_id=1, source_target_pairs={{16,32},{32,16},{48,64},{64,48},{80,96},{96,80},{112,128},{128,112... | collective-permute-start | bytes 294920 | tf_op jit(solution)/shard_map/ppermute | solution.py:36
  105.4 4.6 %copy-start.11 = (bf16[2,64,384]{2,1,0:T(8,128)(2,1)}, bf16[2,64,384]{2,1,0:T(8,128)(2,1)S(1)}, u32[]{:S(2)}) copy-start(bf16[2,64,384]{2,1,0:T(8,128)(2,1)S(1)} %collective-permute-done.6.from_0) | copy-start | bytes 294916
  110.0 0.6 copy-start.12

commit v2 on v1

v2 whole, which is shorter than its diff:
```python
import functools

import jax
import jax.numpy as jnp
from jax import lax
from jax.experimental import pallas as pl
from jax.experimental.pallas import tpu as pltpu
from jax.sharding import PartitionSpec as P

HEADS = 6
HEAD_DIM = 64
TILE = 8
AREA = TILE * TILE
BOTH = ("row", "col")
VMEM = pltpu.MemorySpace.VMEM
SMEM = pltpu.MemorySpace.SMEM
MASKED = -1e30
GROUPS = ((0, 4), (4, 2))


def dot(a, b, dims=((1,), (0,))):
    return lax.dot_general(a, b, (dims, ((), ())), preferred_element_type=jnp.float32)


NT = ((1,), (1,))
TN = ((0,), (0,))


def swap_pairs(size, kind):
    if kind == 0:
        return [(i, i ^ 1) for i in range(size)]
    return [(i, ((i + 1) ^ 1) - 1) for i in range(1, size - 1)]


def swap(block, axis, kind):
    return lax.ppermute(block, axis, swap_pairs(lax.axis_size(axis), kind))


def by_side(axis, first, second):
    odd = lax.rem(lax.axis_index(axis), 2) == 1
    return jnp.where(odd, first, second), jnp.where(odd, second, first)


def swap_edges(axis, low, high):
    first, second = by_side(axis, low, high)
    return swap(first, axis, 0), swap(second, axis, 1)


def collect_halo(tokens):
    cols = swap_edges("col", tokens[:, :TILE], tokens[:, TILE:])
    rows = swap_edges("row", tokens[:TILE], tokens[TILE:])
    west, east = by_side("col", *cols)
    sides = jnp.concatenate([west, east], axis=1)
    corners = swap_edges("row", sides[:TILE], sides[TILE:])
    return cols + rows + corners


WHOLE = pl.BlockSpec(memory_space=VMEM)
SCALARS = pl.BlockSpec(memory_space=SMEM)
FEATURE = HEADS * HEAD_DIM
OWN = 4 * AREA
ALL = 16 * AREA


def local_call(kernel, outs, scratch, mib, cost, name):
    def call(place, *operands):
        return pl.pallas_call(
            kernel,
            out_shape=tuple(jax.ShapeDtypeStruct(*out) for out in outs),
            in_specs=[SCALARS] + [WHOLE] * len(operands),
            out_specs=(WHOLE,) * len(outs),
            scratch_shapes=[pltpu.VMEM(*each) for each in scratch],
            compiler_params=pltpu.CompilerParams(vmem_limit_bytes=mib * 2**20),
            cost_estimate=pl.CostEstimate(
                flops=cost * 10**9, bytes_accessed=cost * 10**6, transcendentals=0
            ),
            name=name,
        )(place, *operands)

    return call


HALF, FULL = jnp.bfloat16, jnp.float32
SCORE_SCALE = HEAD_DIM**-0.5


def tile_of(block, row, col):
    part = block[row * TILE : (row + 1) * TILE, col * TILE : (col + 1) * TILE, :]
    return part.reshape(AREA, part.shape[-1]).astype(HALF)


def own_kernel(place, tokens, grad_out, w_query, w_key, w_value, w_out, tiles, flat_grad, query, grad_att, key, value):
    del place
    middle, outer = tokens[...].astype(FULL), grad_out[...].astype(FULL)
    for i in range(2):
        for j in range(2):
            at = (i * 2 + j) * AREA
            tiles[at : at + AREA, :] = tile_of(middle, i, j)
            flat_grad[at : at + AREA, :] = tile_of(outer, i, j)
    query[...] = (dot(tiles[...], w_query[...]).astype(HALF).astype(FULL) * SCORE_SCALE).astype(HALF)
    grad_att[...] = dot(flat_grad[...], w_out[...], NT).astype(HALF)
    key[...] = dot(tiles[...], w_key[...]).astype(HALF)
    value[...] = dot(tiles[...], w_value[...]).astype(HALF)


own_projections = local_call(own_kernel, [((OWN, FEATURE), HALF)] * 6, [], 8, 1, "own_projections")


def attention_kernel(
    place, tiles, query, grad_att, own_key, own_value, col_0, col_1, row_0, row_1, corner_0, corner_1,
    w_key, w_value,
    padded, key_grad, value_grad, attended, grad_q, send_0, send_1,
    key, value, key_total, value_total, halo,
):
    row_at, row_last, col_at, col_last = place[0], place[1], place[2], place[3]
    row_even, col_even = lax.rem(row_at, 2) == 0, lax.rem(col_at, 2) == 0

    def sides(even, first, second):
        a, b = first[...].astype(FULL), second[...].astype(FULL)
        return jnp.where(even, b, a), jnp.where(even, a, b)

    west, east = sides(col_even, col_0, col_1)
    north, south = sides(row_even, row_0, row_1)
    above, below = sides(row_even, corner_0, corner_1)
    outside = {
        (0, 0): (above, 0, 0), (0, 1): (north, 0, 0), (0, 2): (north, 0, 1), (0, 3): (above, 0, 1),
        (1, 0): (west, 0, 0), (1, 3): (east, 0, 0), (2, 0): (west, 1, 0), (2, 3): (east, 1, 0),
        (3, 0): (below, 0, 0), (3, 1): (south, 0, 0), (3, 2): (south, 0, 1), (3, 3): (below, 0, 1),
    }
    for n, (i, j) in enumerate(outside):
        tile = tile_of(*outside[i, j])
        padded[(i * 4 + j) * AREA : (i * 4 + j + 1) * AREA, :] = tile
        halo[n * AREA : (n + 1) * AREA, :] = tile
    for i in (1, 2):
        at, mine = (i * 4 + 1) * AREA, slice((i - 1) * 2 * AREA, i * 2 * AREA)
        padded[at : at + 2 * AREA, :] = tiles[mine, :]
        key[at : at + 2 * AREA, :] = own_key[mine, :]
        value[at : at + 2 * AREA, :] = own_value[mine, :]
    for weight, target in ((w_key, key), (w_value, value)):
        projected = dot(halo[...], weight[...]).astype(HALF)
        for n, (i, j) in enumerate(outside):
            target[(i * 4 + j) * AREA : (i * 4 + j + 1) * AREA, :] = projected[n * AREA : (n + 1) * AREA]
    key_total[...] = jnp.zeros_like(key_total)
    value_total[...] = jnp.zeros_like(value_total)

    zero, masked = jnp.float32(0.0), jnp.float32(MASKED)
    row_bias = [
        jnp.where(row_at == 0, masked, zero), None, None, jnp.where(row_at == row_last, masked, zero)
    ]
    col_bias = [
        jnp.where(col_at == 0, masked, zero), None, None, jnp.where(col_at == col_last, masked, zero)
    ]

    def bias_of(i, j):
        if row_bias[i] is None:
            return col_bias[j]
        if col_bias[j] is None:
            return row_bias[i]
        return jnp.minimum(row_bias[i], col_bias[j])

    for i in range(2):
        for j in range(2):
            mine = slice((i * 2 + j) * AREA, (i * 2 + j + 1) * AREA)
            rows = [((i + a) * 4 + j) * AREA for a in range(3)]
            for first, count in GROUPS:
                wide = count * HEAD_DIM
                cols = slice(first * HEAD_DIM, first * HEAD_DIM + wide)
                here = lax.broadcasted_iota(jnp.int32, (wide, wide), 0) // HEAD_DIM
                there = lax.broadcasted_iota(jnp.int32, (wide, wide), 1) // HEAD_DIM
                same = here == there

                def spread_heads(x):
                    full = jnp.concatenate([x.astype(jnp.float32)] * count, axis=0)
                    return jnp.where(same, full, 0.0).astype(jnp.bfloat16)

                def gather_heads(x):
                    kept = jnp.where(same, x, 0.0)
                    total = kept[:AREA]
                    for h in range(1, count):
                        total = total + kept[h * AREA : (h + 1) * AREA]
                    return total

                query_heads = spread_heads(query[mine, cols])
                grad_heads = spread_heads(grad_att[mine, cols])
                key_win = jnp.concatenate([key[r : r + 3 * AREA, cols] for r in rows], axis=0)
                value_win = jnp.concatenate([value[r : r + 3 * AREA, cols] for r in rows], axis=0)
                scores = dot(key_win, query_heads, NT)
                slabs = []
                for a in range(3):
                    for b in range(3):
                        slab = scores[(a * 3 + b) * AREA : (a * 3 + b + 1) * AREA]
                        bias = bias_of(i + a, j + b)
                        slabs.append(slab if bias is None else slab + bias)
                scores = jnp.concatenate(slabs, axis=0)
                top = jnp.max(scores, axis=0, keepdims=True)
                terms = jnp.exp(scores - top)
                weight = terms * (1.0 / jnp.sum(terms, axis=0, keepdims=True))
                weight_half = weight.astype(jnp.bfloat16)
                grad_weight = dot(value_win, grad_heads, NT)
                row_dot = jnp.sum(weight * grad_weight, axis=0, keepdims=True)
                grad_score = (weight * (grad_weight - row_dot)).astype(jnp.bfloat16)
                value_part = dot(weight_half, grad_heads)
                key_part = dot(grad_score, query_heads)
                for a in range(3):
                    span, part = slice(rows[a], rows[a] + 3 * AREA), slice(a * 192, a * 192 + 192)
                    value_total[span, cols] += value_part[part]
                    key_total[span, cols] += key_part[part]
                attended[mine, cols] = gather_heads(dot(weight_half, value_win, TN)).astype(
                    jnp.bfloat16
                )
                grad_q[mine, cols] = (
                    gather_heads(dot(grad_score, key_win, TN)) * SCORE_SCALE
                ).astype(jnp.bfloat16)

    key_grad[...] = key_total[...].astype(HALF)
    value_grad[...] = value_total[...].astype(HALF)
    rim = [(i * 4 + j) * AREA for i in range(4) for j in (0, 3)]
    key_rim = jnp.concatenate([key_grad[at : at + AREA, :] for at in rim], axis=0)
    value_rim = jnp.concatenate([value_grad[at : at + AREA, :] for at in rim], axis=0)
    spread = dot(key_rim, w_key[...], NT) + dot(value_rim, w_value[...], NT)
    for i in range(4):
        at = i * 2 * AREA
        west, east = spread[at : at + AREA], spread[at + AREA : at + 2 * AREA]
        send_0[i, :, :] = jnp.where(col_even, east, west).astype(HALF)
        send_1[i, :, :] = jnp.where(col_even, west, east).astype(HALF)


attention = local_call(
    attention_kernel,
    [((ALL, FEATURE), HALF)] * 3
    + [((OWN, FEATURE), HALF)] * 2
    + [((4, AREA, FEATURE), HALF)] * 2,
    [((ALL, FEATURE), HALF)] * 2 + [((ALL, FEATURE), FULL)] * 2 + [((12 * AREA, FEATURE), HALF)],
    24,
    6,
    "attention",
)


def weights_kernel(
    place, padded, key_grad, value_grad, tiles, flat_grad, attended, grad_q, w_query, w_key, w_value,
    keep, give, own,
):
    even = lax.rem(place[2], 2) == 0
    tokens_all = padded[...]
    grad_output = dot(attended[...], flat_grad[...], TN)
    grad_value = dot(tokens_all, value_grad[...], TN)
    grad_query = dot(tiles[...], grad_q[...], TN)
    grad_key = dot(tokens_all, key_grad[...], TN)
    for n, (zero, one) in enumerate(((grad_output, grad_query), (grad_value, grad_key))):
        keep[n * FEATURE : (n + 1) * FEATURE, :] = jnp.where(even, zero, one).astype(HALF)
        give[n * FEATURE : (n + 1) * FEATURE, :] = jnp.where(even, one, zero).astype(HALF)
    middle = [(i * 4 + 1) * AREA for i in range(4)]
    key_mid = jnp.concatenate([key_grad[at : at + 2 * AREA, :] for at in middle], axis=0)
    value_mid = jnp.concatenate([value_grad[at : at + 2 * AREA, :] for at in middle], axis=0)
    spread = dot(key_mid, w_key[...], NT) + dot(value_mid, w_value[...], NT)
    query_part = dot(grad_q[...], w_query[...], NT)
    for i in range(4):
        centre = spread[i * 2 * AREA : (i + 1) * 2 * AREA]
        if i in (1, 2):
            centre = centre + query_part[(i - 1) * 2 * AREA : i * 2 * AREA]
        own[i, 0, :, :] = centre[:AREA]
        own[i, 1, :, :] = centre[AREA:]


weight_grads = local_call(
    weights_kernel,
    [((2 * FEATURE, FEATURE), HALF)] * 2 + [((4, 2, AREA, FEATURE), FULL)],
    [],
    16,
    2,
    "weight_grads",
)


def columns_kernel(place, own, from_0, from_1, summed, send_0, send_1):
    row_even, col_even = lax.rem(place[0], 2) == 0, lax.rem(place[2], 2) == 0
    west = jnp.where(col_even, from_1[...].astype(FULL), from_0[...].astype(FULL))
    east = jnp.where(col_even, from_0[...].astype(FULL), from_1[...].astype(FULL))
    for j, got in ((0, west), (1, east)):
        total = own[:, j, :, :] + got
        north, south = total[0], total[3]
        send_0[j, :, :] = jnp.where(row_even, south, north).astype(HALF)
        send_1[j, :, :] = jnp.where(row_even, north, south).astype(HALF)
        summed[0, j, :, :] = total[1]
        summed[1, j, :, :] = total[2]


add_columns = local_call(
    columns_kernel,
    [((2, 2, AREA, FEATURE), FULL)] + [((2, AREA, FEATURE), HALF)] * 2,
    [],
    6,
    1,
    "columns",
)


def rows_kernel(place, summed, from_0, from_1, out, whole):
    row_even = lax.rem(place[0], 2) == 0
    north = jnp.where(row_even, from_1[...].astype(FULL), from_0[...].astype(FULL))
    south = jnp.where(row_even, from_0[...].astype(FULL), from_1[...].astype(FULL))
    for i, got in ((0, north), (1, south)):
        for j in range(2):
            total = summed[i, j, :, :] + got[j]
            whole[i * TILE : (i + 1) * TILE, j * TILE : (j + 1) * TILE, :] = total.reshape(
                TILE, TILE, total.shape[-1]
            )
    out[...] = whole[...].astype(HALF)


EDGE = 2 * TILE
add_rows = local_call(
    rows_kernel, [((EDGE, EDGE, FEATURE), HALF)], [((EDGE, EDGE, FEATURE), FULL)], 6, 1, "rows"
)


def device_groups():
    planes = [
        [(a << 7) | (z << 4) | (b << 1) | c for a in range(2) for b in range(8)]
        for z in range(8)
        for c in range(2)
    ]
    lines = [[(a << 7) | (z << 4) | b for z in range(8)] for a in range(2) for b in range(16)]
    return planes, lines


def exchange(pieces, groups):
    return lax.all_to_all(pieces, BOTH, 0, 0, tiled=True, axis_index_groups=groups)


def add_pieces(pieces, copies):
    total = pieces[0].astype(FULL)
    for n in range(1, pieces.shape[0]):
        total = total + pieces[n].astype(FULL)
    total = lax.optimization_barrier(total.astype(HALF))
    return jnp.broadcast_to(total, (copies,) + total.shape)


def sum_over_devices(part):
    planes, lines = device_groups()
    with jax.named_scope("plane_sum"):
        part = exchange(part.reshape(16, -1, FEATURE), planes)
        part = add_pieces(part, 8)
    with jax.named_scope("line_sum"):
        part = exchange(part, lines)
        part = add_pieces(part, 16)
    with jax.named_scope("plane_gather"):
        return exchange(part, planes).reshape(-1, FEATURE)


def per_device(tokens, grad_out, w_query, w_key, w_value, w_out):
    place = jnp.stack(
        [
            lax.axis_index("row"),
            lax.axis_size("row") - 1,
            lax.axis_index("col"),
            lax.axis_size("col") - 1,
        ]
    ).astype(jnp.int32)
    core = lax.rem(lax.axis_index("col"), 2)
    tied = lax.optimization_barrier
    with jax.named_scope("halo"):
        halo = collect_halo(tokens)
    tiles, flat_grad, query, grad_att, key, value = own_projections(
        place, tokens, grad_out, w_query, w_key, w_value, w_out
    )
    padded, key_grad, value_grad, attended, grad_q, send_0, send_1 = attention(
        place, tiles, query, grad_att, key, value, *halo, w_key, w_value
    )
    with jax.named_scope("columns_out"):
        from_0, from_1 = swap(send_0, "col", 0), swap(send_1, "col", 1)
    keep, give, own = weight_grads(
        place, padded, key_grad, value_grad, tiles, flat_grad, attended, grad_q,
        w_query, w_key, w_value,
    )
    give, from_0, from_1 = tied((give, from_0, from_1))
    with jax.named_scope("core_sum"):
        part = keep.astype(FULL) + swap(give, "col", 0).astype(FULL)
    summed, send_0, send_1 = add_columns(place, own, from_0, from_1)
    part, send_0, send_1 = tied((part.astype(HALF), send_0, send_1))
    part = sum_over_devices(part)
    with jax.named_scope("rows_out"):
        from_0, from_1 = swap(send_0, "row", 0), swap(send_1, "row", 1)
    with jax.named_scope("core_gather"):
        other = swap(part, "col", 0)
        first = jnp.where(core == 0, part, other).astype(FULL)
        second = jnp.where(core == 0, other, part).astype(FULL)
    sums = (first[:FEATURE], first[FEATURE:], second[:FEATURE], second[FEATURE:])
    sums, from_0, from_1 = tied((sums, from_0, from_1))
    grad_output, grad_value, grad_query, grad_key = sums
    (grad_tokens,) = add_rows(place, summed, from_0, from_1)
    return grad_tokens, grad_query, grad_key, grad_value, grad_output


def solution(mesh):
    in_specs = (P("row", "col", None), P("row", "col", None), P(), P(), P(), P())
    out_specs = (P("row", "col", None), P(), P(), P(), P())
    return jax.shard_map(
        per_device, mesh=mesh, in_specs=in_specs, out_specs=out_specs, check_vma=False
    )
```

time: 114 us -> 103 us (0.904); the launches traced: 114 us -> 101 us
  waiting for transfers between devices: 21.8 us -> 13.2 us
  blocking collectives: 47.8 us -> 44.6 us
  local copies, waits for them, and re-layouts: 4.48 us -> 1.55 us
  starting transfers between devices: 22.7 us -> 25 us
    ppermute x10 -> x12, waiting for transfers between devices: 21.8 us -> 13.2 us  [swap(): return lax.ppermute(block, axis, swap_pairs(lax.axis_size(axis), kind))]
    all_to_all x3, blocking collectives: 47.8 us -> 44.6 us  [exchange(): lax.all_to_all(pieces, BOTH, 0, 0, tiled=True, axis_index_groups=groups)]
    unnamed x26 -> x12, local copies, waits for them, and re-layouts: 2.9 us -> 0.03 us
    ppermute x10 -> x12, starting transfers between devices: 22.7 us -> 25 us  [swap(): return lax.ppermute(block, axis, swap_pairs(lax.axis_size(axis), kind))]
    pallas_call x3 -> x5, Pallas kernels: 13.7 us -> 13.2 us  [call(): pl.pallas_call(kernel, out_shape=tuple((jax.ShapeDtypeStruct(*out) for ou...]
  transfers between devices with their start and end apart: 10 -> 12, of which waited for: 5 -> 4; matrix products, arithmetic and copies ran while one was open for 0% -> 3% of each run, Pallas kernels for 3% -> 4%
where the time goes in v2:
time: 103 us; the launch traced here: 101 us
  blocking collectives  44.6 us (43%)
  starting transfers between devices  25 us (24%)
  waiting for transfers between devices  13.2 us (13%)
  Pallas kernels  13.2 us (13%)
  other arithmetic  2.71 us (3%)
  local copies, waits for them, and re-layouts  1.55 us (2%)
    all_to_all x3, blocking collectives, exchange(): lax.all_to_all(pieces, BOTH, 0, 0, tiled=True, axis_index_groups=groups)  44.6 us
    ppermute x12, starting transfers between devices, swap(): return lax.ppermute(block, axis, swap_pairs(lax.axis_size(axis), kind))  25 us
    pallas_call x5, Pallas kernels, call(): pl.pallas_call(kernel, out_shape=tuple((jax.ShapeDtypeStruct(*out) for ou...  13.2 us
    ppermute x12, waiting for transfers between devices, swap(): return lax.ppermute(block, axis, swap_pairs(lax.axis_size(axis), kind))  13.2 us
    select_n x4, other arithmetic, by_side(): return (jnp.where(odd, first, second), jnp.where(odd, second, first))  2.11 us
  transfers between devices with their start and end apart: 12, of which 4 were waited for; matrix products, arithmetic and copies ran while one was open for 3% of the time, Pallas kernels for 4%

profile of v2, /device:TPU:10, one launch (start us, length us, event | category | flops | bytes accessed | tf_op | source)
XLA Modules:
  0.0 101.2 jit_solution(16719279336743789095)
XLA Ops:
  0.7 1.1 %broadcast_select_fusion.6 = (bf16[16,8,384]{2,1,0:T(8,128)(2,1)S(1)}, bf16[16,8,384]{2,1,0:T(8,128)(2,1)S(1)}) fusion(pred[]{:T(512)S(6)} %eq.12, bf16[16,16,384]{2,1,0:T(8,128)(2,1)} %tokens.1), kind=kLoop, calls=%fused_computation.13 | loop fusion | flops 98304 | bytes 393217 | tf_op jit(solution)/shard_map/halo/jit(_where)/select_n | solution.py:41
  1.8 3.4 %collective-permute-start.1 = (bf16[16,8,384]{2,1,0:T(8,128)(2,1)S(1)}, bf16[16,8,384]{2,1,0:T(8,128)(2,1)S(1)}, u32[]{:S(2)}, u32[]{:S(2)}) collective-permute-start(bf16[16,8,384]{2,1,0:T(8,128)(2,1)S(1)} %get-tuple-element.79), channel_id=1, source_target_pairs={{1,2},{2,1},{3,4},{4,3},{5,6},{6,5},{7,8},{8,7},{9,10},{10,9},{11,... | collective-permute-start | bytes 294920 | tf_op jit(solution)/shard_map/halo/ppermute | solution.py:36
  5.1 0.9 collective-permute-start
  6.0 1.0 broadcast_select_fusion.2
  7.0 8.6 %collective-permute-start.3 = (bf16[8,16,384]{2,1,0:T(8,128)(2,1)S(1)}, bf16[8,16,384]{2,1,0:T(8,128)(2,1)S(1)}, u32[]{:S(2)}, u32[]{:S(2)}) collective-permute-start(bf16[8,16,384]{2,1,0:T(8,128)(2,1)S(1)} %get-tuple-element.77), channel_id=1, source_target_pairs={{16,32},{32,16},{48,64},{64,48},{80,96},{96,80},{112,128},{128,112... | collective-permute-start | bytes 294920 | tf_op jit(solution)/shard_map/halo/ppermute | solution.py:36
  15.8 3.9 %collective-permute-start.5 = (bf16[8,16,384]{2,1,0:T(8,128)(2,1)S(1)}, bf16[8,16,384]{2,1,0:T(8,128)(2,1)S(1)}, u32[]{:S(2)}, u32[]{:S(2)}) collective-permute-start(bf16[8,16,384]{2,1,0:T(8,128)(2,1)S(1)} %get-tuple-element.73), channel_id=1, source_target_pairs={{16,32},{32,16},{48,64},{64,48},{80,96},{96,80},{112,128},{128,112... | collective-permute-start | bytes 294920 | tf_op jit(solution)/shard_map/halo/ppermute | solution.py:36
  19.7 0.2 collective-permute-start.4
  20.1 1.2 %own_projections.1 = (bf16[256,384]{1,0:T(8,128)(2,1)S(1)}, bf16[256,384]{1,0:T(8,128)(2,1)S(1)}, bf16[256,384]{1,0:T(8,128)(2,1)S(1)}, bf16[256,384]{1,0:T(8,12...) custom-call(s32[4]{0:T(128)S(1)} %pad_add_fusion.place, bf16[16,16,384]{2,1,0:T(8,128)(2,1)S(1)} %copy-done, ...), custom_call_target="tpu_custom_call" | custom-call | flops 1000000000 | bytes 1000000 | tf_op jit(solution)/shard_map/own_projections/pallas_call | solution.py:67
  21.3 3.2 %collective-permute-done.5.corner_1 = bf16[8,16,384]{2,1,0:T(8,128)(2,1)S(1)} collective-permute-done((bf16[8,16,384]{2,1,0:T(8,128)(2,1)S(1)}, bf16[8,16,384]{2,1,0:T(8,128)(2,1)S(1)}, u32[]{:S(2)}, u32[]{:S(2)}) %collective-permute-start.5) | collective-permute-done | bytes 98336 | tf_op jit(solution)/shard_map/halo/ppermute | solution.py:36
  24.5 7.7 %attention.1 = (bf16[1024,384]{1,0:T(8,128)(2,1)S(1)}, bf16[1024,384]{1,0:T(8,128)(2,1)S(1)}, bf16[1024,384]{1,0:T(8,128)(2,1)S(1)}, bf16[256,384]{1,0:T(8,128)(...) custom-call(s32[4]{0:T(128)S(1)} %pad_add_fusion.place, ...), custom_call_target="tpu_custom_call" | custom-call | flops 6000000000 | bytes 6000000 | tf_op jit(solution)/shard_map/attention/pallas_call | solution.py:67
  32.3 3.1 %collective-permute-start.7 = (bf16[4,64,384]{2,1,0:T(8,128)(2,1)S(1)}, bf16[4,64,384]{2,1,0:T(8,128)(2,1)S(1)}, u32[]{:S(2)}, u32[]{:S(2)}) collective-permute-start(bf16[4,64,384]{2,1,0:T(8,128)(2,1)S(1)} %get-tuple-element.50), channel_id=1, source_target_pairs={{1,2},{2,1},{3,4},{4,3},{5,6},{6,5},{7,8},{8,7},{9,10},{10,9},{11,... | collective-permute-start | bytes 589832 | tf_op jit(solution)/shard_map/columns_out/ppermute | solution.py:36
  35.3 2.4 %weight_grads.1 = (bf16[768,384]{1,0:T(8,128)(2,1)S(1)}, bf16[768,384]{1,0:T(8,128)(2,1)S(1)}, f32[4,2,64,384]{3,2,1,0:T(8,128)S(1)}) custom-call(s32[4]{0:T(128)S(1)} %pad_add_fusion.place, bf16[1024,384]{1,0:T(8,128)(2,1)S(1)} %get-tuple-element.41.padded, bf16[1024,384]{1,0:T(8,128)(2,1)S(1)} %get-tuple-element.42.key_grad, ...), custom_call_target="tpu_custom_call" | custom-call | flops 2000000000 | bytes 2000000 | tf_op jit(solution)/shard_map/weight_grads/pallas_call | solution.py:67
  37.7 5.7 %collective-permute-done.7.from_1 = bf16[4,64,384]{2,1,0:T(8,128)(2,1)S(1)} collective-permute-done((bf16[4,64,384]{2,1,0:T(8,128)(2,1)S(1)}, bf16[4,64,384]{2,1,0:T(8,128)(2,1)S(1)}, u32[]{:S(2)}, u32[]{:S(2)}) %collective-permute-start.7) | collective-permute-done | bytes 196640 | tf_op jit(solution)/shard_map/columns_out/ppermute | solution.py:36
  43.4 0.7 columns.1
  44.1 1.3 %collective-permute-done.8 = bf16[768,384]{1,0:T(8,128)(2,1)S(1)} collective-permute-done((bf16[768,384]{1,0:T(8,128)(2,1)S(1)}, bf16[768,384]{1,0:T(8,128)(2,1)S(1)}, u32[]{:S(2)}, u32[]{:S(2)}) %collective-permute-start.8) | collective-permute-done | bytes 589856 | tf_op jit(solution)/shard_map/core_sum/ppermute | solution.py:36
  45.6 16.1 %all_to_all.15 = bf16[16,48,384]{2,1,0:T(8,128)(2,1)S(1)} all-to-all(bf16[16,48,384]{2,1,0:T(8,128)(2,1)S(1)} %bitcast.15), channel_id=1, replica_groups={{0,2,4,6,8,10,12,14,128,130,132,134,136,138,140,142},{1,3,5,7,9,11,13,1..., dimensions={0} | all-to-all | bytes 1179648 | tf_op jit(solution)/shard_map/plane_sum/all_to_all | solution.py:329
  61.8 14.5 %all_to_all.16 = bf16[8,48,384]{2,1,0:T(8,128)(2,1)S(1)} all-to-all(bf16[8,48,384]{2,1,0:T(8,128)(2,1)S(1)} %broadcast_in_dim.6), channel_id=1, replica_groups={{0,16,32,48,64,80,96,112},{1,17,33,49,65,81,97,113},{2,18,34,50,66,82,9..., dimensions={0} | all-to-all | bytes 589824 | tf_op jit(solution)/shard_map/line_sum/all_to_all | solution.py:329
  76.4 14.0 %all_to_all.17 = bf16[16,48,384]{2,1,0:T(8,128)(2,1)S(1)} all-to-all(bf16[16,48,384]{2,1,0:T(8,128)(2,1)S(1)} %broadcast_in_dim.7), channel_id=1, replica_groups={{0,2,4,6,8,10,12,14,128,130,132,134,136,138,140,142},{1,3,5,7,9,11,13,1..., dimensions={0} | all-to-all | bytes 1179648 | tf_op jit(solution)/shard_map/plane_gather/all_to_all | solution.py:329
  90.4 0.6 collective-permute-start.10
  91.0 4.2 %collective-permute-start.11 = (bf16[2,64,384]{2,1,0:T(8,128)(2,1)S(1)}, bf16[2,64,384]{2,1,0:T(8,128)(2,1)S(1)}, u32[]{:S(2)}, u32[]{:S(2)}) collective-permute-start(bf16[2,64,384]{2,1,0:T(8,128)(2,1)S(1)} %get-tuple-element.60), channel_id=1, source_target_pairs={{16,32},{32,16},{48,64},{64,48},{80,96},{96,80},{112,128},{128,112... | collective-permute-start | bytes 294920 | tf_op jit(solution)/shard_map/rows_out/ppermute | solution.py:36
  95.2 0.2 select_convert_fusion
  95.4 1.4 %fusion.3 = (f32[384,384]{1,0:T(8,128)}, f32[384,384]{1,0:T(8,128)}, f32[384,384]{1,0:T(8,128)}, f32[384,384]{1,0:T(8,128)}) fusion(f32[768,384]{1,0:T(8,128)S(1)} %get-tuple-element.69, f32[768,384]{1,0:T(8,128)S(1)} %get-tuple-element.70), kind=kLoop, calls=%fused_computation.21 | loop fusion | bytes 4718592 | tf_op jit(solution)/shard_map/slice | solution.py:389
  96.8 3.1 %collective-permute-done.11.from_1 = bf16[2,64,384]{2,1,0:T(8,128)(2,1)S(1)} collective-permute-done((bf16[2,64,384]{2,1,0:T(8,128)(2,1)S(1)}, bf16[2,64,384]{2,1,0:T(8,128)(2,1)S(1)}, u32[]{:S(2)}, u32[]{:S(2)}) %collective-permute-start.11) | collective-permute-done | bytes 98336 | tf_op jit(solution)/shard_map/rows_out/ppermute | solution.py:36
  99.9 1.3 %rows.1 = bf16[16,16,384]{2,1,0:T(8,128)(2,1)} custom-call(s32[4]{0:T(128)S(1)} %pad_add_fusion.place, f32[2,2,64,384]{3,2,1,0:T(8,128)S(1)} %get-tuple-element.53.summed, bf16[2,64,384]{2,1,0:T(8,128)(2,1)S(1)} %collective-permute-done.10.from_0, bf16[2,64,384]{2,1,0:T(8,128)(2,1)S(1)} %collective-permute-done.11.from_1), custom_call_target="tpu_custom_call" | custom-call | flops 1000000000 | bytes 1000000 | tf_op jit(solution)/shard_map/rows/pallas_call | solution.py:67
  (32 shorter events, 0.8 us)
Async XLA Ops:
  0.6 19.4 %copy-start = (bf16[16,16,384]{2,1,0:T(8,128)(2,1)S(1)}, bf16[16,16,384]{2,1,0:T(8,128)(2,1)}, u32[]{:S(2)}) copy-start(bf16[16,16,384]{2,1,0:T(8,128)(2,1)} %tokens.1) | copy-start | bytes 589828
  0.6 19.4 %copy-start.4 = (bf16[384,384]{1,0:T(8,128)(2,1)S(1)}, bf16[384,384]{1,0:T(8,128)(2,1)}, u32[]{:S(2)}) copy-start(bf16[384,384]{1,0:T(8,128)(2,1)} %w_value.5) | copy-start | bytes 884740
  0.7 19.4 %copy-start.3 = (bf16[384,384]{1,0:T(8,128)(2,1)S(1)}, bf16[384,384]{1,0:T(8,128)(2,1)}, u32[]{:S(2)}) copy-start(bf16[384,384]{1,0:T(8,128)(2,1)} %w_key.5) | copy-start | bytes 884740
  0.7 19.4 %copy-start.2 = (bf16[384,384]{1,0:T(8,128)(2,1)S(1)}, bf16[384,384]{1,0:T(8,128)(2,1)}, u32[]{:S(2)}) copy-start(bf16[384,384]{1,0:T(8,128)(2,1)} %w_query.3) | copy-start | bytes 884740
  0.7 19.4 %copy-start.1 = (bf16[384,384]{1,0:T(8,128)(2,1)S(1)}, bf16[384,384]{1,0:T(8,128)(2,1)}, u32[]{:S(2)}) copy-start(bf16[384,384]{1,0:T(8,128)(2,1)} %w_out.1) | copy-start | bytes 884740
  0.7 19.4 %copy-start.5 = (bf16[16,16,384]{2,1,0:T(8,128)(2,1)S(1)}, bf16[16,16,384]{2,1,0:T(8,128)(2,1)}, u32[]{:S(2)}) copy-start(bf16[16,16,384]{2,1,0:T(8,128)(2,1)} %grad_out.1) | copy-start | bytes 589828
  1.8 14.0 %collective-permute-start.1 = (bf16[16,8,384]{2,1,0:T(8,128)(2,1)S(1)}, bf16[16,8,384]{2,1,0:T(8,128)(2,1)S(1)}, u32[]{:S(2)}, u32[]{:S(2)}) collective-permute-start(bf16[16,8,384]{2,1,0:T(8,128)(2,1)S(1)} %get-tuple-element.79), channel_id=1, source_target_pairs={{1,2},{2,1},{3,4},{4,3},{5,6},{6,5},{7,8},{8,7},{9,10},{10,9},{11,... | collective-permute-start | bytes 294920 | tf_op jit(solution)/shard_map/halo/ppermute | solution.py:36
  5.1 10.6 %collective-permute-start = (bf16[16,8,384]{2,1,0:T(8,128)(2,1)S(1)}, bf16[16,8,384]{2,1,0:T(8,128)(2,1)S(1)}, u32[]{:S(2)}, u32[]{:S(2)}) collective-permute-start(bf16[16,8,384]{2,1,0:T(8,128)(2,1)S(1)} %get-tuple-element.80), channel_id=1, source_target_pairs={{0,1},{1,0},{2,3},{3,2},{4,5},{5,4},{6,7},{7,6},{8,9},{9,8},{10,11... | collective-permute-start | bytes 294920 | tf_op jit(solution)/shard_map/halo/ppermute | solution.py:36
  7.0 14.3 %collective-permute-start.3 = (bf16[8,16,384]{2,1,0:T(8,128)(2,1)S(1)}, bf16[8,16,384]{2,1,0:T(8,128)(2,1)S(1)}, u32[]{:S(2)}, u32[]{:S(2)}) collective-permute-start(bf16[8,16,384]{2,1,0:T(8,128)(2,1)S(1)} %get-tuple-element.77), channel_id=1, source_target_pairs={{16,32},{32,16},{48,64},{64,48},{80,96},{96,80},{112,128},{128,112... | collective-permute-start | bytes 294920 | tf_op jit(solution)/shard_map/halo/ppermute | solution.py:36
  15.6 5.7 %collective-permute-start.2 = (bf16[8,16,384]{2,1,0:T(8,128)(2,1)S(1)}, bf16[8,16,384]{2,1,0:T(8,128)(2,1)S(1)}, u32[]{:S(2)}, u32[]{:S(2)}) collective-permute-start(bf16[8,16,384]{2,1,0:T(8,128)(2,1)S(1)} %get-tuple-element.78), channel_id=1, source_target_pairs={{0,16},{16,0},{32,48},{48,32},{64,80},{80,64},{96,112},{112,96},{1... | collective-permute-start | bytes 294920 | tf_op jit(solution)/shard_map/halo/ppermute | solution.py:36
  15.8 8.6 %collective-permute-start.5 = (bf16[8,16,384]{2,1,0:T(8,128)(2,1)S(1)}, bf16[8,16,384]{2,1,0:T(8,128)(2,1)S(1)}, u32[]{:S(2)}, u32[]{:S(2)}) collective-permute-start(bf16[8,16,384]{2,1,0:T(8,128)(2,1)S(1)} %get-tuple-element.73), channel_id=1, source_target_pairs={{16,32},{32,16},{48,64},{64,48},{80,96},{96,80},{112,128},{128,112... | collective-permute-start | bytes 294920 | tf_op jit(solution)/shard_map/halo/ppermute | solution.py:36
  19.7 4.7 %collective-permute-start.4 = (bf16[8,16,384]{2,1,0:T(8,128)(2,1)S(1)}, bf16[8,16,384]{2,1,0:T(8,128)(2,1)S(1)}, u32[]{:S(2)}, u32[]{:S(2)}) collective-permute-start(bf16[8,16,384]{2,1,0:T(8,128)(2,1)S(1)} %get-tuple-element.74), channel_id=1, source_target_pairs={{0,16},{16,0},{32,48},{48,32},{64,80},{80,64},{96,112},{112,96},{1... | collective-permute-start | bytes 294920 | tf_op jit(solution)/shard_map/halo/ppermute | solution.py:36
  32.2 5.6 %collective-permute-start.6 = (bf16[4,64,384]{2,1,0:T(8,128)(2,1)S(1)}, bf16[4,64,384]{2,1,0:T(8,128)(2,1)S(1)}, u32[]{:S(2)}, u32[]{:S(2)}) collective-permute-start(bf16[4,64,384]{2,1,0:T(8,128)(2,1)S(1)} %get-tuple-element.49), channel_id=1, source_target_pairs={{0,1},{1,0},{2,3},{3,2},{4,5},{5,4},{6,7},{7,6},{8,9},{9,8},{10,11... | collective-permute-start | bytes 589832 | tf_op jit(solution)/shard_map/columns_out/ppermute | solution.py:36
  32.3 11.1 %collective-permute-start.7 = (bf16[4,64,384]{2,1,0:T(8,128)(2,1)S(1)}, bf16[4,64,384]{2,1,0:T(8,128)(2,1)S(1)}, u32[]{:S(2)}, u32[]{:S(2)}) collective-permute-start(bf16[4,64,384]{2,1,0:T(8,128)(2,1)S(1)} %get-tuple-element.50), channel_id=1, source_target_pairs={{1,2},{2,1},{3,4},{4,3},{5,6},{6,5},{7,8},{8,7},{9,10},{10,9},{11,... | collective-permute-start | bytes 589832 | tf_op jit(solution)/shard_map/columns_out/ppermute | solution.py:36
  43.4 2.0 %collective-permute-start.8 = (bf16[768,384]{1,0:T(8,128)(2,1)S(1)}, bf16[768,384]{1,0:T(8,128)(2,1)S(1)}, u32[]{:S(2)}, u32[]{:S(2)}) collective-permute-start(bf16[768,384]{1,0:T(8,128)(2,1)S(1)} %get-tuple-element.55), channel_id=1, source_target_pairs={{0,1},{1,0},{2,3},{3,2},{4,5},{5,4},{6,7},{7,6},{8,9},{9,8},{10,11... | collective-permute-start | bytes 1769480 | tf_op jit(solution)/shard_map/core_sum/ppermute | solution.py:36
  90.4 4.7 %collective-permute-start.9 = (bf16[768,384]{1,0:T(8,128)(2,1)S(1)}, bf16[768,384]{1,0:T(8,128)(2,1)S(1)}, u32[]{:S(2)}, u32[]{:S(2)}) collective-permute-start(bf16[768,384]{1,0:T(8,128)(2,1)S(1)} %bitcast.16), channel_id=1, source_target_pairs={{0,1},{1,0},{2,3},{3,2},{4,5},{5,4},{6,7},{7,6},{8,9},{9,8},{10,11... | collective-permute-start | bytes 1769480 | tf_op jit(solution)/shard_map/core_gather/ppermute | solution.py:36
  90.4 6.4 %collective-permute-start.10 = (bf16[2,64,384]{2,1,0:T(8,128)(2,1)S(1)}, bf16[2,64,384]{2,1,0:T(8,128)(2,1)S(1)}, u32[]{:S(2)}, u32[]{:S(2)}) collective-permute-start(bf16[2,64,384]{2,1,0:T(8,128)(2,1)S(1)} %get-tuple-element.59), channel_id=1, source_target_pairs={{0,16},{16,0},{32,48},{48,32},{64,80},{80,64},{96,112},{112,96},{1... | collective-permute-start | bytes 294920 | tf_op jit(solution)/shard_map/rows_out/ppermute | solution.py:36
  91.0 8.9 %collective-permute-start.11 = (bf16[2,64,384]{2,1,0:T(8,128)(2,1)S(1)}, bf16[2,64,384]{2,1,0:T(8,128)(2,1)S(1)}, u32[]{:S(2)}, u32[]{:S(2)}) collective-permute-start(bf16[2,64,384]{2,1,0:T(8,128)(2,1)S(1)} %get-tuple-element.60), channel_id=1, source_target_pairs={{16,32},{32,16},{48,64},{64,48},{80,96},{96,80},{112,128},{128,112... | collective-permute-start | bytes 294920 | tf_op jit(solution)/shard_map/rows_out/ppermute | solution.py:36

commit v3 on v2

--- a/solution.py
+++ b/solution.py
@@ -214,22 +214,20 @@
 
     key_grad[...] = key_total[...].astype(HALF)
     value_grad[...] = value_total[...].astype(HALF)
-    rim = [(i * 4 + j) * AREA for i in range(4) for j in (0, 3)]
-    key_rim = jnp.concatenate([key_grad[at : at + AREA, :] for at in rim], axis=0)
-    value_rim = jnp.concatenate([value_grad[at : at + AREA, :] for at in rim], axis=0)
+    north, south = slice(0, 4 * AREA), slice(12 * AREA, ALL)
+    key_rim = jnp.concatenate([key_grad[north, :], key_grad[south, :]], axis=0)
+    value_rim = jnp.concatenate([value_grad[north, :], value_grad[south, :]], axis=0)
     spread = dot(key_rim, w_key[...], NT) + dot(value_rim, w_value[...], NT)
-    for i in range(4):
-        at = i * 2 * AREA
-        west, east = spread[at : at + AREA], spread[at + AREA : at + 2 * AREA]
-        send_0[i, :, :] = jnp.where(col_even, east, west).astype(HALF)
-        send_1[i, :, :] = jnp.where(col_even, west, east).astype(HALF)
+    above, below = spread[: 4 * AREA], spread[4 * AREA :]
+    send_0[...] = jnp.where(row_even, below, above).astype(HALF)
+    send_1[...] = jnp.where(row_even, above, below).astype(HALF)
 
 
 attention = local_call(
     attention_kernel,
     [((ALL, FEATURE), HALF)] * 3
     + [((OWN, FEATURE), HALF)] * 2
-    + [((4, AREA, FEATURE), HALF)] * 2,
+    + [((4 * AREA, FEATURE), HALF)] * 2,
     [((ALL, FEATURE), HALF)] * 2 + [((ALL, FEATURE), FULL)] * 2 + [((12 * AREA, FEATURE), HALF)],
     24,
     6,
@@ -250,22 +248,21 @@
     for n, (zero, one) in enumerate(((grad_output, grad_query), (grad_value, grad_key))):
         keep[n * FEATURE : (n + 1) * FEATURE, :] = jnp.where(even, zero, one).astype(HALF)
         give[n * FEATURE : (n + 1) * FEATURE, :] = jnp.where(even, one, zero).astype(HALF)
-    middle = [(i * 4 + 1) * AREA for i in range(4)]
-    key_mid = jnp.concatenate([key_grad[at : at + 2 * AREA, :] for at in middle], axis=0)
-    value_mid = jnp.concatenate([value_grad[at : at + 2 * AREA, :] for at in middle], axis=0)
-    spread = dot(key_mid, w_key[...], NT) + dot(value_mid, w_value[...], NT)
+    middle = slice(4 * AREA, 12 * AREA)
+    spread = dot(key_grad[middle, :], w_key[...], NT) + dot(value_grad[middle, :], w_value[...], NT)
     query_part = dot(grad_q[...], w_query[...], NT)
-    for i in range(4):
-        centre = spread[i * 2 * AREA : (i + 1) * 2 * AREA]
-        if i in (1, 2):
-            centre = centre + query_part[(i - 1) * 2 * AREA : i * 2 * AREA]
-        own[i, 0, :, :] = centre[:AREA]
-        own[i, 1, :, :] = centre[AREA:]
+    for i in range(2):
+        row, mine = i * 4 * AREA, i * 2 * AREA
+        own[row : row + AREA, :] = spread[row : row + AREA]
+        own[row + AREA : row + 3 * AREA, :] = (
+            spread[row + AREA : row + 3 * AREA] + query_part[mine : mine + 2 * AREA]
+        )
+        own[row + 3 * AREA : row + 4 * AREA, :] = spread[row + 3 * AREA : row + 4 * AREA]
 
 
 weight_grads = local_call(
     weights_kernel,
-    [((2 * FEATURE, FEATURE), HALF)] * 2 + [((4, 2, AREA, FEATURE), FULL)],
+    [((2 * FEATURE, FEATURE), HALF)] * 2 + [((8 * AREA, FEATURE), FULL)],
     [],
     16,
     2,
@@ -273,36 +270,37 @@
 )
 
 
-def columns_kernel(place, own, from_0, from_1, summed, send_0, send_1):
+def rows_kernel(place, own, from_0, from_1, summed, send_0, send_1):
     row_even, col_even = lax.rem(place[0], 2) == 0, lax.rem(place[2], 2) == 0
-    west = jnp.where(col_even, from_1[...].astype(FULL), from_0[...].astype(FULL))
-    east = jnp.where(col_even, from_0[...].astype(FULL), from_1[...].astype(FULL))
-    for j, got in ((0, west), (1, east)):
-        total = own[:, j, :, :] + got
-        north, south = total[0], total[3]
-        send_0[j, :, :] = jnp.where(row_even, south, north).astype(HALF)
-        send_1[j, :, :] = jnp.where(row_even, north, south).astype(HALF)
-        summed[0, j, :, :] = total[1]
-        summed[1, j, :, :] = total[2]
-
-
-add_columns = local_call(
-    columns_kernel,
-    [((2, 2, AREA, FEATURE), FULL)] + [((2, AREA, FEATURE), HALF)] * 2,
+    first, second = from_0[...].astype(FULL), from_1[...].astype(FULL)
+    got = (jnp.where(row_even, second, first), jnp.where(row_even, first, second))
+    for i in range(2):
+        total = own[i * 4 * AREA : (i + 1) * 4 * AREA, :] + got[i]
+        west, east = total[:AREA], total[3 * AREA :]
+        mine = slice(i * AREA, (i + 1) * AREA)
+        send_0[mine, :] = jnp.where(col_even, east, west).astype(HALF)
+        send_1[mine, :] = jnp.where(col_even, west, east).astype(HALF)
+        summed[i * 2 * AREA : (i + 1) * 2 * AREA, :] = total[AREA : 3 * AREA]
+
+
+add_rows = local_call(
+    rows_kernel,
+    [((OWN, FEATURE), FULL)] + [((2 * AREA, FEATURE), HALF)] * 2,
     [],
     6,
     1,
-    "columns",
+    "add_rows",
 )
 
 
-def rows_kernel(place, summed, from_0, from_1, out, whole):
-    row_even = lax.rem(place[0], 2) == 0
-    north = jnp.where(row_even, from_1[...].astype(FULL), from_0[...].astype(FULL))
-    south = jnp.where(row_even, from_0[...].astype(FULL), from_1[...].astype(FULL))
-    for i, got in ((0, north), (1, south)):
+def columns_kernel(place, summed, from_0, from_1, out, whole):
+    col_even = lax.rem(place[2], 2) == 0
+    first, second = from_0[...].astype(FULL), from_1[...].astype(FULL)
+    got = (jnp.where(col_even, second, first), jnp.where(col_even, first, second))
+    for i in range(2):
         for j in range(2):
-            total = summed[i, j, :, :] + got[j]
+            at = (i * 2 + j) * AREA
+            total = summed[at : at + AREA, :] + got[j][i * AREA : (i + 1) * AREA]
             whole[i * TILE : (i + 1) * TILE, j * TILE : (j + 1) * TILE, :] = total.reshape(
                 TILE, TILE, total.shape[-1]
             )
@@ -310,43 +308,40 @@
 
 
 EDGE = 2 * TILE
-add_rows = local_call(
-    rows_kernel, [((EDGE, EDGE, FEATURE), HALF)], [((EDGE, EDGE, FEATURE), FULL)], 6, 1, "rows"
+add_columns = local_call(
+    columns_kernel,
+    [((EDGE, EDGE, FEATURE), HALF)],
+    [((EDGE, EDGE, FEATURE), FULL)],
+    6,
+    1,
+    "add_columns",
 )
 
 
-def device_groups():
-    planes = [
+LINE_STEPS = (16, 32, 112)
+
+
+def plane_groups():
+    return [
         [(a << 7) | (z << 4) | (b << 1) | c for a in range(2) for b in range(8)]
         for z in range(8)
         for c in range(2)
     ]
-    lines = [[(a << 7) | (z << 4) | b for z in range(8)] for a in range(2) for b in range(16)]
-    return planes, lines
+
+
+def cross(block, step):
+    return lax.ppermute(block, BOTH, [(i, i ^ step) for i in range(lax.axis_size(BOTH))])
 
 
 def exchange(pieces, groups):
     return lax.all_to_all(pieces, BOTH, 0, 0, tiled=True, axis_index_groups=groups)
 
 
-def add_pieces(pieces, copies):
+def add_pieces(pieces):
     total = pieces[0].astype(FULL)
     for n in range(1, pieces.shape[0]):
         total = total + pieces[n].astype(FULL)
-    total = lax.optimization_barrier(total.astype(HALF))
-    return jnp.broadcast_to(total, (copies,) + total.shape)
-
-
-def sum_over_devices(part):
-    planes, lines = device_groups()
-    with jax.named_scope("plane_sum"):
-        part = exchange(part.reshape(16, -1, FEATURE), planes)
-        part = add_pieces(part, 8)
-    with jax.named_scope("line_sum"):
-        part = exchange(part, lines)
-        part = add_pieces(part, 16)
-    with jax.named_scope("plane_gather"):
-        return exchange(part, planes).reshape(-1, FEATURE)
+    return total.astype(HALF)
 
 
 def per_device(tokens, grad_out, w_query, w_key, w_value, w_out):
@@ -359,6 +354,7 @@
         ]
     ).astype(jnp.int32)
     core = lax.rem(lax.axis_index("col"), 2)
+    planes = plane_groups()
     tied = lax.optimization_barrier
     with jax.named_scope("halo"):
         halo = collect_halo(tokens)
@@ -368,28 +364,39 @@
     padded, key_grad, value_grad, attended, grad_q, send_0, send_1 = attention(
         place, tiles, query, grad_att, key, value, *halo, w_key, w_value
     )
-    with jax.named_scope("columns_out"):
-        from_0, from_1 = swap(send_0, "col", 0), swap(send_1, "col", 1)
+    with jax.named_scope("rows_out"):
+        from_0, from_1 = swap(send_0, "row", 0), swap(send_1, "row", 1)
     keep, give, own = weight_grads(
         place, padded, key_grad, value_grad, tiles, flat_grad, attended, grad_q,
         w_query, w_key, w_value,
     )
-    give, from_0, from_1 = tied((give, from_0, from_1))
     with jax.named_scope("core_sum"):
         part = keep.astype(FULL) + swap(give, "col", 0).astype(FULL)
-    summed, send_0, send_1 = add_columns(place, own, from_0, from_1)
-    part, send_0, send_1 = tied((part.astype(HALF), send_0, send_1))
-    part = sum_over_devices(part)
-    with jax.named_scope("rows_out"):
-        from_0, from_1 = swap(send_0, "row", 0), swap(send_1, "row", 1)
+    part = part.astype(HALF)
+    with jax.named_scope("plane_sum"):
+        part = exchange(part.reshape(16, -1, FEATURE), planes)
+        part, from_0, from_1 = tied((part, from_0, from_1))
+        part = add_pieces(part)
+    summed, send_0, send_1 = add_rows(place, own, from_0, from_1)
+    with jax.named_scope("line_sum"):
+        columns = []
+        for step, strip, kind in zip(LINE_STEPS, (send_0, send_1, None), (0, 1, None)):
+            other = cross(part, step)
+            if strip is not None:
+                other, strip = tied((other, swap(strip, "col", kind)))
+                columns.append(strip)
+            part = (part.astype(FULL) + other.astype(FULL)).astype(HALF)
+    (grad_tokens,) = add_columns(place, summed, *columns)
+    with jax.named_scope("plane_gather"):
+        part, grad_tokens = tied((part, grad_tokens))
+        part = jnp.broadcast_to(part, (16,) + part.shape)
+        part = exchange(part, planes).reshape(-1, FEATURE)
     with jax.named_scope("core_gather"):
         other = swap(part, "col", 0)
         first = jnp.where(core == 0, part, other).astype(FULL)
         second = jnp.where(core == 0, other, part).astype(FULL)
-    sums = (first[:FEATURE], first[FEATURE:], second[:FEATURE], second[FEATURE:])
-    sums, from_0, from_1 = tied((sums, from_0, from_1))
-    grad_output, grad_value, grad_query, grad_key = sums
-    (grad_tokens,) = add_rows(place, summed, from_0, from_1)
+    grad_output, grad_value = first[:FEATURE], first[FEATURE:]
+    grad_query, grad_key = second[:FEATURE], second[FEATURE:]
     return grad_tokens, grad_query, grad_key, grad_value, grad_output
 
 

time: 103 us -> 95.2 us (0.924)
  the two profiles are of different devices: /device:TPU:10 before, /device:TPU:33 now
where the time goes in v3:
time: 95.2 us; the launch traced here: 94.8 us
  starting transfers between devices  43.5 us (46%)
  waiting for transfers between devices  18.6 us (20%)
  blocking collectives  13.5 us (14%)
  Pallas kernels  13.2 us (14%)
  other arithmetic  3.59 us (4%)
  local copies, waits for them, and re-layouts  1.52 us (2%)
    ppermute x12, starting transfers between devices, swap(): return lax.ppermute(block, axis, swap_pairs(lax.axis_size(axis), kind))  30.6 us
    ppermute x12, waiting for transfers between devices, swap(): return lax.ppermute(block, axis, swap_pairs(lax.axis_size(axis), kind))  15 us
    all_to_all x1, blocking collectives, exchange(): lax.all_to_all(pieces, BOTH, 0, 0, tiled=True, axis_index_groups=groups)  13.5 us
    pallas_call x5, Pallas kernels, call(): pl.pallas_call(kernel, out_shape=tuple((jax.ShapeDtypeStruct(*out) for ou...  13.2 us
    ppermute x3, starting transfers between devices, cross(): lax.ppermute(block, BOTH, [(i, i ^ step) for i in range(lax.axis_size(BOT...  7.33 us
    all_to_all x1, starting transfers between devices, exchange(): lax.all_to_all(pieces, BOTH, 0, 0, tiled=True, axis_index_groups=groups)  5.59 us
    select_n x4, other arithmetic, by_side(): return (jnp.where(odd, first, second), jnp.where(odd, second, first))  2.12 us
  transfers between devices with their start and end apart: 16, of which 9 were waited for; matrix products, arithmetic and copies ran while one was open for 1% of the time, Pallas kernels for 3%

profile of v3, /device:TPU:33, one launch (start us, length us, event | category | flops | bytes accessed | tf_op | source)
XLA Modules:
  0.0 94.8 jit_solution(10358342130522273832)
XLA Ops:
  1.8 5.2 %collective-permute-start.1 = (bf16[16,8,384]{2,1,0:T(8,128)(2,1)S(1)}, bf16[16,8,384]{2,1,0:T(8,128)(2,1)S(1)}, u32[]{:S(2)}, u32[]{:S(2)}) collective-permute-start(bf16[16,8,384]{2,1,0:T(8,128)(2,1)S(1)} %get-tuple-element.73), channel_id=1, source_target_pairs={{1,2},{2,1},{3,4},{4,3},{5,6},{6,5},{7,8},{8,7},{9,10},{10,9},{11,... | collective-permute-start | bytes 294920 | tf_op jit(solution)/shard_map/halo/ppermute | solution.py:36
  8.1 3.5 %collective-permute-start.3 = (bf16[8,16,384]{2,1,0:T(8,128)(2,1)S(1)}, bf16[8,16,384]{2,1,0:T(8,128)(2,1)S(1)}, u32[]{:S(2)}, u32[]{:S(2)}) collective-permute-start(bf16[8,16,384]{2,1,0:T(8,128)(2,1)S(1)} %get-tuple-element.71), channel_id=1, source_target_pairs={{16,32},{32,16},{48,64},{64,48},{80,96},{96,80},{112,128},{128,112... | collective-permute-start | bytes 294920 | tf_op jit(solution)/shard_map/halo/ppermute | solution.py:36
  11.8 6.4 %collective-permute-start.5 = (bf16[8,16,384]{2,1,0:T(8,128)(2,1)S(1)}, bf16[8,16,384]{2,1,0:T(8,128)(2,1)S(1)}, u32[]{:S(2)}, u32[]{:S(2)}) collective-permute-start(bf16[8,16,384]{2,1,0:T(8,128)(2,1)S(1)} %get-tuple-element.67), channel_id=1, source_target_pairs={{16,32},{32,16},{48,64},{64,48},{80,96},{96,80},{112,128},{128,112... | collective-permute-start | bytes 294920 | tf_op jit(solution)/shard_map/halo/ppermute | solution.py:36
  20.2 1.6 %collective-permute-done.4.corner_0 = bf16[8,16,384]{2,1,0:T(8,128)(2,1)S(1)} collective-permute-done((bf16[8,16,384]{2,1,0:T(8,128)(2,1)S(1)}, bf16[8,16,384]{2,1,0:T(8,128)(2,1)S(1)}, u32[]{:S(2)}, u32[]{:S(2)}) %collective-permute-start.4) | collective-permute-done | bytes 98336 | tf_op jit(solution)/shard_map/halo/ppermute | solution.py:36
  21.8 7.7 %attention.1 = (bf16[1024,384]{1,0:T(8,128)(2,1)S(1)}, bf16[1024,384]{1,0:T(8,128)(2,1)S(1)}, bf16[1024,384]{1,0:T(8,128)(2,1)S(1)}, bf16[256,384]{1,0:T(8,128)(...) custom-call(s32[4]{0:T(128)S(1)} %pad_add_fusion.place, ...), custom_call_target="tpu_custom_call" | custom-call | flops 6000000000 | bytes 6000000 | tf_op jit(solution)/shard_map/attention/pallas_call | solution.py:67
  29.4 2.4 %weight_grads.1 = (bf16[768,384]{1,0:T(8,128)(2,1)S(1)}, bf16[768,384]{1,0:T(8,128)(2,1)S(1)}, f32[512,384]{1,0:T(8,128)S(1)}) custom-call(s32[4]{0:T(128)S(1)} %pad_add_fusion.place, bf16[1024,384]{1,0:T(8,128)(2,1)S(1)} %get-tuple-element.38.padded, bf16[1024,384]{1,0:T(8,128)(2,1)S(1)} %get-tuple-element.39.key_grad, ...), custom_call_target="tpu_custom_call" | custom-call | flops 2000000000 | bytes 2000000 | tf_op jit(solution)/shard_map/weight_grads/pallas_call | solution.py:67
  31.8 2.6 %collective-permute-start.6 = (bf16[768,384]{1,0:T(8,128)(2,1)S(1)}, bf16[768,384]{1,0:T(8,128)(2,1)S(1)}, u32[]{:S(2)}, u32[]{:S(2)}) collective-permute-start(bf16[768,384]{1,0:T(8,128)(2,1)S(1)} %get-tuple-element.45), channel_id=1, source_target_pairs={{0,1},{1,0},{2,3},{3,2},{4,5},{5,4},{6,7},{7,6},{8,9},{9,8},{10,11... | collective-permute-start | bytes 1769480 | tf_op jit(solution)/shard_map/core_sum/ppermute | solution.py:36
  34.4 1.6 %collective-permute-done.6 = bf16[768,384]{1,0:T(8,128)(2,1)S(1)} collective-permute-done((bf16[768,384]{1,0:T(8,128)(2,1)S(1)}, bf16[768,384]{1,0:T(8,128)(2,1)S(1)}, u32[]{:S(2)}, u32[]{:S(2)}) %collective-permute-start.6) | collective-permute-done | bytes 589856 | tf_op jit(solution)/shard_map/core_sum/ppermute | solution.py:36
  37.0 5.6 %all-to-all-start = ((bf16[16,48,384]{2,1,0:T(8,128)(2,1)}), bf16[16,48,384]{2,1,0:T(8,128)(2,1)S(1)}, u32[]{:S(2)}, u32[]{:S(2)}) async-start(bf16[16,48,384]{2,1,0:T(8,128)(2,1)} %bitcast.2), calls=%async_computation | async-start | bytes 1179648 | tf_op jit(solution)/shard_map/plane_sum/all_to_all | solution.py:337
  43.5 2.8 %collective-permute-start.8 = (bf16[256,384]{1,0:T(8,128)(2,1)S(1)}, bf16[256,384]{1,0:T(8,128)(2,1)S(1)}, u32[]{:S(2)}, u32[]{:S(2)}) collective-permute-start(bf16[256,384]{1,0:T(8,128)(2,1)S(1)} %get-tuple-element.47), channel_id=1, source_target_pairs={{16,32},{32,16},{48,64},{64,48},{80,96},{96,80},{112,128},{128,112... | collective-permute-start | bytes 589832 | tf_op jit(solution)/shard_map/rows_out/ppermute | solution.py:36
  46.3 2.4 %collective-permute-done.7.from_0 = bf16[256,384]{1,0:T(8,128)(2,1)S(1)} collective-permute-done((bf16[256,384]{1,0:T(8,128)(2,1)S(1)}, bf16[256,384]{1,0:T(8,128)(2,1)S(1)}, u32[]{:S(2)}, u32[]{:S(2)}) %collective-permute-start.7) | collective-permute-done | bytes 196640 | tf_op jit(solution)/shard_map/rows_out/ppermute | solution.py:36
  48.7 2.2 %collective-permute-done.8.from_1 = bf16[256,384]{1,0:T(8,128)(2,1)S(1)} collective-permute-done((bf16[256,384]{1,0:T(8,128)(2,1)S(1)}, bf16[256,384]{1,0:T(8,128)(2,1)S(1)}, u32[]{:S(2)}, u32[]{:S(2)}) %collective-permute-start.8) | collective-permute-done | bytes 196640 | tf_op jit(solution)/shard_map/rows_out/ppermute | solution.py:36
  50.8 1.9 %all-to-all-done = bf16[16,48,384]{2,1,0:T(8,128)(2,1)S(1)} async-done(((bf16[16,48,384]{2,1,0:T(8,128)(2,1)}), bf16[16,48,384]{2,1,0:T(8,128)(2,1)S(1)}, u32[]{:S(2)}, u32[]{:S(2)}) %all-to-all-start) | async-done | bytes 589856 | tf_op jit(solution)/shard_map/plane_sum/all_to_all | solution.py:337
  53.4 2.6 %collective-permute-start.10 = (bf16[128,384]{1,0:T(8,128)(2,1)S(1)}, bf16[128,384]{1,0:T(8,128)(2,1)S(1)}, u32[]{:S(2)}, u32[]{:S(2)}) collective-permute-start(bf16[128,384]{1,0:T(8,128)(2,1)S(1)} %get-tuple-element.52), channel_id=1, source_target_pairs={{0,1},{1,0},{2,3},{3,2},{4,5},{5,4},{6,7},{7,6},{8,9},{9,8},{10,11... | collective-permute-start | bytes 294920 | tf_op jit(solution)/shard_map/line_sum/ppermute | solution.py:36
  56.1 3.8 %collective-permute-start.9 = (bf16[48,384]{1,0:T(8,128)(2,1)S(1)}, bf16[48,384]{1,0:T(8,128)(2,1)S(1)}, u32[]{:S(2)}, u32[]{:S(2)}) collective-permute-start(bf16[48,384]{1,0:T(8,128)(2,1)S(1)} %fusion.1), channel_id=1, source_target_pairs={{0,16},{1,17},{2,18},{3,19},{4,20},{5,21},{6,22},{7,23},{8,24},{9,... | collective-permute-start | bytes 110600 | tf_op jit(solution)/shard_map/line_sum/ppermute | solution.py:333
  59.9 2.8 %collective-permute-start.12 = (bf16[128,384]{1,0:T(8,128)(2,1)S(1)}, bf16[128,384]{1,0:T(8,128)(2,1)S(1)}, u32[]{:S(2)}, u32[]{:S(2)}) collective-permute-start(bf16[128,384]{1,0:T(8,128)(2,1)S(1)} %get-tuple-element.54), channel_id=1, source_target_pairs={{1,2},{2,1},{3,4},{4,3},{5,6},{6,5},{7,8},{8,7},{9,10},{10,9},{11,... | collective-permute-start | bytes 294920 | tf_op jit(solution)/shard_map/line_sum/ppermute | solution.py:36
  62.9 5.1 %collective-permute-done.12.from_1 = bf16[128,384]{1,0:T(8,128)(2,1)S(1)} collective-permute-done((bf16[128,384]{1,0:T(8,128)(2,1)S(1)}, bf16[128,384]{1,0:T(8,128)(2,1)S(1)}, u32[]{:S(2)}, u32[]{:S(2)}) %collective-permute-start.12) | collective-permute-done | bytes 98336 | tf_op jit(solution)/shard_map/line_sum/ppermute | solution.py:36
  68.0 3.4 %collective-permute-start.13 = (bf16[48,384]{1,0:T(8,128)(2,1)S(1)}, bf16[48,384]{1,0:T(8,128)(2,1)S(1)}, u32[]{:S(2)}, u32[]{:S(2)}) collective-permute-start(bf16[48,384]{1,0:T(8,128)(2,1)S(1)} %add_convert_fusion.2), channel_id=1, source_target_pairs={{0,112},{1,113},{2,114},{3,115},{4,116},{5,117},{6,118},{7,119},{8... | collective-permute-start | bytes 110600 | tf_op jit(solution)/shard_map/line_sum/ppermute | solution.py:333
  71.4 1.3 %add_columns.1 = bf16[16,16,384]{2,1,0:T(8,128)(2,1)} custom-call(s32[4]{0:T(128)S(1)} %pad_add_fusion.place, f32[256,384]{1,0:T(8,128)S(1)} %get-tuple-element.56.summed, bf16[128,384]{1,0:T(8,128)(2,1)S(1)} %collective-permute-done.10.from_0, bf16[128,384]{1,0:T(8,128)(2,1)S(1)} %collective-permute-done.12.from_1), custom_call_target="tpu_custom_call" | custom-call | flops 1000000000 | bytes 1000000 | tf_op jit(solution)/shard_map/add_columns/pallas_call | solution.py:67
  72.7 1.7 %collective-permute-done.13 = bf16[48,384]{1,0:T(8,128)(2,1)S(1)} collective-permute-done((bf16[48,384]{1,0:T(8,128)(2,1)S(1)}, bf16[48,384]{1,0:T(8,128)(2,1)S(1)}, u32[]{:S(2)}, u32[]{:S(2)}) %collective-permute-start.13) | collective-permute-done | bytes 36896 | tf_op jit(solution)/shard_map/line_sum/ppermute | solution.py:333
  74.4 13.5 %all_to_all.10 = bf16[16,48,384]{2,1,0:T(8,128)(2,1)S(1)} all-to-all(bf16[16,48,384]{2,1,0:T(8,128)(2,1)S(1)} %broadcast_in_dim.3), channel_id=1, replica_groups={{0,2,4,6,8,10,12,14,128,130,132,134,136,138,140,142},{1,3,5,7,9,11,13,1..., dimensions={0} | all-to-all | bytes 1179648 | tf_op jit(solution)/shard_map/plane_gather/all_to_all | solution.py:337
  88.0 3.6 %collective-permute-start.14 = (bf16[768,384]{1,0:T(8,128)(2,1)S(1)}, bf16[768,384]{1,0:T(8,128)(2,1)S(1)}, u32[]{:S(2)}, u32[]{:S(2)}) collective-permute-start(bf16[768,384]{1,0:T(8,128)(2,1)S(1)} %bitcast.15), channel_id=1, source_target_pairs={{0,1},{1,0},{2,3},{3,2},{4,5},{5,4},{6,7},{7,6},{8,9},{9,8},{10,11... | collective-permute-start | bytes 1769480 | tf_op jit(solution)/shard_map/core_gather/ppermute | solution.py:36
  91.5 1.6 %collective-permute-done.14 = bf16[768,384]{1,0:T(8,128)(2,1)S(1)} collective-permute-done((bf16[768,384]{1,0:T(8,128)(2,1)S(1)}, bf16[768,384]{1,0:T(8,128)(2,1)S(1)}, u32[]{:S(2)}, u32[]{:S(2)}) %collective-permute-start.14) | collective-permute-done | bytes 589856 | tf_op jit(solution)/shard_map/core_gather/ppermute | solution.py:36
  93.4 1.4 %fusion.2 = (f32[384,384]{1,0:T(8,128)}, f32[384,384]{1,0:T(8,128)}, f32[384,384]{1,0:T(8,128)}, f32[384,384]{1,0:T(8,128)}) fusion(f32[768,384]{1,0:T(8,128)S(1)} %get-tuple-element.63, f32[768,384]{1,0:T(8,128)S(1)} %get-tuple-element.64), kind=kLoop, calls=%fused_computation.21 | loop fusion | bytes 4718592 | tf_op jit(solution)/shard_map/slice | solution.py:398
  (39 shorter events, 7.4 us)
Async XLA Ops:
  0.6 17.8 %copy-start = (bf16[16,16,384]{2,1,0:T(8,128)(2,1)S(1)}, bf16[16,16,384]{2,1,0:T(8,128)(2,1)}, u32[]{:S(2)}) copy-start(bf16[16,16,384]{2,1,0:T(8,128)(2,1)} %tokens.1) | copy-start | bytes 589828
  0.6 17.8 %copy-start.4 = (bf16[384,384]{1,0:T(8,128)(2,1)S(1)}, bf16[384,384]{1,0:T(8,128)(2,1)}, u32[]{:S(2)}) copy-start(bf16[384,384]{1,0:T(8,128)(2,1)} %w_value.5) | copy-start | bytes 884740
  0.7 17.7 %copy-start.3 = (bf16[384,384]{1,0:T(8,128)(2,1)S(1)}, bf16[384,384]{1,0:T(8,128)(2,1)}, u32[]{:S(2)}) copy-start(bf16[384,384]{1,0:T(8,128)(2,1)} %w_key.5) | copy-start | bytes 884740
  0.7 17.7 %copy-start.2 = (bf16[384,384]{1,0:T(8,128)(2,1)S(1)}, bf16[384,384]{1,0:T(8,128)(2,1)}, u32[]{:S(2)}) copy-start(bf16[384,384]{1,0:T(8,128)(2,1)} %w_query.3) | copy-start | bytes 884740
  0.7 17.7 %copy-start.1 = (bf16[384,384]{1,0:T(8,128)(2,1)S(1)}, bf16[384,384]{1,0:T(8,128)(2,1)}, u32[]{:S(2)}) copy-start(bf16[384,384]{1,0:T(8,128)(2,1)} %w_out.1) | copy-start | bytes 884740
  0.7 17.7 %copy-start.5 = (bf16[16,16,384]{2,1,0:T(8,128)(2,1)S(1)}, bf16[16,16,384]{2,1,0:T(8,128)(2,1)}, u32[]{:S(2)}) copy-start(bf16[16,16,384]{2,1,0:T(8,128)(2,1)} %grad_out.1) | copy-start | bytes 589828
  1.8 10.0 %collective-permute-start.1 = (bf16[16,8,384]{2,1,0:T(8,128)(2,1)S(1)}, bf16[16,8,384]{2,1,0:T(8,128)(2,1)S(1)}, u32[]{:S(2)}, u32[]{:S(2)}) collective-permute-start(bf16[16,8,384]{2,1,0:T(8,128)(2,1)S(1)} %get-tuple-element.73), channel_id=1, source_target_pairs={{1,2},{2,1},{3,4},{4,3},{5,6},{6,5},{7,8},{8,7},{9,10},{10,9},{11,... | collective-permute-start | bytes 294920 | tf_op jit(solution)/shard_map/halo/ppermute | solution.py:36
  7.0 4.7 %collective-permute-start = (bf16[16,8,384]{2,1,0:T(8,128)(2,1)S(1)}, bf16[16,8,384]{2,1,0:T(8,128)(2,1)S(1)}, u32[]{:S(2)}, u32[]{:S(2)}) collective-permute-start(bf16[16,8,384]{2,1,0:T(8,128)(2,1)S(1)} %get-tuple-element.74), channel_id=1, source_target_pairs={{0,1},{1,0},{2,3},{3,2},{4,5},{5,4},{6,7},{7,6},{8,9},{9,8},{10,11... | collective-permute-start | bytes 294920 | tf_op jit(solution)/shard_map/halo/ppermute | solution.py:36
  8.1 11.6 %collective-permute-start.3 = (bf16[8,16,384]{2,1,0:T(8,128)(2,1)S(1)}, bf16[8,16,384]{2,1,0:T(8,128)(2,1)S(1)}, u32[]{:S(2)}, u32[]{:S(2)}) collective-permute-start(bf16[8,16,384]{2,1,0:T(8,128)(2,1)S(1)} %get-tuple-element.71), channel_id=1, source_target_pairs={{16,32},{32,16},{48,64},{64,48},{80,96},{96,80},{112,128},{128,112... | collective-permute-start | bytes 294920 | tf_op jit(solution)/shard_map/halo/ppermute | solution.py:36
  11.6 8.0 %collective-permute-start.2 = (bf16[8,16,384]{2,1,0:T(8,128)(2,1)S(1)}, bf16[8,16,384]{2,1,0:T(8,128)(2,1)S(1)}, u32[]{:S(2)}, u32[]{:S(2)}) collective-permute-start(bf16[8,16,384]{2,1,0:T(8,128)(2,1)S(1)} %get-tuple-element.72), channel_id=1, source_target_pairs={{0,16},{16,0},{32,48},{48,32},{64,80},{80,64},{96,112},{112,96},{1... | collective-permute-start | bytes 294920 | tf_op jit(solution)/shard_map/halo/ppermute | solution.py:36
  11.8 8.4 %collective-permute-start.5 = (bf16[8,16,384]{2,1,0:T(8,128)(2,1)S(1)}, bf16[8,16,384]{2,1,0:T(8,128)(2,1)S(1)}, u32[]{:S(2)}, u32[]{:S(2)}) collective-permute-start(bf16[8,16,384]{2,1,0:T(8,128)(2,1)S(1)} %get-tuple-element.67), channel_id=1, source_target_pairs={{16,32},{32,16},{48,64},{64,48},{80,96},{96,80},{112,128},{128,112... | collective-permute-start | bytes 294920 | tf_op jit(solution)/shard_map/halo/ppermute | solution.py:36
  18.2 3.6 %collective-permute-start.4 = (bf16[8,16,384]{2,1,0:T(8,128)(2,1)S(1)}, bf16[8,16,384]{2,1,0:T(8,128)(2,1)S(1)}, u32[]{:S(2)}, u32[]{:S(2)}) collective-permute-start(bf16[8,16,384]{2,1,0:T(8,128)(2,1)S(1)} %get-tuple-element.68), channel_id=1, source_target_pairs={{0,16},{16,0},{32,48},{48,32},{64,80},{80,64},{96,112},{112,96},{1... | collective-permute-start | bytes 294920 | tf_op jit(solution)/shard_map/halo/ppermute | solution.py:36
  31.8 4.2 %collective-permute-start.6 = (bf16[768,384]{1,0:T(8,128)(2,1)S(1)}, bf16[768,384]{1,0:T(8,128)(2,1)S(1)}, u32[]{:S(2)}, u32[]{:S(2)}) collective-permute-start(bf16[768,384]{1,0:T(8,128)(2,1)S(1)} %get-tuple-element.45), channel_id=1, source_target_pairs={{0,1},{1,0},{2,3},{3,2},{4,5},{5,4},{6,7},{7,6},{8,9},{9,8},{10,11... | collective-permute-start | bytes 1769480 | tf_op jit(solution)/shard_map/core_sum/ppermute | solution.py:36
  37.0 15.7 %all-to-all-start = ((bf16[16,48,384]{2,1,0:T(8,128)(2,1)}), bf16[16,48,384]{2,1,0:T(8,128)(2,1)S(1)}, u32[]{:S(2)}, u32[]{:S(2)}) async-start(bf16[16,48,384]{2,1,0:T(8,128)(2,1)} %bitcast.2), calls=%async_computation | async-start | bytes 1179648 | tf_op jit(solution)/shard_map/plane_sum/all_to_all | solution.py:337
  42.6 6.1 %collective-permute-start.7 = (bf16[256,384]{1,0:T(8,128)(2,1)S(1)}, bf16[256,384]{1,0:T(8,128)(2,1)S(1)}, u32[]{:S(2)}, u32[]{:S(2)}) collective-permute-start(bf16[256,384]{1,0:T(8,128)(2,1)S(1)} %get-tuple-element.46), channel_id=1, source_target_pairs={{0,16},{16,0},{32,48},{48,32},{64,80},{80,64},{96,112},{112,96},{1... | collective-permute-start | bytes 589832 | tf_op jit(solution)/shard_map/rows_out/ppermute | solution.py:36
  43.5 7.3 %collective-permute-start.8 = (bf16[256,384]{1,0:T(8,128)(2,1)S(1)}, bf16[256,384]{1,0:T(8,128)(2,1)S(1)}, u32[]{:S(2)}, u32[]{:S(2)}) collective-permute-start(bf16[256,384]{1,0:T(8,128)(2,1)S(1)} %get-tuple-element.47), channel_id=1, source_target_pairs={{16,32},{32,16},{48,64},{64,48},{80,96},{96,80},{112,128},{128,112... | collective-permute-start | bytes 589832 | tf_op jit(solution)/shard_map/rows_out/ppermute | solution.py:36
  53.4 9.3 %collective-permute-start.10 = (bf16[128,384]{1,0:T(8,128)(2,1)S(1)}, bf16[128,384]{1,0:T(8,128)(2,1)S(1)}, u32[]{:S(2)}, u32[]{:S(2)}) collective-permute-start(bf16[128,384]{1,0:T(8,128)(2,1)S(1)} %get-tuple-element.52), channel_id=1, source_target_pairs={{0,1},{1,0},{2,3},{3,2},{4,5},{5,4},{6,7},{7,6},{8,9},{9,8},{10,11... | collective-permute-start | bytes 294920 | tf_op jit(solution)/shard_map/line_sum/ppermute | solution.py:36
  56.1 6.6 %collective-permute-start.9 = (bf16[48,384]{1,0:T(8,128)(2,1)S(1)}, bf16[48,384]{1,0:T(8,128)(2,1)S(1)}, u32[]{:S(2)}, u32[]{:S(2)}) collective-permute-start(bf16[48,384]{1,0:T(8,128)(2,1)S(1)} %fusion.1), channel_id=1, source_target_pairs={{0,16},{1,17},{2,18},{3,19},{4,20},{5,21},{6,22},{7,23},{8,24},{9,... | collective-permute-start | bytes 110600 | tf_op jit(solution)/shard_map/line_sum/ppermute | solution.py:333
  59.9 8.0 %collective-permute-start.12 = (bf16[128,384]{1,0:T(8,128)(2,1)S(1)}, bf16[128,384]{1,0:T(8,128)(2,1)S(1)}, u32[]{:S(2)}, u32[]{:S(2)}) collective-permute-start(bf16[128,384]{1,0:T(8,128)(2,1)S(1)} %get-tuple-element.54), channel_id=1, source_target_pairs={{1,2},{2,1},{3,4},{4,3},{5,6},{6,5},{7,8},{8,7},{9,10},{10,9},{11,... | collective-permute-start | bytes 294920 | tf_op jit(solution)/shard_map/line_sum/ppermute | solution.py:36
  62.8 5.2 %collective-permute-start.11 = (bf16[48,384]{1,0:T(8,128)(2,1)S(1)}, bf16[48,384]{1,0:T(8,128)(2,1)S(1)}, u32[]{:S(2)}, u32[]{:S(2)}) collective-permute-start(bf16[48,384]{1,0:T(8,128)(2,1)S(1)} %add_convert_fusion.3), channel_id=1, source_target_pairs={{0,32},{1,33},{2,34},{3,35},{4,36},{5,37},{6,38},{7,39},{8,40},{9,... | collective-permute-start | bytes 110600 | tf_op jit(solution)/shard_map/line_sum/ppermute | solution.py:333
  68.0 6.4 %collective-permute-start.13 = (bf16[48,384]{1,0:T(8,128)(2,1)S(1)}, bf16[48,384]{1,0:T(8,128)(2,1)S(1)}, u32[]{:S(2)}, u32[]{:S(2)}) collective-permute-start(bf16[48,384]{1,0:T(8,128)(2,1)S(1)} %add_convert_fusion.2), channel_id=1, source_target_pairs={{0,112},{1,113},{2,114},{3,115},{4,116},{5,117},{6,118},{7,119},{8... | collective-permute-start | bytes 110600 | tf_op jit(solution)/shard_map/line_sum/ppermute | solution.py:333
  88.0 5.2 %collective-permute-start.14 = (bf16[768,384]{1,0:T(8,128)(2,1)S(1)}, bf16[768,384]{1,0:T(8,128)(2,1)S(1)}, u32[]{:S(2)}, u32[]{:S(2)}) collective-permute-start(bf16[768,384]{1,0:T(8,128)(2,1)S(1)} %bitcast.15), channel_id=1, source_target_pairs={{0,1},{1,0},{2,3},{3,2},{4,5},{5,4},{6,7},{7,6},{8,9},{9,8},{10,11... | collective-permute-start | bytes 1769480 | tf_op jit(solution)/shard_map/core_gather/ppermute | solution.py:36

commit v4 on v3

--- a/solution.py
+++ b/solution.py
@@ -109,7 +109,7 @@
 def attention_kernel(
     place, tiles, query, grad_att, own_key, own_value, col_0, col_1, row_0, row_1, corner_0, corner_1,
     w_key, w_value,
-    padded, key_grad, value_grad, attended, grad_q, send_0, send_1,
+    padded, key_grad, value_grad, attended, grad_q,
     key, value, key_total, value_total, halo,
 ):
     row_at, row_last, col_at, col_last = place[0], place[1], place[2], place[3]
@@ -214,20 +214,12 @@
 
     key_grad[...] = key_total[...].astype(HALF)
     value_grad[...] = value_total[...].astype(HALF)
-    north, south = slice(0, 4 * AREA), slice(12 * AREA, ALL)
-    key_rim = jnp.concatenate([key_grad[north, :], key_grad[south, :]], axis=0)
-    value_rim = jnp.concatenate([value_grad[north, :], value_grad[south, :]], axis=0)
-    spread = dot(key_rim, w_key[...], NT) + dot(value_rim, w_value[...], NT)
-    above, below = spread[: 4 * AREA], spread[4 * AREA :]
-    send_0[...] = jnp.where(row_even, below, above).astype(HALF)
-    send_1[...] = jnp.where(row_even, above, below).astype(HALF)
 
 
 attention = local_call(
     attention_kernel,
     [((ALL, FEATURE), HALF)] * 3
-    + [((OWN, FEATURE), HALF)] * 2
-    + [((4 * AREA, FEATURE), HALF)] * 2,
+    + [((OWN, FEATURE), HALF)] * 2,
     [((ALL, FEATURE), HALF)] * 2 + [((ALL, FEATURE), FULL)] * 2 + [((12 * AREA, FEATURE), HALF)],
     24,
     6,
@@ -236,8 +228,7 @@
 
 
 def weights_kernel(
-    place, padded, key_grad, value_grad, tiles, flat_grad, attended, grad_q, w_query, w_key, w_value,
-    keep, give, own,
+    place, padded, key_grad, value_grad, tiles, flat_grad, attended, grad_q, keep, give,
 ):
     even = lax.rem(place[2], 2) == 0
     tokens_all = padded[...]
@@ -248,25 +239,35 @@
     for n, (zero, one) in enumerate(((grad_output, grad_query), (grad_value, grad_key))):
         keep[n * FEATURE : (n + 1) * FEATURE, :] = jnp.where(even, zero, one).astype(HALF)
         give[n * FEATURE : (n + 1) * FEATURE, :] = jnp.where(even, one, zero).astype(HALF)
-    middle = slice(4 * AREA, 12 * AREA)
-    spread = dot(key_grad[middle, :], w_key[...], NT) + dot(value_grad[middle, :], w_value[...], NT)
+
+
+weight_grads = local_call(
+    weights_kernel, [((2 * FEATURE, FEATURE), HALF)] * 2, [], 16, 2, "weight_grads"
+)
+
+
+def spread_kernel(place, key_grad, value_grad, grad_q, w_query, w_key, w_value, own, send_0, send_1):
+    row_even = lax.rem(place[0], 2) == 0
+    spread = dot(key_grad[...], w_key[...], NT) + dot(value_grad[...], w_value[...], NT)
+    above, below = spread[: 4 * AREA], spread[12 * AREA :]
+    send_0[...] = jnp.where(row_even, below, above).astype(HALF)
+    send_1[...] = jnp.where(row_even, above, below).astype(HALF)
     query_part = dot(grad_q[...], w_query[...], NT)
     for i in range(2):
         row, mine = i * 4 * AREA, i * 2 * AREA
-        own[row : row + AREA, :] = spread[row : row + AREA]
-        own[row + AREA : row + 3 * AREA, :] = (
-            spread[row + AREA : row + 3 * AREA] + query_part[mine : mine + 2 * AREA]
-        )
-        own[row + 3 * AREA : row + 4 * AREA, :] = spread[row + 3 * AREA : row + 4 * AREA]
-
-
-weight_grads = local_call(
-    weights_kernel,
-    [((2 * FEATURE, FEATURE), HALF)] * 2 + [((8 * AREA, FEATURE), FULL)],
+        part = spread[(i + 1) * 4 * AREA : (i + 2) * 4 * AREA]
+        own[row : row + AREA, :] = part[:AREA]
+        own[row + AREA : row + 3 * AREA, :] = part[AREA : 3 * AREA] + query_part[mine : mine + 2 * AREA]
+        own[row + 3 * AREA : row + 4 * AREA, :] = part[3 * AREA :]
+
+
+spread_grads = local_call(
+    spread_kernel,
+    [((8 * AREA, FEATURE), FULL)] + [((4 * AREA, FEATURE), HALF)] * 2,
     [],
     16,
-    2,
-    "weight_grads",
+    1,
+    "spread_grads",
 )
 
 
@@ -361,36 +362,35 @@
     tiles, flat_grad, query, grad_att, key, value = own_projections(
         place, tokens, grad_out, w_query, w_key, w_value, w_out
     )
-    padded, key_grad, value_grad, attended, grad_q, send_0, send_1 = attention(
+    padded, key_grad, value_grad, attended, grad_q = attention(
         place, tiles, query, grad_att, key, value, *halo, w_key, w_value
     )
-    with jax.named_scope("rows_out"):
-        from_0, from_1 = swap(send_0, "row", 0), swap(send_1, "row", 1)
-    keep, give, own = weight_grads(
-        place, padded, key_grad, value_grad, tiles, flat_grad, attended, grad_q,
-        w_query, w_key, w_value,
+    keep, give = weight_grads(
+        place, padded, key_grad, value_grad, tiles, flat_grad, attended, grad_q
+    )
+    own, send_0, send_1 = spread_grads(
+        place, key_grad, value_grad, grad_q, w_query, w_key, w_value
     )
     with jax.named_scope("core_sum"):
-        part = keep.astype(FULL) + swap(give, "col", 0).astype(FULL)
-    part = part.astype(HALF)
+        other, own = tied((swap(give, "col", 0), own))
+        part = (keep.astype(FULL) + other.astype(FULL)).astype(HALF)
     with jax.named_scope("plane_sum"):
         part = exchange(part.reshape(16, -1, FEATURE), planes)
+        part, from_0 = tied((part, swap(send_0, "row", 0)))
+        part = add_pieces(part)
+    with jax.named_scope("line_sum"):
+        for n, step in enumerate(LINE_STEPS):
+            other = cross(part, step)
+            if n == 1:
+                other, from_2 = tied((other, swap(send_1, "row", 1)))
+            part = (part.astype(FULL) + other.astype(FULL)).astype(HALF)
+    summed, send_0, send_1 = add_rows(place, own, from_0, from_2)
+    with jax.named_scope("plane_gather"):
+        part = exchange(jnp.broadcast_to(part, (16,) + part.shape), planes)
+        from_0, from_1 = swap(send_0, "col", 0), swap(send_1, "col", 1)
         part, from_0, from_1 = tied((part, from_0, from_1))
-        part = add_pieces(part)
-    summed, send_0, send_1 = add_rows(place, own, from_0, from_1)
-    with jax.named_scope("line_sum"):
-        columns = []
-        for step, strip, kind in zip(LINE_STEPS, (send_0, send_1, None), (0, 1, None)):
-            other = cross(part, step)
-            if strip is not None:
-                other, strip = tied((other, swap(strip, "col", kind)))
-                columns.append(strip)
-            part = (part.astype(FULL) + other.astype(FULL)).astype(HALF)
-    (grad_tokens,) = add_columns(place, summed, *columns)
-    with jax.named_scope("plane_gather"):
-        part, grad_tokens = tied((part, grad_tokens))
-        part = jnp.broadcast_to(part, (16,) + part.shape)
-        part = exchange(part, planes).reshape(-1, FEATURE)
+        part = part.reshape(-1, FEATURE)
+    (grad_tokens,) = add_columns(place, summed, from_0, from_1)
     with jax.named_scope("core_gather"):
         other = swap(part, "col", 0)
         first = jnp.where(core == 0, part, other).astype(FULL)

time: 95.2 us -> 90.5 us (0.951)
  the two profiles are of different devices: /device:TPU:33 before, /device:TPU:10 now
where the time goes in v4:
time: 90.5 us; the launch traced here: 89.3 us
  starting transfers between devices  41.8 us (46%)
  waiting for transfers between devices  26.9 us (30%)
  Pallas kernels  13.8 us (15%)
  other arithmetic  3.59 us (4%)
  local copies, waits for them, and re-layouts  2.33 us (3%)
    ppermute x12, starting transfers between devices, swap(): return lax.ppermute(block, axis, swap_pairs(lax.axis_size(axis), kind))  26.4 us
    ppermute x12, waiting for transfers between devices, swap(): return lax.ppermute(block, axis, swap_pairs(lax.axis_size(axis), kind))  19.8 us
    pallas_call x6, Pallas kernels, call(): pl.pallas_call(kernel, out_shape=tuple((jax.ShapeDtypeStruct(*out) for ou...  13.8 us
    all_to_all x2, starting transfers between devices, exchange(): lax.all_to_all(pieces, BOTH, 0, 0, tiled=True, axis_index_groups=groups)  12.2 us
    ppermute x3, waiting for transfers between devices, cross(): lax.ppermute(block, BOTH, [(i, i ^ step) for i in range(lax.axis_size(BOT...  4 us
    ppermute x3, starting transfers between devices, cross(): lax.ppermute(block, BOTH, [(i, i ^ step) for i in range(lax.axis_size(BOT...  3.16 us
    all_to_all x2, waiting for transfers between devices, exchange(): lax.all_to_all(pieces, BOTH, 0, 0, tiled=True, axis_index_groups=groups)  3.14 us
    select_n x4, other arithmetic, by_side(): return (jnp.where(odd, first, second), jnp.where(odd, second, first))  2.11 us
  transfers between devices with their start and end apart: 17, of which 8 were waited for; matrix products, arithmetic and copies ran while one was open for 1% of the time, Pallas kernels for 6%

profile of v4, /device:TPU:10, one launch (start us, length us, event | category | flops | bytes accessed | tf_op | source)
XLA Modules:
  0.0 89.3 jit_solution(10959946084045309351)
XLA Ops:
  0.7 1.1 %broadcast_select_fusion.6 = (bf16[16,8,384]{2,1,0:T(8,128)(2,1)S(1)}, bf16[16,8,384]{2,1,0:T(8,128)(2,1)S(1)}) fusion(pred[]{:T(512)S(6)} %eq.12, bf16[16,16,384]{2,1,0:T(8,128)(2,1)} %tokens.1), kind=kLoop, calls=%fused_computation.13 | loop fusion | flops 98304 | bytes 393217 | tf_op jit(solution)/shard_map/halo/jit(_where)/select_n | solution.py:41
  1.8 3.4 %collective-permute-start.1 = (bf16[16,8,384]{2,1,0:T(8,128)(2,1)S(1)}, bf16[16,8,384]{2,1,0:T(8,128)(2,1)S(1)}, u32[]{:S(2)}, u32[]{:S(2)}) collective-permute-start(bf16[16,8,384]{2,1,0:T(8,128)(2,1)S(1)} %get-tuple-element.73), channel_id=1, source_target_pairs={{1,2},{2,1},{3,4},{4,3},{5,6},{6,5},{7,8},{8,7},{9,10},{10,9},{11,... | collective-permute-start | bytes 294920 | tf_op jit(solution)/shard_map/halo/ppermute | solution.py:36
  7.0 8.6 %collective-permute-start.3 = (bf16[8,16,384]{2,1,0:T(8,128)(2,1)S(1)}, bf16[8,16,384]{2,1,0:T(8,128)(2,1)S(1)}, u32[]{:S(2)}, u32[]{:S(2)}) collective-permute-start(bf16[8,16,384]{2,1,0:T(8,128)(2,1)S(1)} %get-tuple-element.71), channel_id=1, source_target_pairs={{16,32},{32,16},{48,64},{64,48},{80,96},{96,80},{112,128},{128,112... | collective-permute-start | bytes 294920 | tf_op jit(solution)/shard_map/halo/ppermute | solution.py:36
  15.8 3.9 %collective-permute-start.5 = (bf16[8,16,384]{2,1,0:T(8,128)(2,1)S(1)}, bf16[8,16,384]{2,1,0:T(8,128)(2,1)S(1)}, u32[]{:S(2)}, u32[]{:S(2)}) collective-permute-start(bf16[8,16,384]{2,1,0:T(8,128)(2,1)S(1)} %get-tuple-element.67), channel_id=1, source_target_pairs={{16,32},{32,16},{48,64},{64,48},{80,96},{96,80},{112,128},{128,112... | collective-permute-start | bytes 294920 | tf_op jit(solution)/shard_map/halo/ppermute | solution.py:36
  20.1 1.2 %own_projections.1 = (bf16[256,384]{1,0:T(8,128)(2,1)S(1)}, bf16[256,384]{1,0:T(8,128)(2,1)S(1)}, bf16[256,384]{1,0:T(8,128)(2,1)S(1)}, bf16[256,384]{1,0:T(8,12...) custom-call(s32[4]{0:T(128)S(1)} %pad_add_fusion.place, bf16[16,16,384]{2,1,0:T(8,128)(2,1)S(1)} %copy-done, ...), custom_call_target="tpu_custom_call" | custom-call | flops 1000000000 | bytes 1000000 | tf_op jit(solution)/shard_map/own_projections/pallas_call | solution.py:67
  21.3 3.2 %collective-permute-done.5.corner_1 = bf16[8,16,384]{2,1,0:T(8,128)(2,1)S(1)} collective-permute-done((bf16[8,16,384]{2,1,0:T(8,128)(2,1)S(1)}, bf16[8,16,384]{2,1,0:T(8,128)(2,1)S(1)}, u32[]{:S(2)}, u32[]{:S(2)}) %collective-permute-start.5) | collective-permute-done | bytes 98336 | tf_op jit(solution)/shard_map/halo/ppermute | solution.py:36
  24.5 7.0 %attention.1 = (bf16[1024,384]{1,0:T(8,128)(2,1)S(1)}, bf16[1024,384]{1,0:T(8,128)(2,1)S(1)}, bf16[1024,384]{1,0:T(8,128)(2,1)S(1)}, bf16[256,384]{1,0:T(8,128)(2,1)S(1)}, bf16[256,384]{1,0:T(8,128)(2,1)S(1)}) custom-call(s32[4]{0:T(128)S(1)} %pad_add_fusion.place, bf16[256,384]{1,0:T(8,128)(2,1)S(1)} %get-tuple-element.33.tiles, ...), custom_call_target="tpu_custom_call" | custom-call | flops 6000000000 | bytes 6000000 | tf_op jit(solution)/shard_map/attention/pallas_call | solution.py:67
  31.5 1.8 %weight_grads.1 = (bf16[768,384]{1,0:T(8,128)(2,1)S(1)}, bf16[768,384]{1,0:T(8,128)(2,1)S(1)}) custom-call(s32[4]{0:T(128)S(1)} %pad_add_fusion.place, bf16[1024,384]{1,0:T(8,128)(2,1)S(1)} %get-tuple-element.38.padded, bf16[1024,384]{1,0:T(8,128)(2,1)S(1)} %get-tuple-element.39.key_grad, bf16[1024,384]{1,0:T(8,128)(2,1)S(1)} %get-tuple-element.40.value_grad, ...), custom_call_target="tpu_custom_call" | custom-call | flops 2000000000 | bytes 2000000 | tf_op jit(solution)/shard_map/weight_grads/pallas_call | solution.py:67
  33.4 1.8 %spread_grads.1 = (f32[512,384]{1,0:T(8,128)S(1)}, bf16[256,384]{1,0:T(8,128)(2,1)S(1)}, bf16[256,384]{1,0:T(8,128)(2,1)S(1)}) custom-call(s32[4]{0:T(128)S(1)} %pad_add_fusion.place, bf16[1024,384]{1,0:T(8,128)(2,1)S(1)} %get-tuple-element.39.key_grad, bf16[1024,384]{1,0:T(8,128)(2,1)S(1)} %get-tuple-element.40.value_grad, ...), custom_call_target="tpu_custom_call" | custom-call | flops 1000000000 | bytes 1000000 | tf_op jit(solution)/shard_map/spread_grads/pallas_call | solution.py:67
  35.4 1.0 %add_convert_fusion = bf16[768,384]{1,0:T(8,128)(2,1)} fusion(bf16[768,384]{1,0:T(8,128)(2,1)S(1)} %collective-permute-done.6, bf16[768,384]{1,0:T(8,128)(2,1)S(1)} %get-tuple-element.47), kind=kLoop, calls=%fused_computation | loop fusion | flops 1179648 | bytes 1769472 | tf_op jit(solution)/shard_map/core_sum/convert_element_type | solution.py:376
  36.3 6.1 %all-to-all-start = ((bf16[16,48,384]{2,1,0:T(8,128)(2,1)}), bf16[16,48,384]{2,1,0:T(8,128)(2,1)S(1)}, u32[]{:S(2)}, u32[]{:S(2)}) async-start(bf16[16,48,384]{2,1,0:T(8,128)(2,1)} %bitcast.2), calls=%async_computation | async-start | bytes 1179648 | tf_op jit(solution)/shard_map/plane_sum/all_to_all | solution.py:338
  42.4 1.1 %collective-permute-start.7 = (bf16[256,384]{1,0:T(8,128)(2,1)S(1)}, bf16[256,384]{1,0:T(8,128)(2,1)S(1)}, u32[]{:S(2)}, u32[]{:S(2)}) collective-permute-start(bf16[256,384]{1,0:T(8,128)(2,1)S(1)} %get-tuple-element.49), channel_id=1, source_target_pairs={{0,16},{16,0},{32,48},{48,32},{64,80},{80,64},{96,112},{112,96},{1... | collective-permute-start | bytes 589832 | tf_op jit(solution)/shard_map/plane_sum/ppermute | solution.py:36
  43.6 5.4 %collective-permute-done.7.from_0 = bf16[256,384]{1,0:T(8,128)(2,1)S(1)} collective-permute-done((bf16[256,384]{1,0:T(8,128)(2,1)S(1)}, bf16[256,384]{1,0:T(8,128)(2,1)S(1)}, u32[]{:S(2)}, u32[]{:S(2)}) %collective-permute-start.7) | collective-permute-done | bytes 196640 | tf_op jit(solution)/shard_map/plane_sum/ppermute | solution.py:36
  49.0 3.1 %all-to-all-done = bf16[16,48,384]{2,1,0:T(8,128)(2,1)S(1)} async-done(((bf16[16,48,384]{2,1,0:T(8,128)(2,1)}), bf16[16,48,384]{2,1,0:T(8,128)(2,1)S(1)}, u32[]{:S(2)}, u32[]{:S(2)}) %all-to-all-start) | async-done | bytes 589856 | tf_op jit(solution)/shard_map/plane_sum/all_to_all | solution.py:338
  52.2 1.2 %collective-permute-start.8 = (bf16[48,384]{1,0:T(8,128)(2,1)S(1)}, bf16[48,384]{1,0:T(8,128)(2,1)S(1)}, u32[]{:S(2)}, u32[]{:S(2)}) collective-permute-start(bf16[48,384]{1,0:T(8,128)(2,1)S(1)} %fusion.1), channel_id=1, source_target_pairs={{0,16},{1,17},{2,18},{3,19},{4,20},{5,21},{6,22},{7,23},{8,24},{9,... | collective-permute-start | bytes 110600 | tf_op jit(solution)/shard_map/line_sum/ppermute | solution.py:334
  53.4 4.0 %collective-permute-start.10 = (bf16[256,384]{1,0:T(8,128)(2,1)S(1)}, bf16[256,384]{1,0:T(8,128)(2,1)S(1)}, u32[]{:S(2)}, u32[]{:S(2)}) collective-permute-start(bf16[256,384]{1,0:T(8,128)(2,1)S(1)} %get-tuple-element.52), channel_id=1, source_target_pairs={{16,32},{32,16},{48,64},{64,48},{80,96},{96,80},{112,128},{128,112... | collective-permute-start | bytes 589832 | tf_op jit(solution)/shard_map/line_sum/ppermute | solution.py:36
  57.9 5.2 %collective-permute-done.10.from_1 = bf16[256,384]{1,0:T(8,128)(2,1)S(1)} collective-permute-done((bf16[256,384]{1,0:T(8,128)(2,1)S(1)}, bf16[256,384]{1,0:T(8,128)(2,1)S(1)}, u32[]{:S(2)}, u32[]{:S(2)}) %collective-permute-start.10) | collective-permute-done | bytes 196640 | tf_op jit(solution)/shard_map/line_sum/ppermute | solution.py:36
  63.1 1.6 %collective-permute-start.11 = (bf16[48,384]{1,0:T(8,128)(2,1)S(1)}, bf16[48,384]{1,0:T(8,128)(2,1)S(1)}, u32[]{:S(2)}, u32[]{:S(2)}) collective-permute-start(bf16[48,384]{1,0:T(8,128)(2,1)S(1)} %add_convert_fusion.2), channel_id=1, source_target_pairs={{0,112},{1,113},{2,114},{3,115},{4,116},{5,117},{6,118},{7,119},{8... | collective-permute-start | bytes 110600 | tf_op jit(solution)/shard_map/line_sum/ppermute | solution.py:334
  64.7 4.0 %collective-permute-done.11 = bf16[48,384]{1,0:T(8,128)(2,1)S(1)} collective-permute-done((bf16[48,384]{1,0:T(8,128)(2,1)S(1)}, bf16[48,384]{1,0:T(8,128)(2,1)S(1)}, u32[]{:S(2)}, u32[]{:S(2)}) %collective-permute-start.11) | collective-permute-done | bytes 36896 | tf_op jit(solution)/shard_map/line_sum/ppermute | solution.py:334
  69.5 6.1 %all-to-all-start.1 = ((bf16[16,48,384]{2,1,0:T(8,128)(2,1)}), bf16[16,48,384]{2,1,0:T(8,128)(2,1)S(1)}, u32[]{:S(2)}, u32[]{:S(2)}) async-start(bf16[16,48,384]{2,1,0:T(8,128)(2,1)} %broadcast_in_dim.3), calls=%async_computation.1 | async-start | bytes 1179648 | tf_op jit(solution)/shard_map/plane_gather/all_to_all | solution.py:338
  76.4 4.1 %collective-permute-start.13 = (bf16[128,384]{1,0:T(8,128)(2,1)S(1)}, bf16[128,384]{1,0:T(8,128)(2,1)S(1)}, u32[]{:S(2)}, u32[]{:S(2)}) collective-permute-start(bf16[128,384]{1,0:T(8,128)(2,1)S(1)} %get-tuple-element.57), channel_id=1, source_target_pairs={{1,2},{2,1},{3,4},{4,3},{5,6},{6,5},{7,8},{8,7},{9,10},{10,9},{11,... | collective-permute-start | bytes 294920 | tf_op jit(solution)/shard_map/plane_gather/ppermute | solution.py:36
  80.5 5.1 %collective-permute-done.13.from_1 = bf16[128,384]{1,0:T(8,128)(2,1)S(1)} collective-permute-done((bf16[128,384]{1,0:T(8,128)(2,1)S(1)}, bf16[128,384]{1,0:T(8,128)(2,1)S(1)}, u32[]{:S(2)}, u32[]{:S(2)}) %collective-permute-start.13) | collective-permute-done | bytes 98336 | tf_op jit(solution)/shard_map/plane_gather/ppermute | solution.py:36
  85.6 1.3 %add_columns.1 = bf16[16,16,384]{2,1,0:T(8,128)(2,1)} custom-call(s32[4]{0:T(128)S(1)} %pad_add_fusion.place, f32[256,384]{1,0:T(8,128)S(1)} %get-tuple-element.54.summed, bf16[128,384]{1,0:T(8,128)(2,1)S(1)} %collective-permute-done.12.from_0, bf16[128,384]{1,0:T(8,128)(2,1)S(1)} %collective-permute-done.13.from_1), custom_call_target="tpu_custom_call" | custom-call | flops 1000000000 | bytes 1000000 | tf_op jit(solution)/shard_map/add_columns/pallas_call | solution.py:67
  87.8 1.4 %fusion.2 = (f32[384,384]{1,0:T(8,128)}, f32[384,384]{1,0:T(8,128)}, f32[384,384]{1,0:T(8,128)}, f32[384,384]{1,0:T(8,128)}) fusion(f32[768,384]{1,0:T(8,128)S(1)} %get-tuple-element.63, f32[768,384]{1,0:T(8,128)S(1)} %get-tuple-element.64), kind=kLoop, calls=%fused_computation.21 | loop fusion | bytes 4718592 | tf_op jit(solution)/shard_map/slice | solution.py:398
  (41 shorter events, 5.8 us)
Async XLA Ops:
  0.6 19.4 %copy-start = (bf16[16,16,384]{2,1,0:T(8,128)(2,1)S(1)}, bf16[16,16,384]{2,1,0:T(8,128)(2,1)}, u32[]{:S(2)}) copy-start(bf16[16,16,384]{2,1,0:T(8,128)(2,1)} %tokens.1) | copy-start | bytes 589828
  0.6 19.4 %copy-start.4 = (bf16[384,384]{1,0:T(8,128)(2,1)S(1)}, bf16[384,384]{1,0:T(8,128)(2,1)}, u32[]{:S(2)}) copy-start(bf16[384,384]{1,0:T(8,128)(2,1)} %w_value.5) | copy-start | bytes 884740
  0.7 19.4 %copy-start.3 = (bf16[384,384]{1,0:T(8,128)(2,1)S(1)}, bf16[384,384]{1,0:T(8,128)(2,1)}, u32[]{:S(2)}) copy-start(bf16[384,384]{1,0:T(8,128)(2,1)} %w_key.5) | copy-start | bytes 884740
  0.7 19.4 %copy-start.2 = (bf16[384,384]{1,0:T(8,128)(2,1)S(1)}, bf16[384,384]{1,0:T(8,128)(2,1)}, u32[]{:S(2)}) copy-start(bf16[384,384]{1,0:T(8,128)(2,1)} %w_query.3) | copy-start | bytes 884740
  0.7 19.4 %copy-start.1 = (bf16[384,384]{1,0:T(8,128)(2,1)S(1)}, bf16[384,384]{1,0:T(8,128)(2,1)}, u32[]{:S(2)}) copy-start(bf16[384,384]{1,0:T(8,128)(2,1)} %w_out.1) | copy-start | bytes 884740
  0.7 19.4 %copy-start.5 = (bf16[16,16,384]{2,1,0:T(8,128)(2,1)S(1)}, bf16[16,16,384]{2,1,0:T(8,128)(2,1)}, u32[]{:S(2)}) copy-start(bf16[16,16,384]{2,1,0:T(8,128)(2,1)} %grad_out.1) | copy-start | bytes 589828
  1.8 14.0 %collective-permute-start.1 = (bf16[16,8,384]{2,1,0:T(8,128)(2,1)S(1)}, bf16[16,8,384]{2,1,0:T(8,128)(2,1)S(1)}, u32[]{:S(2)}, u32[]{:S(2)}) collective-permute-start(bf16[16,8,384]{2,1,0:T(8,128)(2,1)S(1)} %get-tuple-element.73), channel_id=1, source_target_pairs={{1,2},{2,1},{3,4},{4,3},{5,6},{6,5},{7,8},{8,7},{9,10},{10,9},{11,... | collective-permute-start | bytes 294920 | tf_op jit(solution)/shard_map/halo/ppermute | solution.py:36
  5.1 10.6 %collective-permute-start = (bf16[16,8,384]{2,1,0:T(8,128)(2,1)S(1)}, bf16[16,8,384]{2,1,0:T(8,128)(2,1)S(1)}, u32[]{:S(2)}, u32[]{:S(2)}) collective-permute-start(bf16[16,8,384]{2,1,0:T(8,128)(2,1)S(1)} %get-tuple-element.74), channel_id=1, source_target_pairs={{0,1},{1,0},{2,3},{3,2},{4,5},{5,4},{6,7},{7,6},{8,9},{9,8},{10,11... | collective-permute-start | bytes 294920 | tf_op jit(solution)/shard_map/halo/ppermute | solution.py:36
  7.0 14.3 %collective-permute-start.3 = (bf16[8,16,384]{2,1,0:T(8,128)(2,1)S(1)}, bf16[8,16,384]{2,1,0:T(8,128)(2,1)S(1)}, u32[]{:S(2)}, u32[]{:S(2)}) collective-permute-start(bf16[8,16,384]{2,1,0:T(8,128)(2,1)S(1)} %get-tuple-element.71), channel_id=1, source_target_pairs={{16,32},{32,16},{48,64},{64,48},{80,96},{96,80},{112,128},{128,112... | collective-permute-start | bytes 294920 | tf_op jit(solution)/shard_map/halo/ppermute | solution.py:36
  15.6 5.7 %collective-permute-start.2 = (bf16[8,16,384]{2,1,0:T(8,128)(2,1)S(1)}, bf16[8,16,384]{2,1,0:T(8,128)(2,1)S(1)}, u32[]{:S(2)}, u32[]{:S(2)}) collective-permute-start(bf16[8,16,384]{2,1,0:T(8,128)(2,1)S(1)} %get-tuple-element.72), channel_id=1, source_target_pairs={{0,16},{16,0},{32,48},{48,32},{64,80},{80,64},{96,112},{112,96},{1... | collective-permute-start | bytes 294920 | tf_op jit(solution)/shard_map/halo/ppermute | solution.py:36
  15.8 8.6 %collective-permute-start.5 = (bf16[8,16,384]{2,1,0:T(8,128)(2,1)S(1)}, bf16[8,16,384]{2,1,0:T(8,128)(2,1)S(1)}, u32[]{:S(2)}, u32[]{:S(2)}) collective-permute-start(bf16[8,16,384]{2,1,0:T(8,128)(2,1)S(1)} %get-tuple-element.67), channel_id=1, source_target_pairs={{16,32},{32,16},{48,64},{64,48},{80,96},{96,80},{112,128},{128,112... | collective-permute-start | bytes 294920 | tf_op jit(solution)/shard_map/halo/ppermute | solution.py:36
  19.7 4.7 %collective-permute-start.4 = (bf16[8,16,384]{2,1,0:T(8,128)(2,1)S(1)}, bf16[8,16,384]{2,1,0:T(8,128)(2,1)S(1)}, u32[]{:S(2)}, u32[]{:S(2)}) collective-permute-start(bf16[8,16,384]{2,1,0:T(8,128)(2,1)S(1)} %get-tuple-element.68), channel_id=1, source_target_pairs={{0,16},{16,0},{32,48},{48,32},{64,80},{80,64},{96,112},{112,96},{1... | collective-permute-start | bytes 294920 | tf_op jit(solution)/shard_map/halo/ppermute | solution.py:36
  33.3 2.1 %collective-permute-start.6 = (bf16[768,384]{1,0:T(8,128)(2,1)S(1)}, bf16[768,384]{1,0:T(8,128)(2,1)S(1)}, u32[]{:S(2)}, u32[]{:S(2)}) collective-permute-start(bf16[768,384]{1,0:T(8,128)(2,1)S(1)} %get-tuple-element.44), channel_id=1, source_target_pairs={{0,1},{1,0},{2,3},{3,2},{4,5},{5,4},{6,7},{7,6},{8,9},{9,8},{10,11... | collective-permute-start | bytes 1769480 | tf_op jit(solution)/shard_map/core_sum/ppermute | solution.py:36
  36.3 15.8 %all-to-all-start = ((bf16[16,48,384]{2,1,0:T(8,128)(2,1)}), bf16[16,48,384]{2,1,0:T(8,128)(2,1)S(1)}, u32[]{:S(2)}, u32[]{:S(2)}) async-start(bf16[16,48,384]{2,1,0:T(8,128)(2,1)} %bitcast.2), calls=%async_computation | async-start | bytes 1179648 | tf_op jit(solution)/shard_map/plane_sum/all_to_all | solution.py:338
  42.4 6.6 %collective-permute-start.7 = (bf16[256,384]{1,0:T(8,128)(2,1)S(1)}, bf16[256,384]{1,0:T(8,128)(2,1)S(1)}, u32[]{:S(2)}, u32[]{:S(2)}) collective-permute-start(bf16[256,384]{1,0:T(8,128)(2,1)S(1)} %get-tuple-element.49), channel_id=1, source_target_pairs={{0,16},{16,0},{32,48},{48,32},{64,80},{80,64},{96,112},{112,96},{1... | collective-permute-start | bytes 589832 | tf_op jit(solution)/shard_map/plane_sum/ppermute | solution.py:36
  52.2 5.2 %collective-permute-start.8 = (bf16[48,384]{1,0:T(8,128)(2,1)S(1)}, bf16[48,384]{1,0:T(8,128)(2,1)S(1)}, u32[]{:S(2)}, u32[]{:S(2)}) collective-permute-start(bf16[48,384]{1,0:T(8,128)(2,1)S(1)} %fusion.1), channel_id=1, source_target_pairs={{0,16},{1,17},{2,18},{3,19},{4,20},{5,21},{6,22},{7,23},{8,24},{9,... | collective-permute-start | bytes 110600 | tf_op jit(solution)/shard_map/line_sum/ppermute | solution.py:334
  53.4 9.7 %collective-permute-start.10 = (bf16[256,384]{1,0:T(8,128)(2,1)S(1)}, bf16[256,384]{1,0:T(8,128)(2,1)S(1)}, u32[]{:S(2)}, u32[]{:S(2)}) collective-permute-start(bf16[256,384]{1,0:T(8,128)(2,1)S(1)} %get-tuple-element.52), channel_id=1, source_target_pairs={{16,32},{32,16},{48,64},{64,48},{80,96},{96,80},{112,128},{128,112... | collective-permute-start | bytes 589832 | tf_op jit(solution)/shard_map/line_sum/ppermute | solution.py:36
  57.5 5.6 %collective-permute-start.9 = (bf16[48,384]{1,0:T(8,128)(2,1)S(1)}, bf16[48,384]{1,0:T(8,128)(2,1)S(1)}, u32[]{:S(2)}, u32[]{:S(2)}) collective-permute-start(bf16[48,384]{1,0:T(8,128)(2,1)S(1)} %add_convert_fusion.3), channel_id=1, source_target_pairs={{0,32},{1,33},{2,34},{3,35},{4,36},{5,37},{6,38},{7,39},{8,40},{9,... | collective-permute-start | bytes 110600 | tf_op jit(solution)/shard_map/line_sum/ppermute | solution.py:334
  63.1 5.6 %collective-permute-start.11 = (bf16[48,384]{1,0:T(8,128)(2,1)S(1)}, bf16[48,384]{1,0:T(8,128)(2,1)S(1)}, u32[]{:S(2)}, u32[]{:S(2)}) collective-permute-start(bf16[48,384]{1,0:T(8,128)(2,1)S(1)} %add_convert_fusion.2), channel_id=1, source_target_pairs={{0,112},{1,113},{2,114},{3,115},{4,116},{5,117},{6,118},{7,119},{8... | collective-permute-start | bytes 110600 | tf_op jit(solution)/shard_map/line_sum/ppermute | solution.py:334
  69.5 16.0 %all-to-all-start.1 = ((bf16[16,48,384]{2,1,0:T(8,128)(2,1)}), bf16[16,48,384]{2,1,0:T(8,128)(2,1)S(1)}, u32[]{:S(2)}, u32[]{:S(2)}) async-start(bf16[16,48,384]{2,1,0:T(8,128)(2,1)} %broadcast_in_dim.3), calls=%async_computation.1 | async-start | bytes 1179648 | tf_op jit(solution)/shard_map/plane_gather/all_to_all | solution.py:338
  76.3 4.2 %collective-permute-start.12 = (bf16[128,384]{1,0:T(8,128)(2,1)S(1)}, bf16[128,384]{1,0:T(8,128)(2,1)S(1)}, u32[]{:S(2)}, u32[]{:S(2)}) collective-permute-start(bf16[128,384]{1,0:T(8,128)(2,1)S(1)} %get-tuple-element.56), channel_id=1, source_target_pairs={{0,1},{1,0},{2,3},{3,2},{4,5},{5,4},{6,7},{7,6},{8,9},{9,8},{10,11... | collective-permute-start | bytes 294920 | tf_op jit(solution)/shard_map/plane_gather/ppermute | solution.py:36
  76.4 9.2 %collective-permute-start.13 = (bf16[128,384]{1,0:T(8,128)(2,1)S(1)}, bf16[128,384]{1,0:T(8,128)(2,1)S(1)}, u32[]{:S(2)}, u32[]{:S(2)}) collective-permute-start(bf16[128,384]{1,0:T(8,128)(2,1)S(1)} %get-tuple-element.57), channel_id=1, source_target_pairs={{1,2},{2,1},{3,4},{4,3},{5,6},{6,5},{7,8},{8,7},{9,10},{10,9},{11,... | collective-permute-start | bytes 294920 | tf_op jit(solution)/shard_map/plane_gather/ppermute | solution.py:36
  85.6 2.0 %collective-permute-start.14 = (bf16[768,384]{1,0:T(8,128)(2,1)S(1)}, bf16[768,384]{1,0:T(8,128)(2,1)S(1)}, u32[]{:S(2)}, u32[]{:S(2)}) collective-permute-start(bf16[768,384]{1,0:T(8,128)(2,1)S(1)} %bitcast.15), channel_id=1, source_target_pairs={{0,1},{1,0},{2,3},{3,2},{4,5},{5,4},{6,7},{7,6},{8,9},{9,8},{10,11... | collective-permute-start | bytes 1769480 | tf_op jit(solution)/shard_map/core_gather/ppermute | solution.py:36

commit v5 on v4

--- a/solution.py
+++ b/solution.py
@@ -107,10 +107,10 @@
 
 
 def attention_kernel(
-    place, tiles, query, grad_att, own_key, own_value, col_0, col_1, row_0, row_1, corner_0, corner_1,
-    w_key, w_value,
-    padded, key_grad, value_grad, attended, grad_q,
-    key, value, key_total, value_total, halo,
+    place, tiles, flat_grad, query, grad_att, own_key, own_value,
+    col_0, col_1, row_0, row_1, corner_0, corner_1, w_key, w_value,
+    keep, give, key_grad, value_grad, grad_q,
+    padded, attended, key, value, key_total, value_total, halo,
 ):
     row_at, row_last, col_at, col_last = place[0], place[1], place[2], place[3]
     row_even, col_even = lax.rem(row_at, 2) == 0, lax.rem(col_at, 2) == 0
@@ -215,34 +215,28 @@
     key_grad[...] = key_total[...].astype(HALF)
     value_grad[...] = value_total[...].astype(HALF)
 
+    both = jnp.concatenate([value_grad[...], key_grad[...]], axis=1)
+    both = dot(padded[...], both, TN)
+    grad_output = dot(attended[...], flat_grad[...], TN)
+    grad_query = dot(tiles[...], grad_q[...], TN)
+    halves = ((grad_output, grad_query), (both[:, :FEATURE], both[:, FEATURE:]))
+    for n, (zero, one) in enumerate(halves):
+        keep[n * FEATURE : (n + 1) * FEATURE, :] = jnp.where(col_even, zero, one).astype(HALF)
+        give[n * FEATURE : (n + 1) * FEATURE, :] = jnp.where(col_even, one, zero).astype(HALF)
+
 
 attention = local_call(
     attention_kernel,
-    [((ALL, FEATURE), HALF)] * 3
-    + [((OWN, FEATURE), HALF)] * 2,
-    [((ALL, FEATURE), HALF)] * 2 + [((ALL, FEATURE), FULL)] * 2 + [((12 * AREA, FEATURE), HALF)],
+    [((2 * FEATURE, FEATURE), HALF)] * 2
+    + [((ALL, FEATURE), HALF)] * 2
+    + [((OWN, FEATURE), HALF)],
+    [((ALL, FEATURE), HALF), ((OWN, FEATURE), HALF)]
+    + [((ALL, FEATURE), HALF)] * 2
+    + [((ALL, FEATURE), FULL)] * 2
+    + [((12 * AREA, FEATURE), HALF)],
     24,
-    6,
+    8,
     "attention",
-)
-
-
-def weights_kernel(
-    place, padded, key_grad, value_grad, tiles, flat_grad, attended, grad_q, keep, give,
-):
-    even = lax.rem(place[2], 2) == 0
-    tokens_all = padded[...]
-    grad_output = dot(attended[...], flat_grad[...], TN)
-    grad_value = dot(tokens_all, value_grad[...], TN)
-    grad_query = dot(tiles[...], grad_q[...], TN)
-    grad_key = dot(tokens_all, key_grad[...], TN)
-    for n, (zero, one) in enumerate(((grad_output, grad_query), (grad_value, grad_key))):
-        keep[n * FEATURE : (n + 1) * FEATURE, :] = jnp.where(even, zero, one).astype(HALF)
-        give[n * FEATURE : (n + 1) * FEATURE, :] = jnp.where(even, one, zero).astype(HALF)
-
-
-weight_grads = local_call(
-    weights_kernel, [((2 * FEATURE, FEATURE), HALF)] * 2, [], 16, 2, "weight_grads"
 )
 
 
@@ -362,11 +356,8 @@
     tiles, flat_grad, query, grad_att, key, value = own_projections(
         place, tokens, grad_out, w_query, w_key, w_value, w_out
     )
-    padded, key_grad, value_grad, attended, grad_q = attention(
-        place, tiles, query, grad_att, key, value, *halo, w_key, w_value
-    )
-    keep, give = weight_grads(
-        place, padded, key_grad, value_grad, tiles, flat_grad, attended, grad_q
+    keep, give, key_grad, value_grad, grad_q = attention(
+        place, tiles, flat_grad, query, grad_att, key, value, *halo, w_key, w_value
     )
     own, send_0, send_1 = spread_grads(
         place, key_grad, value_grad, grad_q, w_query, w_key, w_value
@@ -381,7 +372,7 @@
     with jax.named_scope("line_sum"):
         for n, step in enumerate(LINE_STEPS):
             other = cross(part, step)
-            if n == 1:
+            if n == 2:
                 other, from_2 = tied((other, swap(send_1, "row", 1)))
             part = (part.astype(FULL) + other.astype(FULL)).astype(HALF)
     summed, send_0, send_1 = add_rows(place, own, from_0, from_2)

time: 90.5 us -> 88.9 us (0.982)
  waiting for transfers between devices: 26.9 us -> 24.2 us
  starting transfers between devices: 41.8 us -> 43.9 us
  Pallas kernels: 13.8 us -> 12.8 us
    ppermute x12, waiting for transfers between devices: 19.8 us -> 17.8 us  [swap(): return lax.ppermute(block, axis, swap_pairs(lax.axis_size(axis), kind))]
    ppermute x3, starting transfers between devices: 3.16 us -> 4.52 us  [cross(): lax.ppermute(block, BOTH, [(i, i ^ step) for i in range(lax.axis_size(BOT...]
    pallas_call x6 -> x5, Pallas kernels: 13.8 us -> 12.8 us  [call(): pl.pallas_call(kernel, out_shape=tuple((jax.ShapeDtypeStruct(*out) for ou...]
  transfers between devices with their start and end apart: 17 -> 17, of which waited for: 8 -> 10; matrix products, arithmetic and copies ran while one was open for 1% -> 1% of each run, Pallas kernels for 6% -> 6%
where the time goes in v5:
time: 88.9 us; the launch traced here: 87.7 us
  starting transfers between devices  43.9 us (49%)
  waiting for transfers between devices  24.2 us (27%)
  Pallas kernels  12.8 us (14%)
  other arithmetic  3.6 us (4%)
  local copies, waits for them, and re-layouts  2.33 us (3%)
  between operations  0.89 us (1%)
    ppermute x12, starting transfers between devices, swap(): return lax.ppermute(block, axis, swap_pairs(lax.axis_size(axis), kind))  26.5 us
    ppermute x12, waiting for transfers between devices, swap(): return lax.ppermute(block, axis, swap_pairs(lax.axis_size(axis), kind))  17.8 us
    all_to_all x2, starting transfers between devices, exchange(): lax.all_to_all(pieces, BOTH, 0, 0, tiled=True, axis_index_groups=groups)  12.9 us
    pallas_call x5, Pallas kernels, call(): pl.pallas_call(kernel, out_shape=tuple((jax.ShapeDtypeStruct(*out) for ou...  12.8 us
    ppermute x3, starting transfers between devices, cross(): lax.ppermute(block, BOTH, [(i, i ^ step) for i in range(lax.axis_size(BOT...  4.52 us
    ppermute x3, waiting for transfers between devices, cross(): lax.ppermute(block, BOTH, [(i, i ^ step) for i in range(lax.axis_size(BOT...  3.26 us
    all_to_all x2, waiting for transfers between devices, exchange(): lax.all_to_all(pieces, BOTH, 0, 0, tiled=True, axis_index_groups=groups)  3.14 us
    select_n x4, other arithmetic, by_side(): return (jnp.where(odd, first, second), jnp.where(odd, second, first))  2.11 us
  transfers between devices with their start and end apart: 17, of which 10 were waited for; matrix products, arithmetic and copies ran while one was open for 1% of the time, Pallas kernels for 6%

profile of v5, /device:TPU:10, one launch (start us, length us, event | category | flops | bytes accessed | tf_op | source)
XLA Modules:
  0.0 87.7 jit_solution(7289540899626412585)
XLA Ops:
  0.7 1.1 %broadcast_select_fusion.6 = (bf16[16,8,384]{2,1,0:T(8,128)(2,1)S(1)}, bf16[16,8,384]{2,1,0:T(8,128)(2,1)S(1)}) fusion(pred[]{:T(512)S(6)} %eq.12, bf16[16,16,384]{2,1,0:T(8,128)(2,1)} %tokens.1), kind=kLoop, calls=%fused_computation.13 | loop fusion | flops 98304 | bytes 393217 | tf_op jit(solution)/shard_map/halo/jit(_where)/select_n | solution.py:41
  1.8 3.4 %collective-permute-start.1 = (bf16[16,8,384]{2,1,0:T(8,128)(2,1)S(1)}, bf16[16,8,384]{2,1,0:T(8,128)(2,1)S(1)}, u32[]{:S(2)}, u32[]{:S(2)}) collective-permute-start(bf16[16,8,384]{2,1,0:T(8,128)(2,1)S(1)} %get-tuple-element.69), channel_id=1, source_target_pairs={{1,2},{2,1},{3,4},{4,3},{5,6},{6,5},{7,8},{8,7},{9,10},{10,9},{11,... | collective-permute-start | bytes 294920 | tf_op jit(solution)/shard_map/halo/ppermute | solution.py:36
  7.0 8.6 %collective-permute-start.3 = (bf16[8,16,384]{2,1,0:T(8,128)(2,1)S(1)}, bf16[8,16,384]{2,1,0:T(8,128)(2,1)S(1)}, u32[]{:S(2)}, u32[]{:S(2)}) collective-permute-start(bf16[8,16,384]{2,1,0:T(8,128)(2,1)S(1)} %get-tuple-element.67), channel_id=1, source_target_pairs={{16,32},{32,16},{48,64},{64,48},{80,96},{96,80},{112,128},{128,112... | collective-permute-start | bytes 294920 | tf_op jit(solution)/shard_map/halo/ppermute | solution.py:36
  15.8 3.9 %collective-permute-start.5 = (bf16[8,16,384]{2,1,0:T(8,128)(2,1)S(1)}, bf16[8,16,384]{2,1,0:T(8,128)(2,1)S(1)}, u32[]{:S(2)}, u32[]{:S(2)}) collective-permute-start(bf16[8,16,384]{2,1,0:T(8,128)(2,1)S(1)} %get-tuple-element.63), channel_id=1, source_target_pairs={{16,32},{32,16},{48,64},{64,48},{80,96},{96,80},{112,128},{128,112... | collective-permute-start | bytes 294920 | tf_op jit(solution)/shard_map/halo/ppermute | solution.py:36
  20.1 1.2 %own_projections.1 = (bf16[256,384]{1,0:T(8,128)(2,1)S(1)}, bf16[256,384]{1,0:T(8,128)(2,1)S(1)}, bf16[256,384]{1,0:T(8,128)(2,1)S(1)}, bf16[256,384]{1,0:T(8,12...) custom-call(s32[4]{0:T(128)S(1)} %pad_add_fusion.place, bf16[16,16,384]{2,1,0:T(8,128)(2,1)S(1)} %copy-done, ...), custom_call_target="tpu_custom_call" | custom-call | flops 1000000000 | bytes 1000000 | tf_op jit(solution)/shard_map/own_projections/pallas_call | solution.py:67
  21.3 3.2 %collective-permute-done.5.corner_1 = bf16[8,16,384]{2,1,0:T(8,128)(2,1)S(1)} collective-permute-done((bf16[8,16,384]{2,1,0:T(8,128)(2,1)S(1)}, bf16[8,16,384]{2,1,0:T(8,128)(2,1)S(1)}, u32[]{:S(2)}, u32[]{:S(2)}) %collective-permute-start.5) | collective-permute-done | bytes 98336 | tf_op jit(solution)/shard_map/halo/ppermute | solution.py:36
  24.5 7.8 %attention.1 = (bf16[768,384]{1,0:T(8,128)(2,1)S(1)}, bf16[768,384]{1,0:T(8,128)(2,1)S(1)}, bf16[1024,384]{1,0:T(8,128)(2,1)S(1)}, bf16[1024,384]{1,0:T(8,128)(2,1)S(1)}, bf16[256,384]{1,0:T(8,128)(2,1)S(1)}) custom-call(s32[4]{0:T(128)S(1)} %pad_add_fusion.place, bf16[256,384]{1,0:T(8,128)(2,1)S(1)} %get-tuple-element.31.tiles, ...), custom_call_target="tpu_custom_call" | custom-call | flops 8000000000 | bytes 8000000 | tf_op jit(solution)/shard_map/attention/pallas_call | solution.py:67
  32.4 1.8 %spread_grads.1 = (f32[512,384]{1,0:T(8,128)S(1)}, bf16[256,384]{1,0:T(8,128)(2,1)S(1)}, bf16[256,384]{1,0:T(8,128)(2,1)S(1)}) custom-call(s32[4]{0:T(128)S(1)} %pad_add_fusion.place, bf16[1024,384]{1,0:T(8,128)(2,1)S(1)} %get-tuple-element.38.key_grad, bf16[1024,384]{1,0:T(8,128)(2,1)S(1)} %get-tuple-element.39.value_grad, ...), custom_call_target="tpu_custom_call" | custom-call | flops 1000000000 | bytes 1000000 | tf_op jit(solution)/shard_map/spread_grads/pallas_call | solution.py:67
  34.4 1.0 %add_convert_fusion = bf16[768,384]{1,0:T(8,128)(2,1)} fusion(bf16[768,384]{1,0:T(8,128)(2,1)S(1)} %collective-permute-done.6, bf16[768,384]{1,0:T(8,128)(2,1)S(1)} %get-tuple-element.43), kind=kLoop, calls=%fused_computation | loop fusion | flops 1179648 | bytes 1769472 | tf_op jit(solution)/shard_map/core_sum/convert_element_type | solution.py:367
  35.4 6.1 %all-to-all-start = ((bf16[16,48,384]{2,1,0:T(8,128)(2,1)}), bf16[16,48,384]{2,1,0:T(8,128)(2,1)S(1)}, u32[]{:S(2)}, u32[]{:S(2)}) async-start(bf16[16,48,384]{2,1,0:T(8,128)(2,1)} %bitcast.2), calls=%async_computation | async-start | bytes 1179648 | tf_op jit(solution)/shard_map/plane_sum/all_to_all | solution.py:332
  41.5 1.1 %collective-permute-start.7 = (bf16[256,384]{1,0:T(8,128)(2,1)S(1)}, bf16[256,384]{1,0:T(8,128)(2,1)S(1)}, u32[]{:S(2)}, u32[]{:S(2)}) collective-permute-start(bf16[256,384]{1,0:T(8,128)(2,1)S(1)} %get-tuple-element.45), channel_id=1, source_target_pairs={{0,16},{16,0},{32,48},{48,32},{64,80},{80,64},{96,112},{112,96},{1... | collective-permute-start | bytes 589832 | tf_op jit(solution)/shard_map/plane_sum/ppermute | solution.py:36
  42.6 5.4 %collective-permute-done.7.from_0 = bf16[256,384]{1,0:T(8,128)(2,1)S(1)} collective-permute-done((bf16[256,384]{1,0:T(8,128)(2,1)S(1)}, bf16[256,384]{1,0:T(8,128)(2,1)S(1)}, u32[]{:S(2)}, u32[]{:S(2)}) %collective-permute-start.7) | collective-permute-done | bytes 196640 | tf_op jit(solution)/shard_map/plane_sum/ppermute | solution.py:36
  48.0 3.1 %all-to-all-done = bf16[16,48,384]{2,1,0:T(8,128)(2,1)S(1)} async-done(((bf16[16,48,384]{2,1,0:T(8,128)(2,1)}), bf16[16,48,384]{2,1,0:T(8,128)(2,1)S(1)}, u32[]{:S(2)}, u32[]{:S(2)}) %all-to-all-start) | async-done | bytes 589856 | tf_op jit(solution)/shard_map/plane_sum/all_to_all | solution.py:332
  51.2 1.2 %collective-permute-start.8 = (bf16[48,384]{1,0:T(8,128)(2,1)S(1)}, bf16[48,384]{1,0:T(8,128)(2,1)S(1)}, u32[]{:S(2)}, u32[]{:S(2)}) collective-permute-start(bf16[48,384]{1,0:T(8,128)(2,1)S(1)} %fusion.1), channel_id=1, source_target_pairs={{0,16},{1,17},{2,18},{3,19},{4,20},{5,21},{6,22},{7,23},{8,24},{9,... | collective-permute-start | bytes 110600 | tf_op jit(solution)/shard_map/line_sum/ppermute | solution.py:328
  52.5 2.8 %collective-permute-done.8 = bf16[48,384]{1,0:T(8,128)(2,1)S(1)} collective-permute-done((bf16[48,384]{1,0:T(8,128)(2,1)S(1)}, bf16[48,384]{1,0:T(8,128)(2,1)S(1)}, u32[]{:S(2)}, u32[]{:S(2)}) %collective-permute-start.8) | collective-permute-done | bytes 36896 | tf_op jit(solution)/shard_map/line_sum/ppermute | solution.py:328
  55.4 1.3 %collective-permute-start.9 = (bf16[48,384]{1,0:T(8,128)(2,1)S(1)}, bf16[48,384]{1,0:T(8,128)(2,1)S(1)}, u32[]{:S(2)}, u32[]{:S(2)}) collective-permute-start(bf16[48,384]{1,0:T(8,128)(2,1)S(1)} %add_convert_fusion.3), channel_id=1, source_target_pairs={{0,32},{1,33},{2,34},{3,35},{4,36},{5,37},{6,38},{7,39},{8,40},{9,... | collective-permute-start | bytes 110600 | tf_op jit(solution)/shard_map/line_sum/ppermute | solution.py:328
  56.7 4.1 %collective-permute-start.11 = (bf16[256,384]{1,0:T(8,128)(2,1)S(1)}, bf16[256,384]{1,0:T(8,128)(2,1)S(1)}, u32[]{:S(2)}, u32[]{:S(2)}) collective-permute-start(bf16[256,384]{1,0:T(8,128)(2,1)S(1)} %get-tuple-element.48), channel_id=1, source_target_pairs={{16,32},{32,16},{48,64},{64,48},{80,96},{96,80},{112,128},{128,112... | collective-permute-start | bytes 589832 | tf_op jit(solution)/shard_map/line_sum/ppermute | solution.py:36
  61.1 2.0 %collective-permute-start.10 = (bf16[48,384]{1,0:T(8,128)(2,1)S(1)}, bf16[48,384]{1,0:T(8,128)(2,1)S(1)}, u32[]{:S(2)}, u32[]{:S(2)}) collective-permute-start(bf16[48,384]{1,0:T(8,128)(2,1)S(1)} %add_convert_fusion.2), channel_id=1, source_target_pairs={{0,112},{1,113},{2,114},{3,115},{4,116},{5,117},{6,118},{7,119},{8... | collective-permute-start | bytes 110600 | tf_op jit(solution)/shard_map/line_sum/ppermute | solution.py:328
  63.2 3.2 %collective-permute-done.11.from_1 = bf16[256,384]{1,0:T(8,128)(2,1)S(1)} collective-permute-done((bf16[256,384]{1,0:T(8,128)(2,1)S(1)}, bf16[256,384]{1,0:T(8,128)(2,1)S(1)}, u32[]{:S(2)}, u32[]{:S(2)}) %collective-permute-start.11) | collective-permute-done | bytes 196640 | tf_op jit(solution)/shard_map/line_sum/ppermute | solution.py:36
  67.3 6.8 %all-to-all-start.1 = ((bf16[16,48,384]{2,1,0:T(8,128)(2,1)}), bf16[16,48,384]{2,1,0:T(8,128)(2,1)S(1)}, u32[]{:S(2)}, u32[]{:S(2)}) async-start(bf16[16,48,384]{2,1,0:T(8,128)(2,1)} %broadcast_in_dim.3), calls=%async_computation.1 | async-start | bytes 1179648 | tf_op jit(solution)/shard_map/plane_gather/all_to_all | solution.py:332
  74.8 4.1 %collective-permute-start.13 = (bf16[128,384]{1,0:T(8,128)(2,1)S(1)}, bf16[128,384]{1,0:T(8,128)(2,1)S(1)}, u32[]{:S(2)}, u32[]{:S(2)}) collective-permute-start(bf16[128,384]{1,0:T(8,128)(2,1)S(1)} %get-tuple-element.53), channel_id=1, source_target_pairs={{1,2},{2,1},{3,4},{4,3},{5,6},{6,5},{7,8},{8,7},{9,10},{10,9},{11,... | collective-permute-start | bytes 294920 | tf_op jit(solution)/shard_map/plane_gather/ppermute | solution.py:36
  78.9 5.1 %collective-permute-done.13.from_1 = bf16[128,384]{1,0:T(8,128)(2,1)S(1)} collective-permute-done((bf16[128,384]{1,0:T(8,128)(2,1)S(1)}, bf16[128,384]{1,0:T(8,128)(2,1)S(1)}, u32[]{:S(2)}, u32[]{:S(2)}) %collective-permute-start.13) | collective-permute-done | bytes 98336 | tf_op jit(solution)/shard_map/plane_gather/ppermute | solution.py:36
  84.0 1.3 %add_columns.1 = bf16[16,16,384]{2,1,0:T(8,128)(2,1)} custom-call(s32[4]{0:T(128)S(1)} %pad_add_fusion.place, f32[256,384]{1,0:T(8,128)S(1)} %get-tuple-element.50.summed, bf16[128,384]{1,0:T(8,128)(2,1)S(1)} %collective-permute-done.12.from_0, bf16[128,384]{1,0:T(8,128)(2,1)S(1)} %collective-permute-done.13.from_1), custom_call_target="tpu_custom_call" | custom-call | flops 1000000000 | bytes 1000000 | tf_op jit(solution)/shard_map/add_columns/pallas_call | solution.py:67
  86.2 1.4 %fusion.2 = (f32[384,384]{1,0:T(8,128)}, f32[384,384]{1,0:T(8,128)}, f32[384,384]{1,0:T(8,128)}, f32[384,384]{1,0:T(8,128)}) fusion(f32[768,384]{1,0:T(8,128)S(1)} %get-tuple-element.59, f32[768,384]{1,0:T(8,128)S(1)} %get-tuple-element.60), kind=kLoop, calls=%fused_computation.21 | loop fusion | bytes 4718592 | tf_op jit(solution)/shard_map/slice | solution.py:389
  (40 shorter events, 5.9 us)
Async XLA Ops:
  0.6 19.4 %copy-start = (bf16[16,16,384]{2,1,0:T(8,128)(2,1)S(1)}, bf16[16,16,384]{2,1,0:T(8,128)(2,1)}, u32[]{:S(2)}) copy-start(bf16[16,16,384]{2,1,0:T(8,128)(2,1)} %tokens.1) | copy-start | bytes 589828
  0.6 19.4 %copy-start.4 = (bf16[384,384]{1,0:T(8,128)(2,1)S(1)}, bf16[384,384]{1,0:T(8,128)(2,1)}, u32[]{:S(2)}) copy-start(bf16[384,384]{1,0:T(8,128)(2,1)} %w_value.5) | copy-start | bytes 884740
  0.7 19.4 %copy-start.3 = (bf16[384,384]{1,0:T(8,128)(2,1)S(1)}, bf16[384,384]{1,0:T(8,128)(2,1)}, u32[]{:S(2)}) copy-start(bf16[384,384]{1,0:T(8,128)(2,1)} %w_key.5) | copy-start | bytes 884740
  0.7 19.4 %copy-start.2 = (bf16[384,384]{1,0:T(8,128)(2,1)S(1)}, bf16[384,384]{1,0:T(8,128)(2,1)}, u32[]{:S(2)}) copy-start(bf16[384,384]{1,0:T(8,128)(2,1)} %w_query.3) | copy-start | bytes 884740
  0.7 19.4 %copy-start.1 = (bf16[384,384]{1,0:T(8,128)(2,1)S(1)}, bf16[384,384]{1,0:T(8,128)(2,1)}, u32[]{:S(2)}) copy-start(bf16[384,384]{1,0:T(8,128)(2,1)} %w_out.1) | copy-start | bytes 884740
  0.7 19.4 %copy-start.5 = (bf16[16,16,384]{2,1,0:T(8,128)(2,1)S(1)}, bf16[16,16,384]{2,1,0:T(8,128)(2,1)}, u32[]{:S(2)}) copy-start(bf16[16,16,384]{2,1,0:T(8,128)(2,1)} %grad_out.1) | copy-start | bytes 589828
  1.8 14.0 %collective-permute-start.1 = (bf16[16,8,384]{2,1,0:T(8,128)(2,1)S(1)}, bf16[16,8,384]{2,1,0:T(8,128)(2,1)S(1)}, u32[]{:S(2)}, u32[]{:S(2)}) collective-permute-start(bf16[16,8,384]{2,1,0:T(8,128)(2,1)S(1)} %get-tuple-element.69), channel_id=1, source_target_pairs={{1,2},{2,1},{3,4},{4,3},{5,6},{6,5},{7,8},{8,7},{9,10},{10,9},{11,... | collective-permute-start | bytes 294920 | tf_op jit(solution)/shard_map/halo/ppermute | solution.py:36
  5.1 10.6 %collective-permute-start = (bf16[16,8,384]{2,1,0:T(8,128)(2,1)S(1)}, bf16[16,8,384]{2,1,0:T(8,128)(2,1)S(1)}, u32[]{:S(2)}, u32[]{:S(2)}) collective-permute-start(bf16[16,8,384]{2,1,0:T(8,128)(2,1)S(1)} %get-tuple-element.70), channel_id=1, source_target_pairs={{0,1},{1,0},{2,3},{3,2},{4,5},{5,4},{6,7},{7,6},{8,9},{9,8},{10,11... | collective-permute-start | bytes 294920 | tf_op jit(solution)/shard_map/halo/ppermute | solution.py:36
  7.0 14.3 %collective-permute-start.3 = (bf16[8,16,384]{2,1,0:T(8,128)(2,1)S(1)}, bf16[8,16,384]{2,1,0:T(8,128)(2,1)S(1)}, u32[]{:S(2)}, u32[]{:S(2)}) collective-permute-start(bf16[8,16,384]{2,1,0:T(8,128)(2,1)S(1)} %get-tuple-element.67), channel_id=1, source_target_pairs={{16,32},{32,16},{48,64},{64,48},{80,96},{96,80},{112,128},{128,112... | collective-permute-start | bytes 294920 | tf_op jit(solution)/shard_map/halo/ppermute | solution.py:36
  15.6 5.7 %collective-permute-start.2 = (bf16[8,16,384]{2,1,0:T(8,128)(2,1)S(1)}, bf16[8,16,384]{2,1,0:T(8,128)(2,1)S(1)}, u32[]{:S(2)}, u32[]{:S(2)}) collective-permute-start(bf16[8,16,384]{2,1,0:T(8,128)(2,1)S(1)} %get-tuple-element.68), channel_id=1, source_target_pairs={{0,16},{16,0},{32,48},{48,32},{64,80},{80,64},{96,112},{112,96},{1... | collective-permute-start | bytes 294920 | tf_op jit(solution)/shard_map/halo/ppermute | solution.py:36
  15.8 8.6 %collective-permute-start.5 = (bf16[8,16,384]{2,1,0:T(8,128)(2,1)S(1)}, bf16[8,16,384]{2,1,0:T(8,128)(2,1)S(1)}, u32[]{:S(2)}, u32[]{:S(2)}) collective-permute-start(bf16[8,16,384]{2,1,0:T(8,128)(2,1)S(1)} %get-tuple-element.63), channel_id=1, source_target_pairs={{16,32},{32,16},{48,64},{64,48},{80,96},{96,80},{112,128},{128,112... | collective-permute-start | bytes 294920 | tf_op jit(solution)/shard_map/halo/ppermute | solution.py:36
  19.7 4.7 %collective-permute-start.4 = (bf16[8,16,384]{2,1,0:T(8,128)(2,1)S(1)}, bf16[8,16,384]{2,1,0:T(8,128)(2,1)S(1)}, u32[]{:S(2)}, u32[]{:S(2)}) collective-permute-start(bf16[8,16,384]{2,1,0:T(8,128)(2,1)S(1)} %get-tuple-element.64), channel_id=1, source_target_pairs={{0,16},{16,0},{32,48},{48,32},{64,80},{80,64},{96,112},{112,96},{1... | collective-permute-start | bytes 294920 | tf_op jit(solution)/shard_map/halo/ppermute | solution.py:36
  32.3 2.1 %collective-permute-start.6 = (bf16[768,384]{1,0:T(8,128)(2,1)S(1)}, bf16[768,384]{1,0:T(8,128)(2,1)S(1)}, u32[]{:S(2)}, u32[]{:S(2)}) collective-permute-start(bf16[768,384]{1,0:T(8,128)(2,1)S(1)} %get-tuple-element.37), channel_id=1, source_target_pairs={{0,1},{1,0},{2,3},{3,2},{4,5},{5,4},{6,7},{7,6},{8,9},{9,8},{10,11... | collective-permute-start | bytes 1769480 | tf_op jit(solution)/shard_map/core_sum/ppermute | solution.py:36
  35.4 15.8 %all-to-all-start = ((bf16[16,48,384]{2,1,0:T(8,128)(2,1)}), bf16[16,48,384]{2,1,0:T(8,128)(2,1)S(1)}, u32[]{:S(2)}, u32[]{:S(2)}) async-start(bf16[16,48,384]{2,1,0:T(8,128)(2,1)} %bitcast.2), calls=%async_computation | async-start | bytes 1179648 | tf_op jit(solution)/shard_map/plane_sum/all_to_all | solution.py:332
  41.5 6.6 %collective-permute-start.7 = (bf16[256,384]{1,0:T(8,128)(2,1)S(1)}, bf16[256,384]{1,0:T(8,128)(2,1)S(1)}, u32[]{:S(2)}, u32[]{:S(2)}) collective-permute-start(bf16[256,384]{1,0:T(8,128)(2,1)S(1)} %get-tuple-element.45), channel_id=1, source_target_pairs={{0,16},{16,0},{32,48},{48,32},{64,80},{80,64},{96,112},{112,96},{1... | collective-permute-start | bytes 589832 | tf_op jit(solution)/shard_map/plane_sum/ppermute | solution.py:36
  51.2 4.0 %collective-permute-start.8 = (bf16[48,384]{1,0:T(8,128)(2,1)S(1)}, bf16[48,384]{1,0:T(8,128)(2,1)S(1)}, u32[]{:S(2)}, u32[]{:S(2)}) collective-permute-start(bf16[48,384]{1,0:T(8,128)(2,1)S(1)} %fusion.1), channel_id=1, source_target_pairs={{0,16},{1,17},{2,18},{3,19},{4,20},{5,21},{6,22},{7,23},{8,24},{9,... | collective-permute-start | bytes 110600 | tf_op jit(solution)/shard_map/line_sum/ppermute | solution.py:328
  55.4 5.7 %collective-permute-start.9 = (bf16[48,384]{1,0:T(8,128)(2,1)S(1)}, bf16[48,384]{1,0:T(8,128)(2,1)S(1)}, u32[]{:S(2)}, u32[]{:S(2)}) collective-permute-start(bf16[48,384]{1,0:T(8,128)(2,1)S(1)} %add_convert_fusion.3), channel_id=1, source_target_pairs={{0,32},{1,33},{2,34},{3,35},{4,36},{5,37},{6,38},{7,39},{8,40},{9,... | collective-permute-start | bytes 110600 | tf_op jit(solution)/shard_map/line_sum/ppermute | solution.py:328
  56.7 9.7 %collective-permute-start.11 = (bf16[256,384]{1,0:T(8,128)(2,1)S(1)}, bf16[256,384]{1,0:T(8,128)(2,1)S(1)}, u32[]{:S(2)}, u32[]{:S(2)}) collective-permute-start(bf16[256,384]{1,0:T(8,128)(2,1)S(1)} %get-tuple-element.48), channel_id=1, source_target_pairs={{16,32},{32,16},{48,64},{64,48},{80,96},{96,80},{112,128},{128,112... | collective-permute-start | bytes 589832 | tf_op jit(solution)/shard_map/line_sum/ppermute | solution.py:36
  61.1 5.3 %collective-permute-start.10 = (bf16[48,384]{1,0:T(8,128)(2,1)S(1)}, bf16[48,384]{1,0:T(8,128)(2,1)S(1)}, u32[]{:S(2)}, u32[]{:S(2)}) collective-permute-start(bf16[48,384]{1,0:T(8,128)(2,1)S(1)} %add_convert_fusion.2), channel_id=1, source_target_pairs={{0,112},{1,113},{2,114},{3,115},{4,116},{5,117},{6,118},{7,119},{8... | collective-permute-start | bytes 110600 | tf_op jit(solution)/shard_map/line_sum/ppermute | solution.py:328
  67.3 16.7 %all-to-all-start.1 = ((bf16[16,48,384]{2,1,0:T(8,128)(2,1)}), bf16[16,48,384]{2,1,0:T(8,128)(2,1)S(1)}, u32[]{:S(2)}, u32[]{:S(2)}) async-start(bf16[16,48,384]{2,1,0:T(8,128)(2,1)} %broadcast_in_dim.3), calls=%async_computation.1 | async-start | bytes 1179648 | tf_op jit(solution)/shard_map/plane_gather/all_to_all | solution.py:332
  74.7 4.2 %collective-permute-start.12 = (bf16[128,384]{1,0:T(8,128)(2,1)S(1)}, bf16[128,384]{1,0:T(8,128)(2,1)S(1)}, u32[]{:S(2)}, u32[]{:S(2)}) collective-permute-start(bf16[128,384]{1,0:T(8,128)(2,1)S(1)} %get-tuple-element.52), channel_id=1, source_target_pairs={{0,1},{1,0},{2,3},{3,2},{4,5},{5,4},{6,7},{7,6},{8,9},{9,8},{10,11... | collective-permute-start | bytes 294920 | tf_op jit(solution)/shard_map/plane_gather/ppermute | solution.py:36
  74.8 9.2 %collective-permute-start.13 = (bf16[128,384]{1,0:T(8,128)(2,1)S(1)}, bf16[128,384]{1,0:T(8,128)(2,1)S(1)}, u32[]{:S(2)}, u32[]{:S(2)}) collective-permute-start(bf16[128,384]{1,0:T(8,128)(2,1)S(1)} %get-tuple-element.53), channel_id=1, source_target_pairs={{1,2},{2,1},{3,4},{4,3},{5,6},{6,5},{7,8},{8,7},{9,10},{10,9},{11,... | collective-permute-start | bytes 294920 | tf_op jit(solution)/shard_map/plane_gather/ppermute | solution.py:36
  84.0 2.0 %collective-permute-start.14 = (bf16[768,384]{1,0:T(8,128)(2,1)S(1)}, bf16[768,384]{1,0:T(8,128)(2,1)S(1)}, u32[]{:S(2)}, u32[]{:S(2)}) collective-permute-start(bf16[768,384]{1,0:T(8,128)(2,1)S(1)} %bitcast.15), channel_id=1, source_target_pairs={{0,1},{1,0},{2,3},{3,2},{4,5},{5,4},{6,7},{7,6},{8,9},{9,8},{10,11... | collective-permute-start | bytes 1769480 | tf_op jit(solution)/shard_map/core_gather/ppermute | solution.py:36

commit v6 on v5

--- a/solution.py
+++ b/solution.py
@@ -106,27 +106,50 @@
 own_projections = local_call(own_kernel, [((OWN, FEATURE), HALF)] * 6, [], 8, 1, "own_projections")
 
 
+EDGES = ((0, 1), (0, 2), (1, 0), (1, 3), (2, 0), (2, 3), (3, 1), (3, 2))
+
+
+def by_parity(even, first, second):
+    a, b = first[...].astype(FULL), second[...].astype(FULL)
+    return jnp.where(even, b, a), jnp.where(even, a, b)
+
+
+def edge_kernel(place, col_0, col_1, row_0, row_1, w_key, w_value, tiles, key, value):
+    west, east = by_parity(lax.rem(place[2], 2) == 0, col_0, col_1)
+    north, south = by_parity(lax.rem(place[0], 2) == 0, row_0, row_1)
+    parts = (
+        (north, 0, 0), (north, 0, 1), (west, 0, 0), (east, 0, 0),
+        (west, 1, 0), (east, 1, 0), (south, 0, 0), (south, 0, 1),
+    )
+    for n, part in enumerate(parts):
+        tiles[n * AREA : (n + 1) * AREA, :] = tile_of(*part)
+    key[...] = dot(tiles[...], w_key[...]).astype(HALF)
+    value[...] = dot(tiles[...], w_value[...]).astype(HALF)
+
+
+edge_projections = local_call(
+    edge_kernel, [((8 * AREA, FEATURE), HALF)] * 3, [], 8, 1, "edge_projections"
+)
+
+
 def attention_kernel(
     place, tiles, flat_grad, query, grad_att, own_key, own_value,
-    col_0, col_1, row_0, row_1, corner_0, corner_1, w_key, w_value,
+    edge_tiles, edge_key, edge_value, corner_0, corner_1, w_key, w_value,
     keep, give, key_grad, value_grad, grad_q,
     padded, attended, key, value, key_total, value_total, halo,
 ):
     row_at, row_last, col_at, col_last = place[0], place[1], place[2], place[3]
     row_even, col_even = lax.rem(row_at, 2) == 0, lax.rem(col_at, 2) == 0
 
-    def sides(even, first, second):
-        a, b = first[...].astype(FULL), second[...].astype(FULL)
-        return jnp.where(even, b, a), jnp.where(even, a, b)
-
-    west, east = sides(col_even, col_0, col_1)
-    north, south = sides(row_even, row_0, row_1)
-    above, below = sides(row_even, corner_0, corner_1)
+    above, below = by_parity(row_even, corner_0, corner_1)
     outside = {
-        (0, 0): (above, 0, 0), (0, 1): (north, 0, 0), (0, 2): (north, 0, 1), (0, 3): (above, 0, 1),
-        (1, 0): (west, 0, 0), (1, 3): (east, 0, 0), (2, 0): (west, 1, 0), (2, 3): (east, 1, 0),
-        (3, 0): (below, 0, 0), (3, 1): (south, 0, 0), (3, 2): (south, 0, 1), (3, 3): (below, 0, 1),
+        (0, 0): (above, 0, 0), (0, 3): (above, 0, 1), (3, 0): (below, 0, 0), (3, 3): (below, 0, 1)
     }
+    for n, (i, j) in enumerate(EDGES):
+        at, mine = (i * 4 + j) * AREA, slice(n * AREA, (n + 1) * AREA)
+        padded[at : at + AREA, :] = edge_tiles[mine, :]
+        key[at : at + AREA, :] = edge_key[mine, :]
+        value[at : at + AREA, :] = edge_value[mine, :]
     for n, (i, j) in enumerate(outside):
         tile = tile_of(*outside[i, j])
         padded[(i * 4 + j) * AREA : (i * 4 + j + 1) * AREA, :] = tile
@@ -233,7 +256,7 @@
     [((ALL, FEATURE), HALF), ((OWN, FEATURE), HALF)]
     + [((ALL, FEATURE), HALF)] * 2
     + [((ALL, FEATURE), FULL)] * 2
-    + [((12 * AREA, FEATURE), HALF)],
+    + [((4 * AREA, FEATURE), HALF)],
     24,
     8,
     "attention",
@@ -356,8 +379,9 @@
     tiles, flat_grad, query, grad_att, key, value = own_projections(
         place, tokens, grad_out, w_query, w_key, w_value, w_out
     )
+    edges = edge_projections(place, *halo[:4], w_key, w_value)
     keep, give, key_grad, value_grad, grad_q = attention(
-        place, tiles, flat_grad, query, grad_att, key, value, *halo, w_key, w_value
+        place, tiles, flat_grad, query, grad_att, key, value, *edges, *halo[4:], w_key, w_value
     )
     own, send_0, send_1 = spread_grads(
         place, key_grad, value_grad, grad_q, w_query, w_key, w_value
@@ -384,10 +408,11 @@
     (grad_tokens,) = add_columns(place, summed, from_0, from_1)
     with jax.named_scope("core_gather"):
         other = swap(part, "col", 0)
-        first = jnp.where(core == 0, part, other).astype(FULL)
-        second = jnp.where(core == 0, other, part).astype(FULL)
-    grad_output, grad_value = first[:FEATURE], first[FEATURE:]
-    grad_query, grad_key = second[:FEATURE], second[FEATURE:]
+        top, bottom = slice(0, FEATURE), slice(FEATURE, 2 * FEATURE)
+        grad_output, grad_value, grad_query, grad_key = (
+            jnp.where(core == which, part[half], other[half]).astype(FULL)
+            for which, half in ((0, top), (0, bottom), (1, top), (1, bottom))
+        )
     return grad_tokens, grad_query, grad_key, grad_value, grad_output
 
 

time: 88.9 us -> 88.3 us (level)
  waiting for transfers between devices: 24.2 us -> 22.4 us
  local copies, waits for them, and re-layouts: 2.33 us -> 0.95 us
  other arithmetic: 3.6 us -> 4.88 us
    slice x1, local copies, waits for them, and re-layouts: 1.44 us -> 0.06 us  [per_device(): part[half]]
    convert_element_type x1, other arithmetic: 0.23 us -> 1.5 us  [per_device(): jnp.where(core == which, part[half], other[half]).astype(FULL)]
    ppermute x12, waiting for transfers between devices: 17.8 us -> 16.5 us  [swap(): return lax.ppermute(block, axis, swap_pairs(lax.axis_size(axis), kind))]
    pallas_call x5 -> x6, Pallas kernels: 12.8 us -> 13.5 us  [call(): pl.pallas_call(kernel, out_shape=tuple((jax.ShapeDtypeStruct(*out) for ou...]
  transfers between devices with their start and end apart: 17 -> 17, of which waited for: 10 -> 8; matrix products, arithmetic and copies ran while one was open for 1% -> 1% of each run, Pallas kernels for 6% -> 7%
where the time goes in v6:
time: 88.3 us; the launch traced here: 87.1 us
  starting transfers between devices  44.4 us (50%)
  waiting for transfers between devices  22.4 us (25%)
  Pallas kernels  13.5 us (15%)
  other arithmetic  4.88 us (6%)
  local copies, waits for them, and re-layouts  0.95 us (1%)
    ppermute x12, starting transfers between devices, swap(): return lax.ppermute(block, axis, swap_pairs(lax.axis_size(axis), kind))  26.5 us
    ppermute x12, waiting for transfers between devices, swap(): return lax.ppermute(block, axis, swap_pairs(lax.axis_size(axis), kind))  16.5 us
    pallas_call x6, Pallas kernels, call(): pl.pallas_call(kernel, out_shape=tuple((jax.ShapeDtypeStruct(*out) for ou...  13.5 us
    all_to_all x2, starting transfers between devices, exchange(): lax.all_to_all(pieces, BOTH, 0, 0, tiled=True, axis_index_groups=groups)  12.8 us
    ppermute x3, starting transfers between devices, cross(): lax.ppermute(block, BOTH, [(i, i ^ step) for i in range(lax.axis_size(BOT...  5.07 us
    all_to_all x2, waiting for transfers between devices, exchange(): lax.all_to_all(pieces, BOTH, 0, 0, tiled=True, axis_index_groups=groups)  3.14 us
    ppermute x3, waiting for transfers between devices, cross(): lax.ppermute(block, BOTH, [(i, i ^ step) for i in range(lax.axis_size(BOT...  2.75 us
    select_n x4, other arithmetic, by_side(): return (jnp.where(odd, first, second), jnp.where(odd, second, first))  2.11 us
  transfers between devices with their start and end apart: 17, of which 8 were waited for; matrix products, arithmetic and copies ran while one was open for 1% of the time, Pallas kernels for 7%

profile of v6, /device:TPU:10, one launch (start us, length us, event | category | flops | bytes accessed | tf_op | source)
XLA Modules:
  0.0 87.1 jit_solution(11607911070355597324)
XLA Ops:
  0.7 1.1 %broadcast_select_fusion.6 = (bf16[16,8,384]{2,1,0:T(8,128)(2,1)S(1)}, bf16[16,8,384]{2,1,0:T(8,128)(2,1)S(1)}) fusion(pred[]{:T(512)S(6)} %eq.6, bf16[16,16,384]{2,1,0:T(8,128)(2,1)} %tokens.1), kind=kLoop, calls=%fused_computation.19 | loop fusion | flops 98304 | bytes 393217 | tf_op jit(solution)/shard_map/halo/jit(_where)/select_n | solution.py:41
  1.8 3.4 %collective-permute-start.1 = (bf16[16,8,384]{2,1,0:T(8,128)(2,1)S(1)}, bf16[16,8,384]{2,1,0:T(8,128)(2,1)S(1)}, u32[]{:S(2)}, u32[]{:S(2)}) collective-permute-start(bf16[16,8,384]{2,1,0:T(8,128)(2,1)S(1)} %get-tuple-element.77), channel_id=1, source_target_pairs={{1,2},{2,1},{3,4},{4,3},{5,6},{6,5},{7,8},{8,7},{9,10},{10,9},{11,... | collective-permute-start | bytes 294920 | tf_op jit(solution)/shard_map/halo/ppermute | solution.py:36
  7.0 8.6 %collective-permute-start.3 = (bf16[8,16,384]{2,1,0:T(8,128)(2,1)S(1)}, bf16[8,16,384]{2,1,0:T(8,128)(2,1)S(1)}, u32[]{:S(2)}, u32[]{:S(2)}) collective-permute-start(bf16[8,16,384]{2,1,0:T(8,128)(2,1)S(1)} %get-tuple-element.75), channel_id=1, source_target_pairs={{16,32},{32,16},{48,64},{64,48},{80,96},{96,80},{112,128},{128,112... | collective-permute-start | bytes 294920 | tf_op jit(solution)/shard_map/halo/ppermute | solution.py:36
  15.9 3.9 %collective-permute-start.5 = (bf16[8,16,384]{2,1,0:T(8,128)(2,1)S(1)}, bf16[8,16,384]{2,1,0:T(8,128)(2,1)S(1)}, u32[]{:S(2)}, u32[]{:S(2)}) collective-permute-start(bf16[8,16,384]{2,1,0:T(8,128)(2,1)S(1)} %get-tuple-element.71), channel_id=1, source_target_pairs={{16,32},{32,16},{48,64},{64,48},{80,96},{96,80},{112,128},{128,112... | collective-permute-start | bytes 294920 | tf_op jit(solution)/shard_map/halo/ppermute | solution.py:36
  20.1 1.2 %own_projections.1 = (bf16[256,384]{1,0:T(8,128)(2,1)S(1)}, bf16[256,384]{1,0:T(8,128)(2,1)S(1)}, bf16[256,384]{1,0:T(8,128)(2,1)S(1)}, bf16[256,384]{1,0:T(8,12...) custom-call(s32[4]{0:T(128)S(1)} %pad_add_fusion.place, bf16[16,16,384]{2,1,0:T(8,128)(2,1)S(1)} %copy-done, ...), custom_call_target="tpu_custom_call" | custom-call | flops 1000000000 | bytes 1000000 | tf_op jit(solution)/shard_map/own_projections/pallas_call | solution.py:67
  21.3 1.2 %edge_projections.1 = (bf16[512,384]{1,0:T(8,128)(2,1)S(1)}, bf16[512,384]{1,0:T(8,128)(2,1)S(1)}, bf16[512,384]{1,0:T(8,128)(2,1)S(1)}) custom-call(s32[4]{0:T(128)S(1)} %pad_add_fusion.place, bf16[16,8,384]{2,1,0:T(8,128)(2,1)S(1)} %collective-permute-done.col_0, bf16[16,8,384]{2,1,0:T(8,128)(2,1)S(1)} %collective-permute-done.1.col_1, ...), custom_call_target="tpu_custom_call" | custom-call | flops 1000000000 | bytes 1000000 | tf_op jit(solution)/shard_map/edge_projections/pallas_call | solution.py:67
  22.5 2.0 %collective-permute-done.5.corner_1 = bf16[8,16,384]{2,1,0:T(8,128)(2,1)S(1)} collective-permute-done((bf16[8,16,384]{2,1,0:T(8,128)(2,1)S(1)}, bf16[8,16,384]{2,1,0:T(8,128)(2,1)S(1)}, u32[]{:S(2)}, u32[]{:S(2)}) %collective-permute-start.5) | collective-permute-done | bytes 98336 | tf_op jit(solution)/shard_map/halo/ppermute | solution.py:36
  24.5 7.3 %attention.1 = (bf16[768,384]{1,0:T(8,128)(2,1)S(1)}, bf16[768,384]{1,0:T(8,128)(2,1)S(1)}, bf16[1024,384]{1,0:T(8,128)(2,1)S(1)}, bf16[1024,384]{1,0:T(8,128)(2,1)S(1)}, bf16[256,384]{1,0:T(8,128)(2,1)S(1)}) custom-call(s32[4]{0:T(128)S(1)} %pad_add_fusion.place, bf16[256,384]{1,0:T(8,128)(2,1)S(1)} %get-tuple-element.34.tiles, ...), custom_call_target="tpu_custom_call" | custom-call | flops 8000000000 | bytes 8000000 | tf_op jit(solution)/shard_map/attention/pallas_call | solution.py:67
  32.0 1.8 %spread_grads.1 = (f32[512,384]{1,0:T(8,128)S(1)}, bf16[256,384]{1,0:T(8,128)(2,1)S(1)}, bf16[256,384]{1,0:T(8,128)(2,1)S(1)}) custom-call(s32[4]{0:T(128)S(1)} %pad_add_fusion.place, bf16[1024,384]{1,0:T(8,128)(2,1)S(1)} %get-tuple-element.44.key_grad, bf16[1024,384]{1,0:T(8,128)(2,1)S(1)} %get-tuple-element.45.value_grad, ...), custom_call_target="tpu_custom_call" | custom-call | flops 1000000000 | bytes 1000000 | tf_op jit(solution)/shard_map/spread_grads/pallas_call | solution.py:67
  34.9 6.0 %all-to-all-start = ((bf16[16,48,384]{2,1,0:T(8,128)(2,1)}), bf16[16,48,384]{2,1,0:T(8,128)(2,1)S(1)}, u32[]{:S(2)}, u32[]{:S(2)}) async-start(bf16[16,48,384]{2,1,0:T(8,128)(2,1)} %bitcast.2), calls=%async_computation | async-start | bytes 1179648 | tf_op jit(solution)/shard_map/plane_sum/all_to_all | solution.py:355
  40.9 1.2 %collective-permute-start.7 = (bf16[256,384]{1,0:T(8,128)(2,1)S(1)}, bf16[256,384]{1,0:T(8,128)(2,1)S(1)}, u32[]{:S(2)}, u32[]{:S(2)}) collective-permute-start(bf16[256,384]{1,0:T(8,128)(2,1)S(1)} %get-tuple-element.51), channel_id=1, source_target_pairs={{0,16},{16,0},{32,48},{48,32},{64,80},{80,64},{96,112},{112,96},{1... | collective-permute-start | bytes 589832 | tf_op jit(solution)/shard_map/plane_sum/ppermute | solution.py:36
  42.2 5.4 %collective-permute-done.7.from_0 = bf16[256,384]{1,0:T(8,128)(2,1)S(1)} collective-permute-done((bf16[256,384]{1,0:T(8,128)(2,1)S(1)}, bf16[256,384]{1,0:T(8,128)(2,1)S(1)}, u32[]{:S(2)}, u32[]{:S(2)}) %collective-permute-start.7) | collective-permute-done | bytes 196640 | tf_op jit(solution)/shard_map/plane_sum/ppermute | solution.py:36
  47.5 3.1 %all-to-all-done = bf16[16,48,384]{2,1,0:T(8,128)(2,1)S(1)} async-done(((bf16[16,48,384]{2,1,0:T(8,128)(2,1)}), bf16[16,48,384]{2,1,0:T(8,128)(2,1)S(1)}, u32[]{:S(2)}, u32[]{:S(2)}) %all-to-all-start) | async-done | bytes 589856 | tf_op jit(solution)/shard_map/plane_sum/all_to_all | solution.py:355
  50.7 1.3 %collective-permute-start.8 = (bf16[48,384]{1,0:T(8,128)(2,1)S(1)}, bf16[48,384]{1,0:T(8,128)(2,1)S(1)}, u32[]{:S(2)}, u32[]{:S(2)}) collective-permute-start(bf16[48,384]{1,0:T(8,128)(2,1)S(1)} %fusion.5), channel_id=1, source_target_pairs={{0,16},{1,17},{2,18},{3,19},{4,20},{5,21},{6,22},{7,23},{8,24},{9,... | collective-permute-start | bytes 110600 | tf_op jit(solution)/shard_map/line_sum/ppermute | solution.py:351
  52.0 2.7 %collective-permute-done.8 = bf16[48,384]{1,0:T(8,128)(2,1)S(1)} collective-permute-done((bf16[48,384]{1,0:T(8,128)(2,1)S(1)}, bf16[48,384]{1,0:T(8,128)(2,1)S(1)}, u32[]{:S(2)}, u32[]{:S(2)}) %collective-permute-start.8) | collective-permute-done | bytes 36896 | tf_op jit(solution)/shard_map/line_sum/ppermute | solution.py:351
  54.9 1.4 %collective-permute-start.9 = (bf16[48,384]{1,0:T(8,128)(2,1)S(1)}, bf16[48,384]{1,0:T(8,128)(2,1)S(1)}, u32[]{:S(2)}, u32[]{:S(2)}) collective-permute-start(bf16[48,384]{1,0:T(8,128)(2,1)S(1)} %add_convert_fusion.3), channel_id=1, source_target_pairs={{0,32},{1,33},{2,34},{3,35},{4,36},{5,37},{6,38},{7,39},{8,40},{9,... | collective-permute-start | bytes 110600 | tf_op jit(solution)/shard_map/line_sum/ppermute | solution.py:351
  56.2 4.0 %collective-permute-start.11 = (bf16[256,384]{1,0:T(8,128)(2,1)S(1)}, bf16[256,384]{1,0:T(8,128)(2,1)S(1)}, u32[]{:S(2)}, u32[]{:S(2)}) collective-permute-start(bf16[256,384]{1,0:T(8,128)(2,1)S(1)} %get-tuple-element.54), channel_id=1, source_target_pairs={{16,32},{32,16},{48,64},{64,48},{80,96},{96,80},{112,128},{128,112... | collective-permute-start | bytes 589832 | tf_op jit(solution)/shard_map/line_sum/ppermute | solution.py:36
  60.3 2.4 %collective-permute-start.10 = (bf16[48,384]{1,0:T(8,128)(2,1)S(1)}, bf16[48,384]{1,0:T(8,128)(2,1)S(1)}, u32[]{:S(2)}, u32[]{:S(2)}) collective-permute-start(bf16[48,384]{1,0:T(8,128)(2,1)S(1)} %add_convert_fusion.2), channel_id=1, source_target_pairs={{0,112},{1,113},{2,114},{3,115},{4,116},{5,117},{6,118},{7,119},{8... | collective-permute-start | bytes 110600 | tf_op jit(solution)/shard_map/line_sum/ppermute | solution.py:351
  62.7 3.2 %collective-permute-done.11.from_1 = bf16[256,384]{1,0:T(8,128)(2,1)S(1)} collective-permute-done((bf16[256,384]{1,0:T(8,128)(2,1)S(1)}, bf16[256,384]{1,0:T(8,128)(2,1)S(1)}, u32[]{:S(2)}, u32[]{:S(2)}) %collective-permute-start.11) | collective-permute-done | bytes 196640 | tf_op jit(solution)/shard_map/line_sum/ppermute | solution.py:36
  66.8 6.8 %all-to-all-start.1 = ((bf16[16,48,384]{2,1,0:T(8,128)(2,1)}), bf16[16,48,384]{2,1,0:T(8,128)(2,1)S(1)}, u32[]{:S(2)}, u32[]{:S(2)}) async-start(bf16[16,48,384]{2,1,0:T(8,128)(2,1)} %broadcast_in_dim.3), calls=%async_computation.1 | async-start | bytes 1179648 | tf_op jit(solution)/shard_map/plane_gather/all_to_all | solution.py:355
  74.4 4.1 %collective-permute-start.13 = (bf16[128,384]{1,0:T(8,128)(2,1)S(1)}, bf16[128,384]{1,0:T(8,128)(2,1)S(1)}, u32[]{:S(2)}, u32[]{:S(2)}) collective-permute-start(bf16[128,384]{1,0:T(8,128)(2,1)S(1)} %get-tuple-element.59), channel_id=1, source_target_pairs={{1,2},{2,1},{3,4},{4,3},{5,6},{6,5},{7,8},{8,7},{9,10},{10,9},{11,... | collective-permute-start | bytes 294920 | tf_op jit(solution)/shard_map/plane_gather/ppermute | solution.py:36
  78.5 5.1 %collective-permute-done.13.from_1 = bf16[128,384]{1,0:T(8,128)(2,1)S(1)} collective-permute-done((bf16[128,384]{1,0:T(8,128)(2,1)S(1)}, bf16[128,384]{1,0:T(8,128)(2,1)S(1)}, u32[]{:S(2)}, u32[]{:S(2)}) %collective-permute-start.13) | collective-permute-done | bytes 98336 | tf_op jit(solution)/shard_map/plane_gather/ppermute | solution.py:36
  83.6 1.3 %add_columns.1 = bf16[16,16,384]{2,1,0:T(8,128)(2,1)} custom-call(s32[4]{0:T(128)S(1)} %pad_add_fusion.place, f32[256,384]{1,0:T(8,128)S(1)} %get-tuple-element.56.summed, bf16[128,384]{1,0:T(8,128)(2,1)S(1)} %collective-permute-done.12.from_0, bf16[128,384]{1,0:T(8,128)(2,1)S(1)} %collective-permute-done.13.from_1), custom_call_target="tpu_custom_call" | custom-call | flops 1000000000 | bytes 1000000 | tf_op jit(solution)/shard_map/add_columns/pallas_call | solution.py:67
  85.6 1.5 %fusion.3 = (f32[384,384]{1,0:T(8,128)}, f32[384,384]{1,0:T(8,128)}, f32[384,384]{1,0:T(8,128)}, f32[384,384]{1,0:T(8,128)}) fusion(bf16[8,48,384]{2,1,0:T(8,128)(2,1)S(1)} %get-tuple-element.70, pred[]{:T(512)S(6)} %eq.16, bf16[768,384]{1,0:T(8,128)(2,1)S(1)} %collective-permute-done.14, pred[]{:T(512)S(6)} %eq.6, bf16[8,48,384]{2,1,0:T(8,128)(2,1)S(1)} %get-tuple-element.69), kind=kLoop, calls=%fused_computation.8 | loop fusion | flops 1179648 | bytes 3538946 | tf_op jit(solution)/shard_map/core_gather/convert_element_type | solution.py:413
  (41 shorter events, 6.2 us)
Async XLA Ops:
  0.6 19.4 %copy-start = (bf16[16,16,384]{2,1,0:T(8,128)(2,1)S(1)}, bf16[16,16,384]{2,1,0:T(8,128)(2,1)}, u32[]{:S(2)}) copy-start(bf16[16,16,384]{2,1,0:T(8,128)(2,1)} %tokens.1) | copy-start | bytes 589828
  0.7 19.4 %copy-start.1 = (bf16[384,384]{1,0:T(8,128)(2,1)S(1)}, bf16[384,384]{1,0:T(8,128)(2,1)}, u32[]{:S(2)}) copy-start(bf16[384,384]{1,0:T(8,128)(2,1)} %w_out.1) | copy-start | bytes 884740
  0.7 19.4 %copy-start.2 = (bf16[384,384]{1,0:T(8,128)(2,1)S(1)}, bf16[384,384]{1,0:T(8,128)(2,1)}, u32[]{:S(2)}) copy-start(bf16[384,384]{1,0:T(8,128)(2,1)} %w_query.3) | copy-start | bytes 884740
  0.7 19.4 %copy-start.3 = (bf16[384,384]{1,0:T(8,128)(2,1)S(1)}, bf16[384,384]{1,0:T(8,128)(2,1)}, u32[]{:S(2)}) copy-start(bf16[384,384]{1,0:T(8,128)(2,1)} %w_key.7) | copy-start | bytes 884740
  0.7 19.4 %copy-start.4 = (bf16[384,384]{1,0:T(8,128)(2,1)S(1)}, bf16[384,384]{1,0:T(8,128)(2,1)}, u32[]{:S(2)}) copy-start(bf16[384,384]{1,0:T(8,128)(2,1)} %w_value.7) | copy-start | bytes 884740
  0.7 19.4 %copy-start.5 = (bf16[16,16,384]{2,1,0:T(8,128)(2,1)S(1)}, bf16[16,16,384]{2,1,0:T(8,128)(2,1)}, u32[]{:S(2)}) copy-start(bf16[16,16,384]{2,1,0:T(8,128)(2,1)} %grad_out.1) | copy-start | bytes 589828
  1.8 14.0 %collective-permute-start.1 = (bf16[16,8,384]{2,1,0:T(8,128)(2,1)S(1)}, bf16[16,8,384]{2,1,0:T(8,128)(2,1)S(1)}, u32[]{:S(2)}, u32[]{:S(2)}) collective-permute-start(bf16[16,8,384]{2,1,0:T(8,128)(2,1)S(1)} %get-tuple-element.77), channel_id=1, source_target_pairs={{1,2},{2,1},{3,4},{4,3},{5,6},{6,5},{7,8},{8,7},{9,10},{10,9},{11,... | collective-permute-start | bytes 294920 | tf_op jit(solution)/shard_map/halo/ppermute | solution.py:36
  5.1 10.7 %collective-permute-start = (bf16[16,8,384]{2,1,0:T(8,128)(2,1)S(1)}, bf16[16,8,384]{2,1,0:T(8,128)(2,1)S(1)}, u32[]{:S(2)}, u32[]{:S(2)}) collective-permute-start(bf16[16,8,384]{2,1,0:T(8,128)(2,1)S(1)} %get-tuple-element.78), channel_id=1, source_target_pairs={{0,1},{1,0},{2,3},{3,2},{4,5},{5,4},{6,7},{7,6},{8,9},{9,8},{10,11... | collective-permute-start | bytes 294920 | tf_op jit(solution)/shard_map/halo/ppermute | solution.py:36
  7.0 14.3 %collective-permute-start.3 = (bf16[8,16,384]{2,1,0:T(8,128)(2,1)S(1)}, bf16[8,16,384]{2,1,0:T(8,128)(2,1)S(1)}, u32[]{:S(2)}, u32[]{:S(2)}) collective-permute-start(bf16[8,16,384]{2,1,0:T(8,128)(2,1)S(1)} %get-tuple-element.75), channel_id=1, source_target_pairs={{16,32},{32,16},{48,64},{64,48},{80,96},{96,80},{112,128},{128,112... | collective-permute-start | bytes 294920 | tf_op jit(solution)/shard_map/halo/ppermute | solution.py:36
  15.6 5.7 %collective-permute-start.2 = (bf16[8,16,384]{2,1,0:T(8,128)(2,1)S(1)}, bf16[8,16,384]{2,1,0:T(8,128)(2,1)S(1)}, u32[]{:S(2)}, u32[]{:S(2)}) collective-permute-start(bf16[8,16,384]{2,1,0:T(8,128)(2,1)S(1)} %get-tuple-element.76), channel_id=1, source_target_pairs={{0,16},{16,0},{32,48},{48,32},{64,80},{80,64},{96,112},{112,96},{1... | collective-permute-start | bytes 294920 | tf_op jit(solution)/shard_map/halo/ppermute | solution.py:36
  15.9 8.6 %collective-permute-start.5 = (bf16[8,16,384]{2,1,0:T(8,128)(2,1)S(1)}, bf16[8,16,384]{2,1,0:T(8,128)(2,1)S(1)}, u32[]{:S(2)}, u32[]{:S(2)}) collective-permute-start(bf16[8,16,384]{2,1,0:T(8,128)(2,1)S(1)} %get-tuple-element.71), channel_id=1, source_target_pairs={{16,32},{32,16},{48,64},{64,48},{80,96},{96,80},{112,128},{128,112... | collective-permute-start | bytes 294920 | tf_op jit(solution)/shard_map/halo/ppermute | solution.py:36
  19.8 4.7 %collective-permute-start.4 = (bf16[8,16,384]{2,1,0:T(8,128)(2,1)S(1)}, bf16[8,16,384]{2,1,0:T(8,128)(2,1)S(1)}, u32[]{:S(2)}, u32[]{:S(2)}) collective-permute-start(bf16[8,16,384]{2,1,0:T(8,128)(2,1)S(1)} %get-tuple-element.72), channel_id=1, source_target_pairs={{0,16},{16,0},{32,48},{48,32},{64,80},{80,64},{96,112},{112,96},{1... | collective-permute-start | bytes 294920 | tf_op jit(solution)/shard_map/halo/ppermute | solution.py:36
  31.9 2.1 %collective-permute-start.6 = (bf16[768,384]{1,0:T(8,128)(2,1)S(1)}, bf16[768,384]{1,0:T(8,128)(2,1)S(1)}, u32[]{:S(2)}, u32[]{:S(2)}) collective-permute-start(bf16[768,384]{1,0:T(8,128)(2,1)S(1)} %get-tuple-element.43), channel_id=1, source_target_pairs={{0,1},{1,0},{2,3},{3,2},{4,5},{5,4},{6,7},{7,6},{8,9},{9,8},{10,11... | collective-permute-start | bytes 1769480 | tf_op jit(solution)/shard_map/core_sum/ppermute | solution.py:36
  34.9 15.7 %all-to-all-start = ((bf16[16,48,384]{2,1,0:T(8,128)(2,1)}), bf16[16,48,384]{2,1,0:T(8,128)(2,1)S(1)}, u32[]{:S(2)}, u32[]{:S(2)}) async-start(bf16[16,48,384]{2,1,0:T(8,128)(2,1)} %bitcast.2), calls=%async_computation | async-start | bytes 1179648 | tf_op jit(solution)/shard_map/plane_sum/all_to_all | solution.py:355
  40.9 6.6 %collective-permute-start.7 = (bf16[256,384]{1,0:T(8,128)(2,1)S(1)}, bf16[256,384]{1,0:T(8,128)(2,1)S(1)}, u32[]{:S(2)}, u32[]{:S(2)}) collective-permute-start(bf16[256,384]{1,0:T(8,128)(2,1)S(1)} %get-tuple-element.51), channel_id=1, source_target_pairs={{0,16},{16,0},{32,48},{48,32},{64,80},{80,64},{96,112},{112,96},{1... | collective-permute-start | bytes 589832 | tf_op jit(solution)/shard_map/plane_sum/ppermute | solution.py:36
  50.7 4.0 %collective-permute-start.8 = (bf16[48,384]{1,0:T(8,128)(2,1)S(1)}, bf16[48,384]{1,0:T(8,128)(2,1)S(1)}, u32[]{:S(2)}, u32[]{:S(2)}) collective-permute-start(bf16[48,384]{1,0:T(8,128)(2,1)S(1)} %fusion.5), channel_id=1, source_target_pairs={{0,16},{1,17},{2,18},{3,19},{4,20},{5,21},{6,22},{7,23},{8,24},{9,... | collective-permute-start | bytes 110600 | tf_op jit(solution)/shard_map/line_sum/ppermute | solution.py:351
  54.9 5.4 %collective-permute-start.9 = (bf16[48,384]{1,0:T(8,128)(2,1)S(1)}, bf16[48,384]{1,0:T(8,128)(2,1)S(1)}, u32[]{:S(2)}, u32[]{:S(2)}) collective-permute-start(bf16[48,384]{1,0:T(8,128)(2,1)S(1)} %add_convert_fusion.3), channel_id=1, source_target_pairs={{0,32},{1,33},{2,34},{3,35},{4,36},{5,37},{6,38},{7,39},{8,40},{9,... | collective-permute-start | bytes 110600 | tf_op jit(solution)/shard_map/line_sum/ppermute | solution.py:351
  56.2 9.7 %collective-permute-start.11 = (bf16[256,384]{1,0:T(8,128)(2,1)S(1)}, bf16[256,384]{1,0:T(8,128)(2,1)S(1)}, u32[]{:S(2)}, u32[]{:S(2)}) collective-permute-start(bf16[256,384]{1,0:T(8,128)(2,1)S(1)} %get-tuple-element.54), channel_id=1, source_target_pairs={{16,32},{32,16},{48,64},{64,48},{80,96},{96,80},{112,128},{128,112... | collective-permute-start | bytes 589832 | tf_op jit(solution)/shard_map/line_sum/ppermute | solution.py:36
  60.3 5.6 %collective-permute-start.10 = (bf16[48,384]{1,0:T(8,128)(2,1)S(1)}, bf16[48,384]{1,0:T(8,128)(2,1)S(1)}, u32[]{:S(2)}, u32[]{:S(2)}) collective-permute-start(bf16[48,384]{1,0:T(8,128)(2,1)S(1)} %add_convert_fusion.2), channel_id=1, source_target_pairs={{0,112},{1,113},{2,114},{3,115},{4,116},{5,117},{6,118},{7,119},{8... | collective-permute-start | bytes 110600 | tf_op jit(solution)/shard_map/line_sum/ppermute | solution.py:351
  66.8 16.8 %all-to-all-start.1 = ((bf16[16,48,384]{2,1,0:T(8,128)(2,1)}), bf16[16,48,384]{2,1,0:T(8,128)(2,1)S(1)}, u32[]{:S(2)}, u32[]{:S(2)}) async-start(bf16[16,48,384]{2,1,0:T(8,128)(2,1)} %broadcast_in_dim.3), calls=%async_computation.1 | async-start | bytes 1179648 | tf_op jit(solution)/shard_map/plane_gather/all_to_all | solution.py:355
  74.3 4.2 %collective-permute-start.12 = (bf16[128,384]{1,0:T(8,128)(2,1)S(1)}, bf16[128,384]{1,0:T(8,128)(2,1)S(1)}, u32[]{:S(2)}, u32[]{:S(2)}) collective-permute-start(bf16[128,384]{1,0:T(8,128)(2,1)S(1)} %get-tuple-element.58), channel_id=1, source_target_pairs={{0,1},{1,0},{2,3},{3,2},{4,5},{5,4},{6,7},{7,6},{8,9},{9,8},{10,11... | collective-permute-start | bytes 294920 | tf_op jit(solution)/shard_map/plane_gather/ppermute | solution.py:36
  74.4 9.2 %collective-permute-start.13 = (bf16[128,384]{1,0:T(8,128)(2,1)S(1)}, bf16[128,384]{1,0:T(8,128)(2,1)S(1)}, u32[]{:S(2)}, u32[]{:S(2)}) collective-permute-start(bf16[128,384]{1,0:T(8,128)(2,1)S(1)} %get-tuple-element.59), channel_id=1, source_target_pairs={{1,2},{2,1},{3,4},{4,3},{5,6},{6,5},{7,8},{8,7},{9,10},{10,9},{11,... | collective-permute-start | bytes 294920 | tf_op jit(solution)/shard_map/plane_gather/ppermute | solution.py:36
  83.6 2.0 %collective-permute-start.14 = (bf16[768,384]{1,0:T(8,128)(2,1)S(1)}, bf16[768,384]{1,0:T(8,128)(2,1)S(1)}, u32[]{:S(2)}, u32[]{:S(2)}) collective-permute-start(bf16[768,384]{1,0:T(8,128)(2,1)S(1)} %bitcast.27), channel_id=1, source_target_pairs={{0,1},{1,0},{2,3},{3,2},{4,5},{5,4},{6,7},{7,6},{8,9},{9,8},{10,11... | collective-permute-start | bytes 1769480 | tf_op jit(solution)/shard_map/core_gather/ppermute | solution.py:36
